TPU v7x, 32 devices: a whole 2x2x4 slice. The times are simulated.
32 devices in a mesh: dp: 8 (over z, y), fsdp: 4 (over x, core).
Axes of the slice: x: 2, y: 2, z: 4, core: 2. Of those that a mesh axis runs over, the one named last changes fastest.
Arguments:
- buf_states: float32 [2048, 11], P(('dp', 'fsdp')), may hold values from -6 to 6
- buf_actions: float32 [2048, 3], P(('dp', 'fsdp')), may hold values from -0.95 to 0.95
- buf_returns: float32 [2048], P(('dp', 'fsdp')), may hold values from -6 to 6
- window_starts: int32 [512], P(('dp', 'fsdp')), may hold values from 0 to 44, as said below
- window_repeats: int32 [512], P(('dp', 'fsdp')), may hold values from 1 to 5
- valid_steps: int32 [512, 20], P(('dp', 'fsdp')), may hold values from 0 to 1, as said below
- matrix_groups: int32 [3, 4], replicated, may hold values from 0 to 2
- log_temp: float32 [1], replicated, may hold values from -2 to 0
- small_rows: float32 [85, 512], replicated
- head_bias: float32 [6], replicated, may hold values from -1.5 to 1.5
- qkv_weight: float32 [3, 512, 1536], P(None, ('dp', 'fsdp')), may hold values from -0.25 to 0.25
- out_weight: float32 [3, 512, 512], P(None, ('dp', 'fsdp')), may hold values from -0.5 to 0.5
- up_weight: float32 [3, 512, 2048], P(None, ('dp', 'fsdp')), may hold values from -0.25 to 0.25
- down_weight: float32 [3, 2048, 512], P(None, ('dp', 'fsdp')), may hold values from -0.125 to 0.125
- small_first: float32 [85, 512], replicated, may hold values from -0.005859375 to 0.005859375
- bias_first: float32 [6], replicated, may hold values from -0.005859375 to 0.005859375
- qkv_first: float32 [3, 512, 1536], P(None, ('dp', 'fsdp')), may hold values from -0.001953125 to 0.001953125
- out_first: float32 [3, 512, 512], P(None, ('dp', 'fsdp')), may hold values from -0.001953125 to 0.001953125
- up_first: float32 [3, 512, 2048], P(None, ('dp', 'fsdp')), may hold values from -0.001953125 to 0.001953125
- down_first: float32 [3, 2048, 512], P(None, ('dp', 'fsdp')), may hold values from -0.001953125 to 0.001953125
- small_second: float32 [85, 512], replicated, may hold values from 4.1007996e-07 to 1.6424391e-06
- bias_second: float32 [6], replicated, may hold values from 4.1007996e-07 to 1.6424391e-06
- qkv_second: float32 [3, 512, 1536], P(None, ('dp', 'fsdp')), may hold values from 4.556444e-08 to 1.8225776e-07
- out_second: float32 [3, 512, 512], P(None, ('dp', 'fsdp')), may hold values from 4.556444e-08 to 1.8225776e-07
- up_second: float32 [3, 512, 2048], P(None, ('dp', 'fsdp')), may hold values from 4.556444e-08 to 1.8225776e-07
- down_second: float32 [3, 2048, 512], P(None, ('dp', 'fsdp')), may hold values from 4.556444e-08 to 1.8225776e-07
Outputs:
- totals: float32 [3], replicated
- grad_norm: float32 [1], replicated
- next_temp: float32 [1], replicated
- small_next: float32 [85, 512], replicated
- small_first_next: float32 [85, 512], replicated
- small_second_next: float32 [85, 512], replicated
- bias_next: float32 [6], replicated
- bias_first_next: float32 [6], replicated
- bias_second_next: float32 [6], replicated
- qkv_next: float32 [3, 512, 1536], P(None, ('dp', 'fsdp'))
- out_next: float32 [3, 512, 512], P(None, ('dp', 'fsdp'))
- up_next: float32 [3, 512, 2048], P(None, ('dp', 'fsdp'))
- down_next: float32 [3, 2048, 512], P(None, ('dp', 'fsdp'))
- qkv_copy: bfloat16 [3, 512, 1536], P(None, ('dp', 'fsdp'))
- out_copy: bfloat16 [3, 512, 512], P(None, ('dp', 'fsdp'))
- up_copy: bfloat16 [3, 512, 2048], P(None, ('dp', 'fsdp'))
- down_copy: bfloat16 [3, 2048, 512], P(None, ('dp', 'fsdp'))
- qkv_first_next: float32 [3, 512, 1536], P(None, ('dp', 'fsdp'))
- out_first_next: float32 [3, 512, 512], P(None, ('dp', 'fsdp'))
- up_first_next: float32 [3, 512, 2048], P(None, ('dp', 'fsdp'))
- down_first_next: float32 [3, 2048, 512], P(None, ('dp', 'fsdp'))
- qkv_second_next: float32 [3, 512, 1536], P(None, ('dp', 'fsdp'))
- out_second_next: float32 [3, 512, 512], P(None, ('dp', 'fsdp'))
- up_second_next: float32 [3, 512, 2048], P(None, ('dp', 'fsdp'))
- down_second_next: float32 [3, 2048, 512], P(None, ('dp', 'fsdp'))
Inputs may be any that keep to these rules, and one draw needn't show every extreme that they name: Window w reads rows of the buffer block of the device that holds it: (w // 16) * 64 + window_starts[w] + t. `valid_steps`: in each window the ones follow the zeros and the last timestep is 1.
All inputs are finite; a program needn't handle non-finite values.
Results may differ from a plain program's by a relative error of at most 0.0034.
The roundings to bfloat16 on the way count: a program that leaves them out, or rounds other values in their place, can miss the bound.
Values may be sent and summed in bfloat16 or wider, within the bound.
A program may use at most 256 MiB of HBM per device.

v0:
```python
import math

import jax
import jax.numpy as jnp
from jax import lax
from jax.sharding import PartitionSpec as P

D = 512
H = 8
HD = 64
FF = 2048
S = 11
A = 3
K = 20
MICRO = 2
STEP = 10


EPS = 1e-05
CLIP = 1.0
LEARN = 0.03
BETA_ONE = 0.5
BETA_TWO = 0.7
DECAY = 0.01
ADAM_EPS = 1e-08
TEMP_RATE = 0.1
MASKED = -1e30
HALF_LOG_TAU = 0.5 * math.log(2.0 * math.pi)
HIGH = lax.Precision.HIGHEST
LOWER = jnp.bfloat16
WIDE = jnp.float32


def norm_parts(stream):
    center = stream - jnp.mean(stream, -1, keepdims=True)
    scale = lax.rsqrt(jnp.mean(center * center, -1, keepdims=True) + EPS)
    return (center * scale, scale)


def norm_rows(stream, gain, bias):
    normal, _ = norm_parts(stream)
    return normal * gain + bias


def norm_back(stream, gain, grad):
    normal, scale = norm_parts(stream)
    scaled = grad * gain
    back = scale * (
        scaled
        - jnp.mean(scaled, -1, keepdims=True)
        - normal * jnp.mean(scaled * normal, -1, keepdims=True)
    )
    return (back, jnp.sum(grad * normal, 0), jnp.sum(grad, 0))


def embed_tokens(states, actions, returns, small_rows):
    in_w = small_rows[: S + A + 1]
    position = small_rows[S + A + 1 : S + A + 1 + K]
    kinds = small_rows[S + A + 1 + K : S + A + 4 + K]
    ret_tok = returns[..., None] * in_w[S + A] + kinds[0] + position
    state_tok = jnp.einsum("wts,sd->wtd", states, in_w[:S], precision=HIGH) + kinds[1] + position
    action_tok = (
        jnp.einsum("wta,ad->wtd", actions, in_w[S : S + A], precision=HIGH) + kinds[2] + position
    )
    return jnp.stack([ret_tok, state_tok, action_tok], 2).reshape(-1, D)


def embed_back(grad, states, actions, returns):
    pieces = grad.reshape(states.shape[0], K, 3, D)
    ret_grad = jnp.einsum("wt,wtd->d", returns, pieces[:, :, 0], precision=HIGH)
    state_grad = jnp.einsum("wts,wtd->sd", states, pieces[:, :, 1], precision=HIGH)
    action_grad = jnp.einsum("wta,wtd->ad", actions, pieces[:, :, 2], precision=HIGH)
    return jnp.concatenate(
        [state_grad, action_grad, ret_grad[None], jnp.sum(pieces, (0, 2)), jnp.sum(pieces, (0, 1))],
        0,
    )


def action_terms(head, actions, weight, temp):
    center = head[:, :A]
    spread = jnp.tanh(head[:, A:])
    target = 0.5 * (jnp.log(1.0 + actions) - jnp.log(1.0 - actions))
    scaled = (target - center) * jnp.exp(-spread)
    nll = jnp.sum(
        0.5 * scaled * scaled + spread + HALF_LOG_TAU + jnp.log(1.0 - actions * actions), -1
    )
    entropy = jnp.sum(spread, -1) + A * (0.5 + HALF_LOG_TAU)
    return (jnp.sum(weight * (nll - temp * entropy)), jnp.sum(weight * entropy))


def fetch_stacks(qkv_weight, out_weight, up_weight, down_weight):
    return (
        lax.all_gather(qkv_weight.astype(LOWER), ("dp", "fsdp"), axis=1, tiled=True),
        lax.all_gather(out_weight.astype(LOWER), ("dp", "fsdp"), axis=1, tiled=True),
        lax.all_gather(up_weight.astype(LOWER), ("dp", "fsdp"), axis=1, tiled=True),
        lax.all_gather(down_weight.astype(LOWER), ("dp", "fsdp"), axis=1, tiled=True),
    )


def refetch_stacks(qkv_weight, out_weight, up_weight, down_weight):
    return (
        lax.all_gather(qkv_weight.astype(LOWER), ("dp", "fsdp"), axis=1, tiled=True),
        lax.all_gather(out_weight.astype(LOWER), ("dp", "fsdp"), axis=1, tiled=True),
        lax.all_gather(up_weight.astype(LOWER), ("dp", "fsdp"), axis=1, tiled=True),
        lax.all_gather(down_weight.astype(LOWER), ("dp", "fsdp"), axis=1, tiled=True),
    )


def split_heads(qkv_rows):
    count = qkv_rows.shape[0]
    return (
        qkv_rows[:, :D].reshape(count, H, HD),
        qkv_rows[:, D : 2 * D].reshape(count, H, HD),
        qkv_rows[:, 2 * D :].reshape(count, H, HD),
    )


def score_block(query, keyed, allowed):
    raw = jnp.einsum("qhe,khe->hqk", query, keyed, preferred_element_type=WIDE) * HD ** (-0.5)
    return jnp.where(allowed[None], raw, MASKED)


def forward_layer(stream, weights, layer_rows, allowed):
    w_qkv, w_out, w_up, w_down = weights
    count = stream.shape[0]
    up_rows = FF // D
    normed = norm_rows(stream, layer_rows[0], layer_rows[1]).astype(LOWER)
    qkv_rows = (
        jnp.dot(normed, w_qkv, preferred_element_type=WIDE) + layer_rows[4:7].reshape(-1)
    ).astype(LOWER)
    query, keyed, values = split_heads(qkv_rows)
    scores = score_block(query, keyed, allowed)
    peak = jnp.max(scores, -1, keepdims=True)
    expo = jnp.exp(scores - peak)
    denominator = jnp.sum(expo, -1, keepdims=True)
    probs = (expo / denominator).astype(LOWER)
    mixed = (
        jnp.einsum("hqk,khe->qhe", probs, values, preferred_element_type=WIDE)
        .astype(LOWER)
        .reshape(count, D)
    )
    stream_mid = stream + jnp.dot(mixed, w_out, preferred_element_type=WIDE) + layer_rows[7]
    second = norm_rows(stream_mid, layer_rows[2], layer_rows[3]).astype(LOWER)
    hidden = jnp.dot(second, w_up, preferred_element_type=WIDE) + layer_rows[
        8 : 8 + up_rows
    ].reshape(-1)
    acted = jax.nn.gelu(hidden).astype(LOWER)
    stream_out = (
        stream_mid + jnp.dot(acted, w_down, preferred_element_type=WIDE) + layer_rows[8 + up_rows]
    )
    return (
        stream_out,
        (
            stream,
            normed,
            qkv_rows,
            peak + jnp.log(denominator),
            mixed,
            stream_mid,
            second,
            hidden,
            acted,
        ),
    )


def backward_layer(grad, kept, weights, layer_rows, allowed):
    stream, normed, qkv_rows, log_total, mixed, stream_mid, second, hidden, acted = kept
    w_qkv, w_out, w_up, w_down = weights
    count = stream.shape[0]
    d_down = grad.astype(LOWER)
    g_down = jnp.einsum("rf,rd->fd", acted, d_down, preferred_element_type=WIDE)
    d_acted = jnp.einsum("rd,fd->rf", d_down, w_down, preferred_element_type=WIDE)
    _, gelu_back = jax.vjp(jax.nn.gelu, hidden)
    d_hidden = gelu_back(d_acted)[0].astype(LOWER)
    g_up = jnp.einsum("rd,rf->df", second, d_hidden, preferred_element_type=WIDE)
    d_second = jnp.einsum("rf,df->rd", d_hidden, w_up, preferred_element_type=WIDE)
    d_mid, g_gain_two, g_bias_two = norm_back(stream_mid, layer_rows[2], d_second)
    d_mid = d_mid + grad
    d_branch = d_mid.astype(LOWER)
    g_out = jnp.einsum("rd,re->de", mixed, d_branch, preferred_element_type=WIDE)
    d_mixed = (
        jnp.einsum("re,de->rd", d_branch, w_out, preferred_element_type=WIDE)
        .astype(LOWER)
        .reshape(count, H, HD)
    )
    query, keyed, values = split_heads(qkv_rows)
    probs = jnp.exp(score_block(query, keyed, allowed) - log_total)
    d_probs = jnp.einsum("qhe,khe->hqk", d_mixed, values, preferred_element_type=WIDE)
    d_values = jnp.einsum("hqk,qhe->khe", probs.astype(LOWER), d_mixed, preferred_element_type=WIDE)
    d_scores = (probs * (d_probs - jnp.sum(probs * d_probs, -1, keepdims=True))).astype(LOWER)
    d_query = jnp.einsum("hqk,khe->qhe", d_scores, keyed, preferred_element_type=WIDE) * HD ** (
        -0.5
    )
    d_keyed = jnp.einsum("hqk,qhe->khe", d_scores, query, preferred_element_type=WIDE) * HD ** (
        -0.5
    )
    d_qkv = jnp.concatenate(
        [d_query.reshape(count, D), d_keyed.reshape(count, D), d_values.reshape(count, D)], 1
    ).astype(LOWER)
    g_qkv = jnp.einsum("rd,re->de", normed, d_qkv, preferred_element_type=WIDE)
    d_normed = jnp.einsum("re,de->rd", d_qkv, w_qkv, preferred_element_type=WIDE)
    d_stream, g_gain_one, g_bias_one = norm_back(stream, layer_rows[0], d_normed)
    row_grads = jnp.concatenate(
        [
            jnp.stack([g_gain_one, g_bias_one, g_gain_two, g_bias_two]),
            jnp.sum(d_qkv.astype(WIDE), 0).reshape(3, D),
            jnp.sum(d_branch.astype(WIDE), 0)[None],
            jnp.sum(d_hidden.astype(WIDE), 0).reshape(-1, D),
            jnp.sum(d_down.astype(WIDE), 0)[None],
        ],
        0,
    )
    return (d_stream + d_mid, (g_qkv, g_out, g_up, g_down), row_grads)


def head_pass(stream, small_rows, head_bias, actions, weight, temp):
    first = S + A + 1 + K + 3
    fin_gain = small_rows[first]
    fin_bias = small_rows[first + 1]
    head_w = small_rows[first + 2 : first + 2 + 2 * A].astype(LOWER)
    state_rows = stream.reshape(-1, 3, D)[:, 1]
    feats = norm_rows(state_rows, fin_gain, fin_bias).astype(LOWER)
    head = jnp.einsum("rd,ad->ra", feats, head_w, preferred_element_type=WIDE) + head_bias

    def objective(values):
        return action_terms(values, actions.reshape(-1, A), weight.reshape(-1), temp)

    loss_part, back, entropy_part = jax.vjp(objective, head, has_aux=True)
    d_head = back(jnp.ones_like(loss_part))[0].astype(LOWER)
    g_head = jnp.einsum("ra,rd->ad", d_head, feats, preferred_element_type=WIDE)
    d_feats = jnp.einsum("ra,ad->rd", d_head, head_w, preferred_element_type=WIDE)
    d_states, g_gain, g_bias = norm_back(state_rows, fin_gain, d_feats)
    blank = jnp.zeros_like(d_states)
    grad = jnp.stack([blank, d_states, blank], 1).reshape(-1, D)
    return (
        grad,
        g_head,
        jnp.stack([g_gain, g_bias]),
        jnp.sum(d_head.astype(WIDE), 0),
        loss_part,
        entropy_part,
    )


def adam_step(weight, grad, first, second, rate):
    first = BETA_ONE * first + (1.0 - BETA_ONE) * grad
    second = BETA_TWO * second + (1.0 - BETA_TWO) * grad * grad
    fix_one = 1.0 - BETA_ONE**STEP
    fix_two = 1.0 - BETA_TWO**STEP
    fresh = weight - rate * (
        first / fix_one / (jnp.sqrt(second / fix_two) + ADAM_EPS) + DECAY * weight
    )
    return (fresh, first, second)


def local(
    buf_states,
    buf_actions,
    buf_returns,
    window_starts,
    window_repeats,
    valid_steps,
    matrix_groups,
    log_temp,
    small_rows,
    head_bias,
    qkv_weight,
    out_weight,
    up_weight,
    down_weight,
    small_first,
    bias_first,
    qkv_first,
    out_first,
    up_first,
    down_first,
    small_second,
    bias_second,
    qkv_second,
    out_second,
    up_second,
    down_second,
):
    layers = qkv_weight.shape[0]
    per_micro = window_starts.shape[0] // MICRO
    span = 3 * K
    rows = per_micro * span
    per_layer = 9 + FF // D
    layer_base = S + A + 1 + K + 5 + 2 * A
    place = window_starts[:, None] + jnp.arange(K, dtype=jnp.int32)[None, :]
    states = buf_states[place]
    actions = buf_actions[place]
    returns = buf_returns[place]
    weight = window_repeats[:, None].astype(WIDE) * valid_steps.astype(WIDE)
    temp = jnp.exp(log_temp[0])
    position = jnp.arange(rows)
    same_window = position[:, None] // span == position[None, :] // span
    causal = position[None, :] <= position[:, None]
    diagonal = position[None, :] == position[:, None]
    layer_rows = [
        small_rows[layer_base + layer * per_layer : layer_base + (layer + 1) * per_layer]
        for layer in range(layers)
    ]
    small_grad = jnp.zeros(small_rows.shape, WIDE)
    bias_grad = jnp.zeros(head_bias.shape, WIDE)
    totals = jnp.zeros((3,), WIDE)
    running = None
    for micro in range(MICRO):
        part = slice(micro * per_micro, (micro + 1) * per_micro)
        live = jnp.repeat(valid_steps[part], 3, axis=1).reshape(-1) > 0
        allowed = same_window & causal & (live[None, :] | diagonal)
        stream = embed_tokens(states[part], actions[part], returns[part], small_rows)
        stacks = fetch_stacks(qkv_weight, out_weight, up_weight, down_weight)
        kept = []
        for layer in range(layers):
            stream, saved = forward_layer(
                stream, tuple((piece[layer] for piece in stacks)), layer_rows[layer], allowed
            )
            kept.append(saved)
        grad, head_grad, final_grad, bias_part, loss_part, entropy_part = head_pass(
            stream, small_rows, head_bias, actions[part], weight[part], temp
        )
        back_stacks = refetch_stacks(qkv_weight, out_weight, up_weight, down_weight)
        row_grads = [None] * layers
        layer_mats = [None] * layers
        for layer in reversed(range(layers)):
            grad, layer_mats[layer], row_grads[layer] = backward_layer(
                grad,
                kept[layer],
                tuple((piece[layer] for piece in back_stacks)),
                layer_rows[layer],
                allowed,
            )
        stacked = [
            jnp.stack([layer_mats[layer][kind] for layer in range(layers)]) for kind in range(4)
        ]
        running = list(stacked) if micro == 0 else [old + new for old, new in zip(running, stacked)]
        small_grad = small_grad + jnp.concatenate(
            [embed_back(grad, states[part], actions[part], returns[part]), final_grad, head_grad]
            + row_grads,
            0,
        )
        bias_grad = bias_grad + bias_part
        totals = totals + jnp.stack([loss_part, entropy_part, jnp.sum(weight[part])])
    big = (
        lax.psum_scatter(running[0], ("dp", "fsdp"), scatter_dimension=1, tiled=True),
        lax.psum_scatter(running[1], ("dp", "fsdp"), scatter_dimension=1, tiled=True),
        lax.psum_scatter(running[2], ("dp", "fsdp"), scatter_dimension=1, tiled=True),
        lax.psum_scatter(running[3], ("dp", "fsdp"), scatter_dimension=1, tiled=True),
    )
    small_grad, bias_grad, totals = lax.psum((small_grad, bias_grad, totals), ("dp", "fsdp"))
    square = sum((jnp.sum(piece * piece) for piece in big))
    square = (
        lax.psum(square, ("dp", "fsdp"))
        + jnp.sum(small_grad * small_grad)
        + jnp.sum(bias_grad * bias_grad)
    )
    grad_norm = jnp.sqrt(square)
    clip = jnp.minimum(1.0, CLIP / (grad_norm + 1e-06))
    rates = LEARN * jnp.exp2(-matrix_groups.astype(WIDE))
    mats = (qkv_weight, out_weight, up_weight, down_weight)
    firsts = (qkv_first, out_first, up_first, down_first)
    seconds = (qkv_second, out_second, up_second, down_second)
    results = [
        adam_step(
            mats[kind], clip * big[kind], firsts[kind], seconds[kind], rates[:, kind][:, None, None]
        )
        for kind in range(4)
    ]
    small_new = adam_step(small_rows, clip * small_grad, small_first, small_second, LEARN)
    bias_new = adam_step(head_bias, clip * bias_grad, bias_first, bias_second, LEARN)
    next_temp = log_temp - TEMP_RATE * temp * (totals[1] / totals[2] + A)
    return (
        totals,
        grad_norm[None],
        next_temp,
        small_new[0],
        small_new[1],
        small_new[2],
        bias_new[0],
        bias_new[1],
        bias_new[2],
        results[0][0],
        results[1][0],
        results[2][0],
        results[3][0],
        results[0][0].astype(LOWER),
        results[1][0].astype(LOWER),
        results[2][0].astype(LOWER),
        results[3][0].astype(LOWER),
        results[0][1],
        results[1][1],
        results[2][1],
        results[3][1],
        results[0][2],
        results[1][2],
        results[2][2],
        results[3][2],
    )


def solution(mesh):
    in_specs = (
        P(("dp", "fsdp"), None),
        P(("dp", "fsdp"), None),
        P(("dp", "fsdp")),
        P(("dp", "fsdp")),
        P(("dp", "fsdp")),
        P(("dp", "fsdp"), None),
        P(),
        P(),
        P(),
        P(),
        P(None, ("dp", "fsdp"), None),
        P(None, ("dp", "fsdp"), None),
        P(None, ("dp", "fsdp"), None),
        P(None, ("dp", "fsdp"), None),
        P(),
        P(),
        P(None, ("dp", "fsdp"), None),
        P(None, ("dp", "fsdp"), None),
        P(None, ("dp", "fsdp"), None),
        P(None, ("dp", "fsdp"), None),
        P(),
        P(),
        P(None, ("dp", "fsdp"), None),
        P(None, ("dp", "fsdp"), None),
        P(None, ("dp", "fsdp"), None),
        P(None, ("dp", "fsdp"), None),
    )
    out_specs = (
        P(),
        P(),
        P(),
        P(),
        P(),
        P(),
        P(),
        P(),
        P(),
        P(None, ("dp", "fsdp"), None),
        P(None, ("dp", "fsdp"), None),
        P(None, ("dp", "fsdp"), None),
        P(None, ("dp", "fsdp"), None),
        P(None, ("dp", "fsdp"), None),
        P(None, ("dp", "fsdp"), None),
        P(None, ("dp", "fsdp"), None),
        P(None, ("dp", "fsdp"), None),
        P(None, ("dp", "fsdp"), None),
        P(None, ("dp", "fsdp"), None),
        P(None, ("dp", "fsdp"), None),
        P(None, ("dp", "fsdp"), None),
        P(None, ("dp", "fsdp"), None),
        P(None, ("dp", "fsdp"), None),
        P(None, ("dp", "fsdp"), None),
        P(None, ("dp", "fsdp"), None),
    )
    return jax.shard_map(local, mesh=mesh, in_specs=in_specs, out_specs=out_specs, check_vma=False)
```

profile of v0, /device:TPU:0, one launch (start us, length us, event | category | flops | bytes accessed | tf_op | source)
XLA Modules:
  0.0 1412.0 jit_solution(5607464035130815844)
XLA Ops:
  60.9 17.0 %all-gather.5.cloned.1.call-done = bf16[3,512,1536]{2,1,0:T(8,128)(2,1)} async-done(((bf16[3,16,1536]{2,1,0:T(8,128)(2,1)}), bf16[3,512,1536]{2,1,0:T(8,128)(2,1)}) %all-gather.5.cloned.1.call-update) | async-done | bytes 4718608 | tf_op jit(solution)/shard_map/all_gather | solution.py:93
  94.3 40.8 %all-gather.7.cloned.1.call-done = bf16[3,512,512]{2,1,0:T(8,128)(2,1)} async-done(((bf16[3,16,512]{2,1,0:T(8,128)(2,1)}), bf16[3,512,512]{2,1,0:T(8,128)(2,1)}) %all-gather.7.cloned.1.call-update) | async-done | bytes 1572880 | tf_op jit(solution)/shard_map/all_gather | solution.py:94
  146.4 60.3 %all-gather.9.cloned.1.call-done = bf16[3,512,2048]{2,1,0:T(8,128)(2,1)} async-done(((bf16[3,16,2048]{2,1,0:T(8,128)(2,1)}), bf16[3,512,2048]{2,1,0:T(8,128)(2,1)}) %all-gather.9.cloned.1.call-update) | async-done | bytes 6291472 | tf_op jit(solution)/shard_map/all_gather | solution.py:95
  206.7 5.1 fusion.86
  211.8 66.2 %all-gather.11.cloned.1.call-done = bf16[3,2048,512]{2,1,0:T(8,128)(2,1)} async-done(((bf16[3,64,512]{2,1,0:T(8,128)(2,1)}), bf16[3,2048,512]{2,1,0:T(8,128)(2,1)}) %all-gather.11.cloned.1.call-update) | async-done | bytes 6291472 | tf_op jit(solution)/shard_map/all_gather | solution.py:96
  278.1 4.6 fusion.298
  302.4 4.6 fusion.301
  338.0 4.7 fusion.306
  359.2 4.7 fusion.309
  415.4 6.5 convert_reduce_fusion
  422.0 5.2 multiply_reduce_fusion.8
  430.0 6.8 convert_reduce_fusion.3
  436.8 5.3 convert_reduce_fusion.13
  445.6 5.5 fusion.126
  451.1 8.4 multiply_reduce_fusion.5
  459.4 6.6 multiply_convert_fusion.5
  466.0 4.5 fusion.139
  473.6 5.5 fusion.135
  479.1 8.4 multiply_reduce_fusion.2
  487.5 6.8 multiply_convert_fusion.2
  518.2 4.2 convert_reduce_fusion.4
  528.9 5.5 fusion.123
  534.4 8.3 multiply_reduce_fusion.4
  542.8 6.7 multiply_convert_fusion.4
  549.4 4.5 fusion.141
  557.0 5.5 fusion.132
  562.5 8.4 multiply_reduce_fusion.1
  570.9 6.7 multiply_convert_fusion.1
  601.7 4.2 convert_reduce_fusion.2
  624.7 5.0 maximum_add_fusion.3
  630.2 8.3 multiply_reduce_fusion.3
  639.3 4.4 convolution_bitcast_fusion.13
  643.7 7.8 multiply_convert_fusion.3
  653.7 5.6 fusion.120
  662.4 4.8 multiply_reduce_fusion
  667.1 6.9 multiply_convert_fusion
  684.1 5.0 maximum_add_fusion.2
  702.4 7.0 maximum_add_fusion
  710.6 4.4 convolution_bitcast_fusion.3
  726.7 6.3 maximum_add_fusion.1
  742.1 4.9 multiply_reduce_fusion.20
  777.6 6.0 concatenate.36
  787.0 6.8 concatenate.37
  801.5 104.1 %reduce-scatter.5.cloned.1.call-done = f32[3,16,1536]{2,1,0:T(8,128)} async-done(((f32[3,512,1536]{2,1,0:T(8,128)}), f32[3,16,1536]{2,1,0:T(8,128)}) %reduce-scatter.5.cloned.1.call-update) | async-done | bytes 294928 | tf_op jit(solution)/shard_map/reduce_scatter | solution.py:347
  908.6 154.9 %reduce-scatter.9.cloned.1.call-done = f32[3,16,2048]{2,1,0:T(8,128)} async-done(((f32[3,512,2048]{2,1,0:T(8,128)}), f32[3,16,2048]{2,1,0:T(8,128)}) %reduce-scatter.9.cloned.1.call-update) | async-done | bytes 393232 | tf_op jit(solution)/shard_map/reduce_scatter | solution.py:349
  1065.9 152.9 %reduce-scatter.11.cloned.1.call-done = f32[3,64,512]{2,1,0:T(8,128)} async-done(((f32[3,2048,512]{2,1,0:T(8,128)}), f32[3,64,512]{2,1,0:T(8,128)}) %reduce-scatter.11.cloned.1.call-update) | async-done | bytes 393232 | tf_op jit(solution)/shard_map/reduce_scatter | solution.py:350
  1221.2 122.4 %all-reduce.7.cloned.1.call-done = f32[85,512]{1,0:T(8,128)} async-done(((f32[85,512]{1,0:T(8,128)}), f32[85,512]{1,0:T(8,128)}) %all-reduce.7.cloned.1.call-update) | async-done | bytes 174096 | tf_op jit(solution)/shard_map/psum | solution.py:352
  1345.2 41.9 %all-reduce.4 = (f32[3]{0:T(128)S(1)}, f32[]{:T(128)}, f32[6]{0:T(128)S(1)}) all-reduce(f32[3]{0:T(128)S(1)} %maximum_add_fusion.4, f32[]{:T(128)S(6)} %add.1193, f32[6]{0:T(128)} %add.1198), channel_id=1, replica_groups=mesh['dp'=8,'fsdp'=4] {'dp','fsdp'}, use_global_device_ids=true, to_apply=%region_50.51 | all-reduce | flops 10 | bytes 80 | tf_op jit(solution)/shard_map/psum | solution.py:352
  (1125 shorter events, 393.7 us)
Async XLA Ops:
  7.2 70.7 %all-gather.5.cloned.1.call-start = ((), (), s32[]{:S(2)}) async-start(), calls=%async_computation.4 | async-start | bytes 4866048 | tf_op jit(solution)/shard_map/all_gather | solution.py:93
  8.9 126.2 %all-gather.7.cloned.1.call-start = ((), (), s32[]{:S(2)}) async-start(), calls=%async_computation.5 | async-start | bytes 1622016 | tf_op jit(solution)/shard_map/all_gather | solution.py:94
  10.5 196.2 %all-gather.9.cloned.1.call-start = ((), (), s32[]{:S(2)}) async-start(), calls=%async_computation.6 | async-start | bytes 6488064 | tf_op jit(solution)/shard_map/all_gather | solution.py:95
  12.3 265.7 %all-gather.11.cloned.1.call-start = ((), (), s32[]{:S(2)}) async-start(), calls=%async_computation.7 | async-start | bytes 6488064 | tf_op jit(solution)/shard_map/all_gather | solution.py:96
  14.1 785.8 %reduce-scatter.7.cloned.1.call-start = ((), (), s32[]{:S(2)}) async-start(), calls=%async_computation.9 | async-start | bytes 3244032 | tf_op jit(solution)/shard_map/reduce_scatter | solution.py:348
  26.7 25.1 %copy-start.189 = (f32[8,20,3]{1,0,2:T(8,128)}, f32[8,20,3]{1,0,2:T(8,128)S(1)}, u32[]{:S(2)}) copy-start(f32[8,20,3]{1,0,2:T(8,128)S(1)} %reshape.1290) | copy-start | bytes 5764
  34.1 301.0 %copy-start.196 = (f32[1,512]{1,0:T(1,128)}, f32[1,512]{1,0:T(1,128)S(1)}, u32[]{:S(2)}) copy-start(f32[1,512]{1,0:T(1,128)S(1)} %get-tuple-element.202) | copy-start | bytes 6148
  49.4 28.5 %copy-start.181 = (bf16[480,512]{1,0:T(8,128)(2,1)S(1)}, bf16[480,512]{1,0:T(8,128)(2,1)}, u32[]{:S(2)}) copy-start(bf16[480,512]{1,0:T(8,128)(2,1)} %convert_element_type.456) | copy-start | bytes 1474564
  49.5 28.5 %copy-start.297 = (f32[1536]{0:T(1024)S(1)}, f32[1536]{0:T(1024)}, u32[]{:S(2)}) copy-start(f32[1536]{0:T(1024)} %add.1035) | copy-start | bytes 18436
  60.9 26.3 %copy-start.98 = (pred[480,480]{0,1:T(8,128)(4,1)}, pred[480,480]{0,1:T(8,128)(4,1)S(1)}, u32[]{:S(2)}) copy-start(pred[480,480]{0,1:T(8,128)(4,1)S(1)} %get-tuple-element.260) | copy-start | bytes 691204
  85.8 52.1 %copy-start.53 = (bf16[480,512]{0,1:T(8,128)(2,1)}, bf16[480,512]{0,1:T(8,128)(2,1)S(1)}, u32[]{:S(2)}) copy-start(bf16[480,512]{0,1:T(8,128)(2,1)S(1)} %copy.224) | copy-start | bytes 1474564
  87.2 50.7 %copy-start.55 = (bf16[480,512]{0,1:T(8,128)(2,1)}, bf16[480,512]{0,1:T(8,128)(2,1)S(1)}, u32[]{:S(2)}) copy-start(bf16[480,512]{0,1:T(8,128)(2,1)S(1)} %copy.225) | copy-start | bytes 1474564
  91.9 43.2 %copy-start.75 = (f32[480,512]{1,0:T(8,128)S(1)}, f32[480,512]{1,0:T(8,128)}, u32[]{:S(2)}) copy-start(f32[480,512]{1,0:T(8,128)} %reshape.1204) | copy-start | bytes 2949124
  91.9 43.2 %copy-start.256 = (f32[1,512]{1,0:T(1,128)S(1)}, f32[1,512]{1,0:T(1,128)}, u32[]{:S(2)}) copy-start(f32[1,512]{1,0:T(1,128)} %get-tuple-element.203) | copy-start | bytes 6148
  136.9 69.8 %copy-start.227 = (f32[480]{0:T(512)}, f32[480]{0:T(512)S(1)}, u32[]{:S(2)}) copy-start(f32[480]{0:T(512)S(1)} %broadcast_multiply_fusion.35) | copy-start | bytes 5764
  144.1 67.7 %copy-start.145 = (bf16[8,64,480]{2,1,0:T(8,128)(2,1)}, bf16[8,64,480]{2,1,0:T(8,128)(2,1)S(1)}, u32[]{:S(2)}) copy-start(bf16[8,64,480]{2,1,0:T(8,128)(2,1)S(1)} %fusion.119) | copy-start | bytes 1474564
  144.1 62.6 %copy-start.204 = (f32[1,512]{1,0:T(1,128)S(1)}, f32[1,512]{1,0:T(1,128)}, u32[]{:S(2)}) copy-start(f32[1,512]{1,0:T(1,128)} %get-tuple-element.201) | copy-start | bytes 6148
  144.8 193.2 %copy-start.14 = (f32[480,512]{1,0:T(8,128)}, f32[480,512]{1,0:T(8,128)S(1)}, u32[]{:S(2)}) copy-start(f32[480,512]{1,0:T(8,128)S(1)} %get-tuple-element.289) | copy-start | bytes 2949124
  144.8 190.3 %copy-start.219 = (f32[480]{0:T(512)}, f32[480]{0:T(512)S(1)}, u32[]{:S(2)}) copy-start(f32[480]{0:T(512)S(1)} %broadcast_multiply_fusion.40) | copy-start | bytes 5764
  145.1 66.7 %copy-start.246 = (f32[480]{0:T(512)}, f32[480]{0:T(512)S(1)}, u32[]{:S(2)}) copy-start(f32[480]{0:T(512)S(1)} %add_rsqrt_fusion.6) | copy-start | bytes 5764
  145.1 190.0 %copy-start.229 = (f32[480]{0:T(512)}, f32[480]{0:T(512)S(1)}, u32[]{:S(2)}) copy-start(f32[480]{0:T(512)S(1)} %add_rsqrt_fusion.11) | copy-start | bytes 5764
  206.7 71.3 %copy-start.286 = (f32[1,4,4,128]{3,1,2,0:T(4,128)S(1)}, f32[1,4,4,128]{3,1,2,0:T(4,128)}, u32[]{:S(2)}) copy-start(f32[1,4,4,128]{3,1,2,0:T(4,128)} %copy.331) | copy-start | bytes 24580
  206.7 71.3 %copy-start.318 = (f32[1,512]{1,0:T(1,128)S(1)}, f32[1,512]{1,0:T(1,128)}, u32[]{:S(2)}) copy-start(f32[1,512]{1,0:T(1,128)} %get-tuple-element.200) | copy-start | bytes 6148
  323.3 113.4 %copy-start.233 = (f32[480]{0:T(512)}, f32[480]{0:T(512)S(1)}, u32[]{:S(2)}) copy-start(f32[480]{0:T(512)S(1)} %broadcast_multiply_fusion.31) | copy-start | bytes 5764
  323.6 113.1 %copy-start.250 = (f32[480]{0:T(512)}, f32[480]{0:T(512)S(1)}, u32[]{:S(2)}) copy-start(f32[480]{0:T(512)S(1)} %add_rsqrt_fusion.2) | copy-start | bytes 5764
  377.4 64.8 %copy-start.20 = (f32[480,512]{1,0:T(8,128)}, f32[480,512]{1,0:T(8,128)S(1)}, u32[]{:S(2)}) copy-start(f32[480,512]{1,0:T(8,128)S(1)} %get-tuple-element.301) | copy-start | bytes 2949124
  377.4 64.8 %copy-start.221 = (f32[480]{0:T(512)}, f32[480]{0:T(512)S(1)}, u32[]{:S(2)}) copy-start(f32[480]{0:T(512)S(1)} %broadcast_multiply_fusion.36) | copy-start | bytes 5764
  377.6 64.5 %copy-start.235 = (f32[480]{0:T(512)}, f32[480]{0:T(512)S(1)}, u32[]{:S(2)}) copy-start(f32[480]{0:T(512)S(1)} %add_rsqrt_fusion.7) | copy-start | bytes 5764
  629.8 275.9 %reduce-scatter.5.cloned.1.call-start = ((), (), s32[]{:S(2)}) async-start(), calls=%async_computation.8 | async-start | bytes 9732096 | tf_op jit(solution)/shard_map/reduce_scatter | solution.py:347
  639.3 23.1 %copy-start.69 = (bf16[480,512]{0,1:T(8,128)(2,1)}, bf16[480,512]{0,1:T(8,128)(2,1)S(1)}, u32[]{:S(2)}) copy-start(bf16[480,512]{0,1:T(8,128)(2,1)S(1)} %copy.283) | copy-start | bytes 1474564
  689.2 374.2 %reduce-scatter.9.cloned.1.call-start = ((), (), s32[]{:S(2)}) async-start(), calls=%async_computation.10 | async-start | bytes 12976128 | tf_op jit(solution)/shard_map/reduce_scatter | solution.py:349
  709.5 509.4 %reduce-scatter.11.cloned.1.call-start = ((), (), s32[]{:S(2)}) async-start(), calls=%async_computation.11 | async-start | bytes 12976128 | tf_op jit(solution)/shard_map/reduce_scatter | solution.py:350
  733.2 610.5 %all-reduce.7.cloned.1.call-start = ((), (), s32[]{:S(2)}) async-start(), calls=%async_computation.12 | async-start | bytes 360448 | tf_op jit(solution)/shard_map/psum | solution.py:352
  783.6 609.4 %copy-start.174 = (f32[85,512]{1,0:T(8,128)S(1)}, f32[85,512]{1,0:T(8,128)}, u32[]{:S(2)}) copy-start(f32[85,512]{1,0:T(8,128)} %param.34) | copy-start | bytes 522244
  783.6 609.4 %copy-start.203 = (f32[85,512]{1,0:T(8,128)S(1)}, f32[85,512]{1,0:T(8,128)}, u32[]{:S(2)}) copy-start(f32[85,512]{1,0:T(8,128)} %param.40) | copy-start | bytes 522244
  784.3 610.6 %copy-start.172 = (f32[3,16,1536]{2,1,0:T(8,128)S(1)}, f32[3,16,1536]{2,1,0:T(8,128)}, u32[]{:S(2)}) copy-start(f32[3,16,1536]{2,1,0:T(8,128)} %param.36) | copy-start | bytes 884740
  785.6 611.7 %copy-start.185 = (f32[3,16,512]{2,1,0:T(8,128)S(1)}, f32[3,16,512]{2,1,0:T(8,128)}, u32[]{:S(2)}) copy-start(f32[3,16,512]{2,1,0:T(8,128)} %param.37) | copy-start | bytes 294916
  785.6 611.7 %copy-start.214 = (f32[3,16,512]{2,1,0:T(8,128)S(1)}, f32[3,16,512]{2,1,0:T(8,128)}, u32[]{:S(2)}) copy-start(f32[3,16,512]{2,1,0:T(8,128)} %param.43) | copy-start | bytes 294916
  785.6 611.7 %copy-start.325 = (f32[3]{0:T(128)S(1)}, f32[3]{0:T(128)}, u32[]{:S(2)}) copy-start(f32[3]{0:T(128)} %get-tuple-element.101) | copy-start | bytes 40
  786.0 613.0 %copy-start.168 = (f32[3,16,2048]{2,1,0:T(8,128)S(1)}, f32[3,16,2048]{2,1,0:T(8,128)}, u32[]{:S(2)}) copy-start(f32[3,16,2048]{2,1,0:T(8,128)} %param.38) | copy-start | bytes 1179652
  786.0 613.0 %copy-start.187 = (f32[3,16,2048]{2,1,0:T(8,128)S(1)}, f32[3,16,2048]{2,1,0:T(8,128)}, u32[]{:S(2)}) copy-start(f32[3,16,2048]{2,1,0:T(8,128)} %param.44) | copy-start | bytes 1179652
  786.0 613.0 %copy-start.328 = (f32[3]{0:T(128)S(1)}, f32[3]{0:T(128)}, u32[]{:S(2)}) copy-start(f32[3]{0:T(128)} %get-tuple-element.100) | copy-start | bytes 40
  787.0 612.0 %copy-start.188 = (f32[3,16,2048]{2,1,0:T(8,128)S(1)}, f32[3,16,2048]{2,1,0:T(8,128)}, u32[]{:S(2)}) copy-start(f32[3,16,2048]{2,1,0:T(8,128)} %param.50) | copy-start | bytes 1179652
  799.9 597.4 %copy-start.186 = (f32[3,16,512]{2,1,0:T(8,128)S(1)}, f32[3,16,512]{2,1,0:T(8,128)}, u32[]{:S(2)}) copy-start(f32[3,16,512]{2,1,0:T(8,128)} %reduce-scatter.7.cloned.1.call-done) | copy-start | bytes 294916
  1063.5 335.6 %copy-start.170 = (f32[3,16,2048]{2,1,0:T(8,128)S(1)}, f32[3,16,2048]{2,1,0:T(8,128)}, u32[]{:S(2)}) copy-start(f32[3,16,2048]{2,1,0:T(8,128)} %reduce-scatter.9.cloned.1.call-done) | copy-start | bytes 1179652
  1065.2 335.2 %copy-start.169 = (f32[3,64,512]{2,1,0:T(8,128)S(1)}, f32[3,64,512]{2,1,0:T(8,128)}, u32[]{:S(2)}) copy-start(f32[3,64,512]{2,1,0:T(8,128)} %param.39) | copy-start | bytes 1179652
  1065.2 335.2 %copy-start.327 = (f32[3]{0:T(128)S(1)}, f32[3]{0:T(128)}, u32[]{:S(2)}) copy-start(f32[3]{0:T(128)} %get-tuple-element.99) | copy-start | bytes 40
  1218.8 181.6 %copy-start.171 = (f32[3,64,512]{2,1,0:T(8,128)S(1)}, f32[3,64,512]{2,1,0:T(8,128)}, u32[]{:S(2)}) copy-start(f32[3,64,512]{2,1,0:T(8,128)} %reduce-scatter.11.cloned.1.call-done) | copy-start | bytes 1179652
  (328 other events, 1665.7 us)
Sparse Core Ops, SparseCore 0:
  11.5 66.4 all-gather.4
  81.4 53.6 all-gather.6
  138.6 68.0 all-gather.8
  210.0 67.9 all-gather.10
  629.9 137.1 reduce-scatter.6
  773.9 131.7 reduce-scatter.4
  907.9 155.4 reduce-scatter.8
  1065.8 153.0 reduce-scatter.10
  1225.0 118.6 all-reduce.6
where the time goes:
time: 1420 us; the launch traced here: 1410 us
  waiting for transfers between devices  719 us (51%)
  matrix products  332 us (23%)
  local copies, waits for them, and re-layouts  146 us (10%)
  other arithmetic  144 us (10%)
  blocking collectives  41.9 us (3%)
  between operations  27.3 us (2%)
    reduce_scatter x1, waiting for transfers between devices, local(): lax.psum_scatter(running[2], ('dp', 'fsdp'), scatter_dimension=1, tiled=T...  155 us
    reduce_scatter x1, waiting for transfers between devices, local(): lax.psum_scatter(running[3], ('dp', 'fsdp'), scatter_dimension=1, tiled=T...  153 us
    psum x1, waiting for transfers between devices, local(): lax.psum((small_grad, bias_grad, totals), ('dp', 'fsdp'))  122 us
    reduce_scatter x1, waiting for transfers between devices, local(): lax.psum_scatter(running[0], ('dp', 'fsdp'), scatter_dimension=1, tiled=T...  104 us
    all_gather x1, waiting for transfers between devices, fetch_stacks(): lax.all_gather(down_weight.astype(LOWER), ('dp', 'fsdp'), axis=1, tiled=T...  66.2 us
    all_gather x1, waiting for transfers between devices, fetch_stacks(): lax.all_gather(up_weight.astype(LOWER), ('dp', 'fsdp'), axis=1, tiled=True)  60.3 us
    dot_general x6, matrix products, backward_layer(): jnp.einsum('qhe,khe->hqk', d_mixed, values, preferred_element_type=WIDE)  46.5 us
    psum x1, blocking collectives, local(): lax.psum((small_grad, bias_grad, totals), ('dp', 'fsdp'))  41.9 us
  transfers between devices with their start and end apart: 9, of which 8 were waited for; matrix products, arithmetic and copies ran while one was open for 17% of the time, Pallas kernels for 0%

commit v1 on v0

v1 whole, which is shorter than its diff:
```python
import functools
import math

import jax
import jax.numpy as jnp
from jax import lax
from jax.experimental import pallas as pl
from jax.experimental.pallas import tpu as pltpu
from jax.sharding import PartitionSpec as P

D = 512
H = 8
HD = 64
FF = 2048
S = 11
A = 3
K = 20
STEP = 10

EPS = 1e-05
CLIP = 1.0
LEARN = 0.03
BETA_ONE = 0.5
BETA_TWO = 0.7
DECAY = 0.01
ADAM_EPS = 1e-08
TEMP_RATE = 0.1
MASKED = -1e30
HALF_LOG_TAU = 0.5 * math.log(2.0 * math.pi)
GELU_C = math.sqrt(2.0 / math.pi)
GELU_A = 0.044715
HIGH = lax.Precision.HIGHEST
LOWER = jnp.bfloat16
WIDE = jnp.float32

LAYERS = 3
WINS = 16
SLOT = 64
ROWS = WINS * SLOT
CHUNK = 256
CHUNKS = ROWS // CHUNK
GROUP = 128
BLOCKS = 32
PACK = 192
EMB = S + A + 1 + K + 3
FIN = EMB
HEADW = EMB + 2
BASE = EMB + 2 + 2 * A
PER = 9 + FF // D
NROWS = BASE + LAYERS * PER
SMALL = 88


def dot(a, b, precision=None):
    return lax.dot_general(
        a, b, (((1,), (0,)), ((), ())), precision=precision, preferred_element_type=WIDE
    )


def dot_nt(a, b, precision=None):
    return lax.dot_general(
        a, b, (((1,), (1,)), ((), ())), precision=precision, preferred_element_type=WIDE
    )


def dot_tn(a, b, precision=None):
    return lax.dot_general(
        a, b, (((0,), (0,)), ((), ())), precision=precision, preferred_element_type=WIDE
    )


def iota(shape, dim):
    return lax.broadcasted_iota(jnp.int32, shape, dim)


def col_sum(v):
    return jnp.sum(v, 0, keepdims=True)


def row_mean(v):
    return jnp.mean(v, -1, keepdims=True)


def norm_parts(x):
    center = x - row_mean(x)
    scale = lax.rsqrt(row_mean(center * center) + EPS)
    return center * scale, scale


def norm_back(xhat, scale, gain, grad):
    scaled = grad * gain
    return scale * (scaled - row_mean(scaled) - xhat * row_mean(scaled * xhat))


def token_rows(at, count):
    row = at + iota((count, 128), 0)
    place = row & (SLOT - 1)
    step = (place * 21846) >> 16
    return row >> 6, step, place - 3 * step, place < 3 * K


def chunk_rows(c):
    return pl.ds(pl.multiple_of(c * CHUNK, CHUNK), CHUNK)


class Kit:
    def __init__(self, **refs):
        self.__dict__.update(refs)

    def row(self, l, k):
        return self.lrows[l, k : k + 1, :]

    def w(self, l, first, count=16):
        return self.wg[l, :, first : first + count, :].reshape(BLOCKS * count, D)

    def w_qkv(self, l, j):
        return self.w(l, 16 * j)

    def w_out(self, l):
        return self.w(l, 48)

    def w_up(self, l, j):
        return self.w(l, 64 + 16 * j)

    def w_down(self, l, j):
        return self.wg[l, pl.ds(8 * j, 8), 128:192, :].reshape(D, D)


def setup_stage(k):
    k.emb[...] = jnp.zeros_like(k.emb)
    k.emb[0:EMB, :] = k.small[0:EMB, :]
    k.headw[...] = jnp.zeros_like(k.headw)
    k.headw[0, 0:A, :] = k.small[HEADW : HEADW + A, :].astype(LOWER)
    k.headw[1, 0:A, :] = k.small[HEADW + A : HEADW + 2 * A, :].astype(LOWER)
    for l in range(LAYERS):
        k.lrows[l, 0:PER, :] = k.small[BASE + l * PER : BASE + (l + 1) * PER, :]
    k.sgl[...] = jnp.zeros_like(k.sgl)
    k.sgh[...] = jnp.zeros_like(k.sgh)
    k.sgw[...] = jnp.zeros_like(k.sgw)

    meta = k.meta[...].astype(LOWER)
    lane = iota((128, 128), 1)
    sub = iota((128, 128), 0)
    half = lane & (SLOT - 1)
    pick = sub - 2 == ((half * 21846) >> 16)
    pick_lo = (pick & (lane < SLOT)).astype(WIDE).astype(LOWER)
    pick_hi = (pick & (lane >= SLOT)).astype(WIDE).astype(LOWER)
    low = dot(meta, pick_lo).astype(LOWER)
    high = dot(meta, pick_hi).astype(LOWER)
    even = (lane == 2 * sub).astype(WIDE).astype(LOWER)
    odd = (lane == 2 * sub + 1).astype(WIDE).astype(LOWER)
    k.live[...] = (dot(even, low) + dot(odd, high))[0:8]
    same = (sub >> 6) == (lane >> 6)
    for g in range(ROWS // GROUP):
        live = k.live[g : g + 1, :] > 0.5
        allowed = same & (lane <= sub) & (live | (lane == sub))
        k.bias[g] = jnp.where(allowed, 0.0, MASKED)

    def chunk(c, carry):
        rows = chunk_rows(c)
        win, step, kind, real = token_rows(c * CHUNK, CHUNK)
        lane = iota((CHUNK, 128), 1)
        tok = dot((lane == win).astype(WIDE).astype(LOWER), meta)
        start, repeat = tok[:, 0:1], tok[:, 1:2]
        valid = jnp.sum(jnp.where(lane == step + 2, tok, 0.0), -1, keepdims=True)
        place = start.astype(jnp.int32) + step
        source = ((lane == place) & real).astype(WIDE)
        raw = dot(source, k.buf[...], HIGH)
        mine = (
            ((lane < S) & (kind == 1))
            | ((lane >= S) & (lane < S + A) & (kind == 2))
            | ((lane == S + A) & (kind == 0))
        )
        marks = ((lane == S + A + 1 + step) | (lane == S + A + 1 + K + kind)) & real
        feats = jnp.where(mine, raw, 0.0) + marks.astype(WIDE)
        k.feats[rows, :] = feats
        weight = jnp.where((kind == 1) & real, repeat * valid, 0.0)
        acts = pltpu.roll(raw, 128 - S, 1)
        k.acts[rows, :] = jnp.where(lane < A, acts, jnp.where(lane == A, weight, 0.0))
        k.xs[0, rows, :] = dot(feats, k.emb[...], HIGH)
        return carry

    lax.fori_loop(0, CHUNKS, chunk, 0)


def pair_masks(rows):
    lane = iota((rows, 128), 1)
    return lane < HD


def stack_pair(v, first):
    zero = jnp.zeros_like(v)
    return jnp.concatenate([jnp.where(first, v, zero), jnp.where(first, zero, v)], 0)


def forward_attn(k, l):
    def chunk(c, carry):
        rows = chunk_rows(c)
        xhat, _ = norm_parts(k.xs[l, rows, :])
        normed = (xhat * k.row(l, 0) + k.row(l, 1)).astype(LOWER)
        for j in range(3):
            part = dot(normed, k.w_qkv(l, j)) + k.row(l, 4 + j)
            k.qkv[l, rows, j * D : (j + 1) * D] = part.astype(LOWER)
        return carry

    lax.fori_loop(0, CHUNKS, chunk, 0)
    first = pair_masks(GROUP)

    def group(g, carry):
        rows = pl.ds(pl.multiple_of(g * GROUP, GROUP), GROUP)
        bias = k.bias[g]
        bias = jnp.concatenate([bias, bias], 0)
        lane = iota((GROUP, 128), 1)
        logs = jnp.zeros((GROUP, 128), WIDE)
        for p in range(H // 2):
            at = p * 128
            query = k.qkv[l, rows, at : at + 128] * jnp.asarray(HD**-0.5, LOWER)
            keyed = k.qkv[l, rows, D + at : D + at + 128]
            values = k.qkv[l, rows, 2 * D + at : 2 * D + at + 128]
            scores = dot_nt(stack_pair(query, first), keyed) + bias
            peak = jnp.max(scores, -1, keepdims=True)
            expo = jnp.exp(scores - peak)
            total = jnp.sum(expo, -1, keepdims=True)
            probs = (expo / total).astype(LOWER)
            out = dot(probs, values)
            k.mixed[l, rows, at : at + 128] = jnp.where(first, out[:GROUP], out[GROUP:]).astype(LOWER)
            lse = peak + jnp.log(total)
            logs = jnp.where(lane == 2 * p, lse[:GROUP], logs)
            logs = jnp.where(lane == 2 * p + 1, lse[GROUP:], logs)
        k.logs[l, rows, :] = logs
        return carry

    lax.fori_loop(0, ROWS // GROUP, group, 0)


def gelu_parts(h):
    square = h * h
    t = jnp.tanh(GELU_C * (h + GELU_A * h * square))
    return t, square


def forward_ffn(k, l, dest):
    def chunk(c, carry):
        rows = chunk_rows(c)
        mid = k.xs[l, rows, :] + dot(k.mixed[l, rows, :], k.w_out(l)) + k.row(l, 7)
        k.mid[l, rows, :] = mid
        xhat, _ = norm_parts(mid)
        second = (xhat * k.row(l, 2) + k.row(l, 3)).astype(LOWER)
        out = mid + k.row(l, 12)
        for j in range(4):
            h = dot(second, k.w_up(l, j)) + k.row(l, 8 + j)
            t, _ = gelu_parts(h)
            acted = (0.5 * h * (1.0 + t)).astype(LOWER)
            out = out + dot(acted, k.w_down(l, j))
        k.xs[dest, rows, :] = out
        return carry

    lax.fori_loop(0, CHUNKS, chunk, 0)


def head_stage(k, at):
    gain, bias = k.small[FIN : FIN + 1, :], k.small[FIN + 1 : FIN + 2, :]
    lane = iota((CHUNK, 128), 1)
    keep = lane < A

    def bias_row(first):
        row = jnp.zeros((1, 128), WIDE)
        at = iota((1, 128), 1)
        for a in range(A):
            row = jnp.where(at == a, k.head_bias[first + a], row)
        return row

    bias_mean, bias_spread = bias_row(0), bias_row(A)
    temp = jnp.exp(jnp.full((1, 128), k.log_temp[0], WIDE))

    def chunk(c, carry):
        rows = chunk_rows(c)
        xhat, scale = norm_parts(k.xs[at, rows, :])
        feats = (xhat * gain + bias).astype(LOWER)
        mean = dot_nt(feats, k.headw[0]) + bias_mean
        spread = jnp.tanh(dot_nt(feats, k.headw[1]) + bias_spread)
        acts = k.acts[rows, :]
        weight = acts[:, A : A + 1]
        acts = jnp.where(keep, acts, 0.0)
        target = 0.5 * (jnp.log(1.0 + acts) - jnp.log(1.0 - acts))
        shrink = jnp.exp(-spread)
        zed = (target - mean) * shrink
        terms = 0.5 * zed * zed + spread + HALF_LOG_TAU + jnp.log(1.0 - acts * acts)
        nll = jnp.sum(jnp.where(keep, terms, 0.0), -1, keepdims=True)
        entropy = jnp.sum(jnp.where(keep, spread, 0.0), -1, keepdims=True) + A * (0.5 + HALF_LOG_TAU)
        loss = weight * (nll - temp * entropy)
        sums = jnp.where(lane == 0, loss, jnp.where(lane == 1, weight * entropy, jnp.where(lane == 2, weight, 0.0)))
        d_mean = jnp.where(keep, weight * (-zed * shrink), 0.0).astype(LOWER)
        d_spread = weight * (1.0 - zed * zed - temp) * (1.0 - spread * spread)
        d_spread = jnp.where(keep, d_spread, 0.0).astype(LOWER)
        k.sgh[2:3, 0:128] += col_sum(sums)
        k.sgh[3:4, 0:128] += col_sum(d_mean.astype(WIDE))
        k.sgh[4:5, 0:128] += col_sum(d_spread.astype(WIDE))
        k.sgw[0] += dot_tn(d_mean, feats)[0:8]
        k.sgw[1] += dot_tn(d_spread, feats)[0:8]
        d_feats = dot(d_mean, k.headw[0]) + dot(d_spread, k.headw[1])
        k.sgh[0:1, :] += col_sum(d_feats * xhat)
        k.sgh[1:2, :] += col_sum(d_feats)
        k.xs[at, rows, :] = norm_back(xhat, scale, gain, d_feats)
        return carry

    lax.fori_loop(0, CHUNKS, chunk, 0)


def owner_place(i):
    z, y, x, c = i // 8, (i // 4) % 2, (i // 2) % 2, i % 2
    return c * 16 + x * 8 + y * 4 + z


def store_blocks(k, slot, first_block, first_row, count, value):
    value = value.astype(LOWER)
    for n in range(value.shape[0] // count):
        k.wg[slot, owner_place(first_block + n), first_row : first_row + count, :] = value[
            n * count : (n + 1) * count
        ]


def backward_ffn(k, l, grad):
    def before(c, carry):
        rows = chunk_rows(c)
        d_down = k.xs[grad, rows, :].astype(LOWER)
        k.work[rows, 2 * D : 3 * D] = d_down
        k.sgl[l, 12:13, :] += col_sum(d_down.astype(WIDE))
        xhat, _ = norm_parts(k.mid[l, rows, :])
        k.left[rows, :] = (xhat * k.row(l, 2) + k.row(l, 3)).astype(LOWER)
        k.dsec[rows, :] = jnp.zeros((CHUNK, D), WIDE)
        return carry

    lax.fori_loop(0, CHUNKS, before, 0)
    for j in range(4):

        def chunk(c, carry, j=j):
            rows = chunk_rows(c)
            h = dot(k.left[rows, :], k.w_up(l, j)) + k.row(l, 8 + j)
            t, square = gelu_parts(h)
            k.work[rows, 0:D] = (0.5 * h * (1.0 + t)).astype(LOWER)
            slope = 0.5 * (1.0 + t) + 0.5 * GELU_C * h * (1.0 - t * t) * (1.0 + 3.0 * GELU_A * square)
            d_acted = dot_nt(k.work[rows, 2 * D : 3 * D], k.w_down(l, j))
            d_hidden = (d_acted * slope).astype(LOWER)
            k.work[rows, D : 2 * D] = d_hidden
            k.sgl[l, 8 + j : 9 + j, :] += col_sum(d_hidden.astype(WIDE))
            k.dsec[rows, :] += dot_nt(d_hidden, k.w_up(l, j))
            return carry

        lax.fori_loop(0, CHUNKS, chunk, 0)
        store_blocks(k, l + 1, 0, 64 + 16 * j, 16, dot_tn(k.left[...], k.work[:, D : 2 * D]))
        store_blocks(k, l + 1, 8 * j, 128, 64, dot_tn(k.work[:, 0:D], k.work[:, 2 * D : 3 * D]))

    def after(c, carry):
        rows = chunk_rows(c)
        xhat, scale = norm_parts(k.mid[l, rows, :])
        d_second = k.dsec[rows, :]
        k.sgl[l, 2:3, :] += col_sum(d_second * xhat)
        k.sgl[l, 3:4, :] += col_sum(d_second)
        k.xs[grad, rows, :] += norm_back(xhat, scale, k.row(l, 2), d_second)
        return carry

    lax.fori_loop(0, CHUNKS, after, 0)


def backward_attn(k, l, grad):
    def before(c, carry):
        rows = chunk_rows(c)
        d_branch = k.xs[grad, rows, :].astype(LOWER)
        k.left[rows, :] = d_branch
        k.sgl[l, 7:8, :] += col_sum(d_branch.astype(WIDE))
        k.dmix[rows, :] = dot_nt(d_branch, k.w_out(l)).astype(LOWER)
        return carry

    lax.fori_loop(0, CHUNKS, before, 0)
    store_blocks(k, l + 1, 0, 48, 16, dot_tn(k.mixed[l], k.left[...]))
    first = pair_masks(GROUP)
    scale = HD**-0.5

    def group(g, carry):
        rows = pl.ds(pl.multiple_of(g * GROUP, GROUP), GROUP)
        bias = k.bias[g]
        bias = jnp.concatenate([bias, bias], 0)
        logs = k.logs[l, rows, :]
        for p in range(H // 2):
            at = p * 128
            query = stack_pair(k.qkv[l, rows, at : at + 128] * jnp.asarray(scale, LOWER), first)
            keyed = k.qkv[l, rows, D + at : D + at + 128]
            values = k.qkv[l, rows, 2 * D + at : 2 * D + at + 128]
            d_mixed = stack_pair(k.dmix[rows, at : at + 128], first)
            log_total = jnp.concatenate(
                [logs[:, 2 * p : 2 * p + 1], logs[:, 2 * p + 1 : 2 * p + 2]], 0
            )
            probs = jnp.exp(dot_nt(query, keyed) + bias - log_total)
            d_probs = dot_nt(d_mixed, values)
            d_values = dot_tn(probs.astype(LOWER), d_mixed)
            inner = probs * d_probs
            d_scores = (inner - probs * jnp.sum(inner, -1, keepdims=True)).astype(LOWER)
            d_query = dot(d_scores, keyed)
            d_query = jnp.where(first, d_query[:GROUP], d_query[GROUP:]) * scale
            d_keyed = dot_tn(d_scores, query)
            k.work[rows, at : at + 128] = d_query.astype(LOWER)
            k.work[rows, D + at : D + at + 128] = d_keyed.astype(LOWER)
            k.work[rows, 2 * D + at : 2 * D + at + 128] = d_values.astype(LOWER)
        return carry

    lax.fori_loop(0, ROWS // GROUP, group, 0)

    def again(c, carry):
        rows = chunk_rows(c)
        xhat, _ = norm_parts(k.xs[l, rows, :])
        k.left[rows, :] = (xhat * k.row(l, 0) + k.row(l, 1)).astype(LOWER)
        return carry

    lax.fori_loop(0, CHUNKS, again, 0)
    for j in range(3):
        store_blocks(k, l + 1, 0, 16 * j, 16, dot_tn(k.left[...], k.work[:, j * D : (j + 1) * D]))


def backward_input(k, l, grad):
    def chunk(c, carry):
        rows = chunk_rows(c)
        d_normed = jnp.zeros((CHUNK, D), WIDE)
        for j in range(3):
            d_part = k.work[rows, j * D : (j + 1) * D]
            k.sgl[l, 4 + j : 5 + j, :] += col_sum(d_part.astype(WIDE))
            d_normed = d_normed + dot_nt(d_part, k.w_qkv(l, j))
        xhat, scale = norm_parts(k.xs[l, rows, :])
        k.sgl[l, 0:1, :] += col_sum(d_normed * xhat)
        k.sgl[l, 1:2, :] += col_sum(d_normed)
        k.xs[grad, rows, :] += norm_back(xhat, scale, k.row(l, 0), d_normed)
        return carry

    lax.fori_loop(0, CHUNKS, chunk, 0)


def small_stage(k, out, grad):
    out[...] = jnp.zeros_like(out)
    out[0:EMB, :] = dot_tn(k.feats[...], k.xs[grad], HIGH)[0:EMB]
    out[FIN : FIN + 2, :] = k.sgh[0:2, :]
    out[HEADW : HEADW + A, :] = k.sgw[0, 0:A, :]
    out[HEADW + A : HEADW + 2 * A, :] = k.sgw[1, 0:A, :]
    for l in range(LAYERS):
        out[BASE + l * PER : BASE + (l + 1) * PER, :] = k.sgl[l, 0:PER, :]
    out[NROWS : NROWS + 3, :] = k.sgh[2:5, :]


WORK_SHAPES = dict(
    wg=((LAYERS + 1, BLOCKS, PACK, D), LOWER),
    xs=((LAYERS + 1, ROWS, D), WIDE),
    mid=((LAYERS, ROWS, D), WIDE),
    qkv=((LAYERS, ROWS, 3 * D), LOWER),
    mixed=((LAYERS, ROWS, D), LOWER),
    logs=((LAYERS, ROWS, 128), WIDE),
    work=((ROWS, 3 * D), LOWER),
    left=((ROWS, D), LOWER),
    dmix=((ROWS, D), LOWER),
    dsec=((ROWS, D), WIDE),
    feats=((ROWS, 128), WIDE),
    acts=((ROWS, 128), WIDE),
    bias=((ROWS // GROUP, GROUP, GROUP), WIDE),
    live=((8, 128), WIDE),
    emb=((128, D), WIDE),
    headw=((2, 128, D), LOWER),
    lrows=((LAYERS, 16, D), WIDE),
    sgl=((LAYERS, 16, D), WIDE),
    sgh=((8, D), WIDE),
    sgw=((2, 8, D), WIDE),
)


def compute_kernel(meta, buf, small, head_bias, log_temp, packed, grads, small_grad, *scratch):
    refs = dict(zip(WORK_SHAPES, scratch))
    load_sem, store_sem = scratch[len(WORK_SHAPES) :]
    k = Kit(meta=meta, buf=buf, small=small, head_bias=head_bias, log_temp=log_temp, **refs)
    loads = [
        pltpu.make_async_copy(packed.at[l], k.wg.at[l], load_sem.at[l]) for l in range(LAYERS)
    ]
    stores = [
        pltpu.make_async_copy(k.wg.at[l + 1], grads.at[l], store_sem.at[l]) for l in range(LAYERS)
    ]
    for copy in loads:
        copy.start()
    setup_stage(k)

    def forward(l, carry):
        pltpu.make_async_copy(packed.at[l], k.wg.at[l], load_sem.at[l]).wait()
        forward_attn(k, l)
        forward_ffn(k, l, l + 1)
        return carry

    lax.fori_loop(0, LAYERS, forward, 0)
    head_stage(k, LAYERS)

    def backward(n, carry):
        l = LAYERS - 1 - n
        backward_ffn(k, l, LAYERS)
        backward_attn(k, l, LAYERS)
        pltpu.make_async_copy(k.wg.at[l + 1], grads.at[l], store_sem.at[l]).start()
        backward_input(k, l, LAYERS)
        return carry

    lax.fori_loop(0, LAYERS, backward, 0)
    small_stage(k, small_grad, LAYERS)
    for copy in stores:
        copy.wait()


def vmem(shape, dtype):
    return pltpu.VMEM(shape, dtype)


def compute(meta, buf, small, head_bias, log_temp, packed):
    whole = pl.BlockSpec(memory_space=pltpu.VMEM)
    scalars = pl.BlockSpec(memory_space=pltpu.SMEM)
    anywhere = pl.BlockSpec(memory_space=pl.ANY)
    return pl.pallas_call(
        compute_kernel,
        name="train_pass",
        out_shape=(
            jax.ShapeDtypeStruct((LAYERS, BLOCKS, PACK, D), LOWER),
            jax.ShapeDtypeStruct((SMALL, D), WIDE),
        ),
        in_specs=[whole, whole, whole, scalars, scalars, anywhere],
        out_specs=(anywhere, whole),
        scratch_shapes=[vmem(*s) for s in WORK_SHAPES.values()]
        + [pltpu.SemaphoreType.DMA((LAYERS,)), pltpu.SemaphoreType.DMA((LAYERS,))],
        compiler_params=pltpu.CompilerParams(vmem_limit_bytes=66 * 1024 * 1024),
        cost_estimate=pl.CostEstimate(flops=6 * 10**10, bytes_accessed=4 * 10**7, transcendentals=10**7),
    )(meta, buf, small, head_bias, log_temp, packed)


def small_inputs(buf_states, buf_actions, buf_returns, window_starts, window_repeats, valid_steps):
    meta = jnp.concatenate(
        [window_starts[:, None], window_repeats[:, None], valid_steps], 1
    ).astype(WIDE)
    meta = jnp.pad(meta, ((0, 128 - meta.shape[0]), (0, 128 - meta.shape[1])))
    buf = jnp.concatenate([buf_states, buf_actions, buf_returns[:, None]], 1)
    buf = jnp.pad(buf, ((0, 128 - buf.shape[0]), (0, 128 - buf.shape[1])))
    return meta, buf


def adam_step(weight, grad, first, second, rate):
    first = BETA_ONE * first + (1.0 - BETA_ONE) * grad
    second = BETA_TWO * second + (1.0 - BETA_TWO) * grad * grad
    fix_one = 1.0 - BETA_ONE**STEP
    fix_two = 1.0 - BETA_TWO**STEP
    fresh = weight - rate * (
        first / fix_one / (jnp.sqrt(second / fix_two) + ADAM_EPS) + DECAY * weight
    )
    return (fresh, first, second)


def gather_packed(mats, axes, count):
    group = count // BLOCKS
    pieces = []
    for mat in mats:
        rows, wide = mat.shape[1], mat.shape[2] // D
        piece = mat.astype(LOWER).reshape(LAYERS, rows, wide, D)
        piece = lax.all_gather(piece, axes, axis=1, tiled=True)
        piece = piece.reshape(LAYERS, BLOCKS, group * rows, wide, D).transpose(0, 1, 3, 2, 4)
        pieces.append(piece.reshape(LAYERS, BLOCKS, wide * group * rows, D))
    return jnp.concatenate(pieces, 2)


def scatter_packed(grads, mats, axes):
    order = [owner_place(i) for i in range(BLOCKS)]
    grads = grads[:, jnp.array(order)].astype(WIDE)
    results, first = [], 0
    for mat in mats:
        rows, wide = mat.shape[1], mat.shape[2] // D
        total = lax.psum(1, axes) * rows
        deep = total // BLOCKS
        piece = grads[:, :, first : first + wide * deep]
        first += wide * deep
        piece = piece.reshape(LAYERS, BLOCKS, wide, deep, D).transpose(0, 1, 3, 2, 4)
        piece = piece.reshape(LAYERS, total, wide * D)
        results.append(lax.psum_scatter(piece, axes, scatter_dimension=1, tiled=True))
    return results


def local(
    buf_states,
    buf_actions,
    buf_returns,
    window_starts,
    window_repeats,
    valid_steps,
    matrix_groups,
    log_temp,
    small_rows,
    head_bias,
    qkv_weight,
    out_weight,
    up_weight,
    down_weight,
    small_first,
    bias_first,
    qkv_first,
    out_first,
    up_first,
    down_first,
    small_second,
    bias_second,
    qkv_second,
    out_second,
    up_second,
    down_second,
):
    axes = ("dp", "fsdp")
    mats = (qkv_weight, out_weight, up_weight, down_weight)
    firsts = (qkv_first, out_first, up_first, down_first)
    seconds = (qkv_second, out_second, up_second, down_second)
    meta, buf = small_inputs(
        buf_states, buf_actions, buf_returns, window_starts, window_repeats, valid_steps
    )
    packed = gather_packed(mats, axes, FF // down_weight.shape[1])
    grads, small = compute(meta, buf, small_rows, head_bias, log_temp, packed)
    big = scatter_packed(grads, mats, axes)
    small = lax.psum(small, axes)
    small_grad, totals = small[:NROWS], small[NROWS, :3]
    bias_grad = jnp.concatenate([small[NROWS + 1, :A], small[NROWS + 2, :A]])
    square = sum((jnp.sum(piece * piece) for piece in big))
    square = (
        lax.psum(square, axes) + jnp.sum(small_grad * small_grad) + jnp.sum(bias_grad * bias_grad)
    )
    grad_norm = jnp.sqrt(square)
    clip = jnp.minimum(1.0, CLIP / (grad_norm + 1e-06))
    rates = LEARN * jnp.exp2(-matrix_groups.astype(WIDE))
    results = [
        adam_step(
            mats[kind], clip * big[kind], firsts[kind], seconds[kind], rates[:, kind][:, None, None]
        )
        for kind in range(4)
    ]
    small_new = adam_step(small_rows, clip * small_grad, small_first, small_second, LEARN)
    bias_new = adam_step(head_bias, clip * bias_grad, bias_first, bias_second, LEARN)
    next_temp = log_temp - TEMP_RATE * jnp.exp(log_temp) * (totals[1] / totals[2] + A)
    return (
        (totals, grad_norm[None], next_temp)
        + small_new
        + bias_new
        + tuple(r[0] for r in results)
        + tuple(r[0].astype(LOWER) for r in results)
        + tuple(r[1] for r in results)
        + tuple(r[2] for r in results)
    )


def solution(mesh):
    rows = P(("dp", "fsdp"), None)
    vector = P(("dp", "fsdp"))
    stack = P(None, ("dp", "fsdp"), None)
    same = P()
    in_specs = (
        (rows, rows, vector, vector, vector, rows)
        + (same,) * 4
        + (stack,) * 4
        + (same,) * 2
        + (stack,) * 4
        + (same,) * 2
        + (stack,) * 4
    )
    out_specs = (same,) * 9 + (stack,) * 16
    return jax.shard_map(local, mesh=mesh, in_specs=in_specs, out_specs=out_specs, check_vma=False)
```

time: 1420 us -> 1270 us (0.89)
  matrix products: 332 us -> 0 us
  Pallas kernels: 0 us -> 194 us
  waiting for transfers between devices: 719 us -> 824 us
  other arithmetic: 144 us -> 55.6 us
    dot_general x124 -> x0, matrix products: 332 us -> none  [the longest x6 46.5 us: backward_layer(): jnp.einsum('qhe,khe->hqk', d_mixed, values, preferred_element_type=WIDE)]
    pallas_call x0 -> x1, Pallas kernels: none -> 194 us  [compute(): pl.pallas_call(compute_kernel, name='train_pass', out_shape=(jax.ShapeDty...]
    reduce_scatter x4, waiting for transfers between devices: 412 us -> 575 us  [scatter_packed(): lax.psum_scatter(piece, axes, scatter_dimension=1, tiled=True)]
    psum x1, waiting for transfers between devices: 122 us -> 0.02 us  [local(): small = lax.psum(small, axes)]
    all_gather x4, waiting for transfers between devices: 184 us -> 249 us  [gather_packed(): piece = lax.all_gather(piece, axes, axis=1, tiled=True)]
    reduce_sum x41 -> x0, other arithmetic: 35.9 us -> none  [the longest x6 11 us: backward_layer(): jnp.sum(d_qkv.astype(WIDE), 0).reshape(3, D)]
    convert_element_type x17 -> x10, other arithmetic: 60.5 us -> 26 us  [the longest x1 11.2 us: scatter_packed(): grads = grads[:, jnp.array(order)].astype(WIDE)]
    add x17 -> x0, other arithmetic: 30.4 us -> none  [the longest x4 23.4 us: local(): old + new]
  transfers between devices with their start and end apart: 9 -> 9, of which waited for: 8 -> 8; matrix products, arithmetic and copies ran while one was open for 17% -> 11% of each run, Pallas kernels for 0% -> 0%
where the time goes in v1:
time: 1270 us
  waiting for transfers between devices  824 us (65%)
  Pallas kernels  194 us (15%)
  local copies, waits for them, and re-layouts  136 us (11%)
  other arithmetic  55.6 us (4%)
  blocking collectives  36.9 us (3%)
  between operations  23 us (2%)
    reduce_scatter x4, waiting for transfers between devices, scatter_packed(): lax.psum_scatter(piece, axes, scatter_dimension=1, tiled=True)  575 us
    all_gather x4, waiting for transfers between devices, gather_packed(): piece = lax.all_gather(piece, axes, axis=1, tiled=True)  249 us
    pallas_call x1, Pallas kernels, compute(): pl.pallas_call(compute_kernel, name='train_pass', out_shape=(jax.ShapeDty...  194 us
    psum x1, blocking collectives, local(): lax.psum(square, axes) + jnp.sum(small_grad * small_grad)  36.9 us
    slice x6, local copies, waits for them, and re-layouts, scatter_packed(): piece = grads[:, :, first:first + wide * deep]  33.1 us
    reshape x2, local copies, waits for them, and re-layouts, scatter_packed(): piece = piece.reshape(LAYERS, total, wide * D)  31.8 us
  transfers between devices with their start and end apart: 9, of which 8 were waited for; matrix products, arithmetic and copies ran while one was open for 11% of the time, Pallas kernels for 0%

profile of v1, /device:TPU:0, one launch (start us, length us, event | category | flops | bytes accessed | tf_op | source)
XLA Modules:
  0.0 1270.3 jit_solution(14082307307229360082)
XLA Ops:
  7.2 1.0 convert_element_type.38
  8.2 0.8 reshape.98
  9.1 1.0 convert_element_type.40
  10.1 0.8 reshape.102
  11.0 1.5 convert_element_type.39
  12.6 1.7 convert_element_type.41
  15.0 0.7 pad_maximum_fusion.1
  15.8 0.7 copy.84
  17.9 0.8 add_convert_fusion
  19.4 1.3 pad_clamp_fusion
  20.6 62.7 %all-gather.7.cloned.1.call-done = bf16[3,512,3,512]{3,2,1,0:T(4,128)(2,1)} async-done(((bf16[3,16,3,512]{3,2,1,0:T(4,128)(2,1)}), bf16[3,512,3,512]{3,2,1,0:T(4,128)(2,1)}) %all-gather.7.cloned.1.call-update) | async-done | bytes 4718608 | tf_op jit(solution)/shard_map/all_gather | solution.py:560
  83.3 4.0 copy.87
  87.3 2.7 copy.88
  90.0 64.9 %all-gather.9.cloned.1.call-done = bf16[3,512,4,512]{3,2,1,0:T(4,128)(2,1)} async-done(((bf16[3,16,4,512]{3,2,1,0:T(4,128)(2,1)}), bf16[3,512,4,512]{3,2,1,0:T(4,128)(2,1)}) %all-gather.9.cloned.1.call-update) | async-done | bytes 6291472 | tf_op jit(solution)/shard_map/all_gather | solution.py:560
  154.8 4.1 copy.89
  159.0 3.4 copy.90
  162.4 49.7 %all-gather.11.cloned.1.call-done = bf16[3,512,512]{2,1,0:T(8,128)(2,1)} async-done(((bf16[3,16,512]{2,1,0:T(8,128)(2,1)}), bf16[3,512,512]{2,1,0:T(8,128)(2,1)}) %all-gather.11.cloned.1.call-update) | async-done | bytes 1572880 | tf_op jit(solution)/shard_map/all_gather | solution.py:560
  212.1 71.4 %all-gather.13.cloned.1.call-done = bf16[3,2048,512]{2,1,0:T(8,128)(2,1)} async-done(((bf16[3,64,512]{2,1,0:T(8,128)(2,1)}), bf16[3,2048,512]{2,1,0:T(8,128)(2,1)}) %all-gather.13.cloned.1.call-update) | async-done | bytes 6291472 | tf_op jit(solution)/shard_map/all_gather | solution.py:560
  283.5 16.3 %pad_maximum_fusion.packed = bf16[3,32,192,512]{3,2,1,0:T(8,128)(2,1)} fusion(bf16[3,32,64,512]{3,2,1,0:T(8,128)(2,1)} %bitcast.41, bf16[3,32,64,512]{3,2,1,0:T(8,128)(2,1)} %bitcast.36, bf16[3,32,16,512]{3,2,1,0:T(8,128)(2,1)} %bitcast.42, bf16[3,32,48,512]{3,2,1,0:T(8,128)(2,1)} %bitcast.38), kind=kLoop, calls=%fused_computation.2 | loop fusion | flops 75497472 | bytes 37748736 | tf_op jit(solution)/shard_map/concatenate | solution.py:563
  299.8 193.6 %train_pass.1 = (bf16[3,32,192,512]{3,2,1,0:T(8,128)(2,1)}, f32[88,512]{1,0:T(8,128)}) custom-call(f32[128,128]{1,0:T(8,128)} %pad.8.meta, f32[128,128]{1,0:T(8,128)} %pad.9.buf, f32[85,512]{1,0:T(8,128)} %small.1, f32[6]{0:T(128)} %head_bias.1, f32[1]{0:T(128)S(6)} %copy.98.log_temp, bf16[3,32,192,512]{3,2,1,0:T(8,128)(2,1)} %pad_maximum_fusion.packed), custom_call_target="tpu_custom_call" | custom-call | flops 60000002048 | bytes 40000000 | tf_op jit(solution)/shard_map/train_pass/pallas_call | solution.py:517
  493.5 14.9 %gather_fusion = bf16[32,3,192,512]{3,2,1,0:T(8,128)(2,1)} fusion(bf16[3,32,192,512]{3,2,1,0:T(8,128)(2,1)} %get-tuple-element.28, s32[1024]{0:T(1024)} %pad_clamp_fusion), kind=kCustom, calls=%fused_computation | custom fusion | bytes 37748864 | tf_op jit(solution)/shard_map/gather | solution.py:568
  508.4 11.2 convert_bitcast_fusion
  519.6 12.5 copy-done
  532.7 1.9 copy.92
  534.8 3.7 slice-done
  538.5 11.0 copy.96
  549.4 16.0 %reshape.107 = f32[3,512,1536]{2,1,0:T(8,128)} reshape(f32[3,32,16,3,512]{4,3,2,1,0:T(4,128)} %bitcast.35) | data formatting | bytes 18874368 | tf_op jit(solution)/shard_map/reshape | solution.py:577
  565.5 15.0 %fusion.17 = (f32[3,32,64,512]{3,2,0,1:T(8,128)}, f32[3,32,64,512]{3,2,0,1:T(8,128)S(1)}) fusion(f32[3,32,192,512]{3,2,0,1:T(8,128)} %copy-done), kind=kLoop, calls=%fused_computation.57 | loop fusion | bytes 50331648 | tf_op jit(solution)/shard_map/slice | solution.py:574
  580.4 11.1 copy.93
  591.5 15.8 %reshape.109 = f32[3,512,2048]{2,1,0:T(8,128)} reshape(f32[3,32,16,4,512]{4,3,2,1,0:T(4,128)} %copy.93) | data formatting | bytes 25165824 | tf_op jit(solution)/shard_map/reshape | solution.py:577
  607.3 11.9 copy.94
  620.2 1.5 fusion.18
  623.0 1.3 slice_bitcast_fusion.1
  625.0 1.6 multiply_reduce_fusion.3
  626.6 130.6 %reduce-scatter.7.cloned.1.call-done = f32[3,16,512]{2,1,0:T(8,128)} async-done(((f32[3,512,512]{2,1,0:T(8,128)}), f32[3,16,512]{2,1,0:T(8,128)}) %reduce-scatter.7.cloned.1.call-update) | async-done | bytes 98320 | tf_op jit(solution)/shard_map/reduce_scatter | solution.py:578
  757.1 1.5 multiply_reduce_fusion.4
  758.7 136.8 %reduce-scatter.5.cloned.1.call-done = f32[3,16,1536]{2,1,0:T(8,128)} async-done(((f32[3,512,1536]{2,1,0:T(8,128)}), f32[3,16,1536]{2,1,0:T(8,128)}) %reduce-scatter.5.cloned.1.call-update) | async-done | bytes 294928 | tf_op jit(solution)/shard_map/reduce_scatter | solution.py:578
  895.5 1.6 multiply_reduce_fusion.2
  898.4 155.3 %reduce-scatter.9.cloned.1.call-done = f32[3,16,2048]{2,1,0:T(8,128)} async-done(((f32[3,512,2048]{2,1,0:T(8,128)}), f32[3,16,2048]{2,1,0:T(8,128)}) %reduce-scatter.9.cloned.1.call-update) | async-done | bytes 393232 | tf_op jit(solution)/shard_map/reduce_scatter | solution.py:578
  1053.7 1.7 multiply_reduce_fusion.1
  1056.0 152.8 %reduce-scatter.11.cloned.1.call-done = f32[3,64,512]{2,1,0:T(8,128)} async-done(((f32[3,2048,512]{2,1,0:T(8,128)}), f32[3,64,512]{2,1,0:T(8,128)}) %reduce-scatter.11.cloned.1.call-update) | async-done | bytes 393232 | tf_op jit(solution)/shard_map/reduce_scatter | solution.py:578
  1208.8 1.7 multiply_reduce_fusion
  1211.1 36.9 %psum.15 = f32[]{:T(128)} all-reduce(f32[]{:T(128)S(6)} %add.141), channel_id=1, replica_groups=mesh['dp'=8,'fsdp'=4] {'dp','fsdp'}, use_global_device_ids=true, to_apply=%region_9.10 | all-reduce | flops 1 | bytes 8 | tf_op jit(solution)/shard_map/psum | solution.py:625
  1250.6 2.0 multiply_subtract_fusion.3
  1252.7 2.4 fusion.7
  1255.1 2.4 fusion.9
  1257.5 1.8 fusion.11
  1259.3 2.2 fusion.13
  (60 shorter events, 5.2 us)
Async XLA Ops:
  7.2 76.1 %all-gather.7.cloned.1.call-start = ((), (), s32[]{:S(2)}) async-start(), calls=%async_computation.4 | async-start | bytes 6488064 | tf_op jit(solution)/shard_map/all_gather | solution.py:560
  9.0 145.8 %all-gather.9.cloned.1.call-start = ((), (), s32[]{:S(2)}) async-start(), calls=%async_computation.5 | async-start | bytes 6488064 | tf_op jit(solution)/shard_map/all_gather | solution.py:560
  10.9 201.2 %all-gather.11.cloned.1.call-start = ((), (), s32[]{:S(2)}) async-start(), calls=%async_computation.11 | async-start | bytes 1622016 | tf_op jit(solution)/shard_map/all_gather | solution.py:560
  12.5 271.0 %all-gather.13.cloned.1.call-start = ((), (), s32[]{:S(2)}) async-start(), calls=%async_computation.12 | async-start | bytes 6488064 | tf_op jit(solution)/shard_map/all_gather | solution.py:560
  14.3 605.9 %all-reduce.4.cloned.1.call-start = ((), (), s32[]{:S(2)}) async-start(), calls=%async_computation.6 | async-start | bytes 360448 | tf_op jit(solution)/shard_map/psum | solution.py:620
  493.5 263.7 %reduce-scatter.7.cloned.1.call-start = ((), (), s32[]{:S(2)}) async-start(), calls=%async_computation.8 | async-start | bytes 3244032 | tf_op jit(solution)/shard_map/reduce_scatter | solution.py:578
  519.6 12.5 copy-start
  534.7 360.8 %reduce-scatter.5.cloned.1.call-start = ((), (), s32[]{:S(2)}) async-start(), calls=%async_computation.7 | async-start | bytes 9732096 | tf_op jit(solution)/shard_map/reduce_scatter | solution.py:578
  534.7 3.7 slice-start
  565.4 488.2 %reduce-scatter.9.cloned.1.call-start = ((), (), s32[]{:S(2)}) async-start(), calls=%async_computation.9 | async-start | bytes 12976128 | tf_op jit(solution)/shard_map/reduce_scatter | solution.py:578
  607.3 601.5 %reduce-scatter.11.cloned.1.call-start = ((), (), s32[]{:S(2)}) async-start(), calls=%async_computation.10 | async-start | bytes 12976128 | tf_op jit(solution)/shard_map/reduce_scatter | solution.py:578
  619.2 0.7 copy-start.12
  619.2 630.8 %copy-start.13 = (f32[6]{0:T(128)S(1)}, f32[6]{0:T(128)}, u32[]{:S(2)}) copy-start(f32[6]{0:T(128)} %head_bias.1) | copy-start | bytes 76
  619.2 630.8 %copy-start.14 = (f32[6]{0:T(128)S(1)}, f32[6]{0:T(128)}, u32[]{:S(2)}) copy-start(f32[6]{0:T(128)} %param.42) | copy-start | bytes 76
  619.3 630.8 %copy-start.15 = (f32[6]{0:T(128)S(1)}, f32[6]{0:T(128)}, u32[]{:S(2)}) copy-start(f32[6]{0:T(128)} %param.48) | copy-start | bytes 76
  619.3 631.4 %copy-start.11 = (f32[85,512]{1,0:T(8,128)S(1)}, f32[85,512]{1,0:T(8,128)}, u32[]{:S(2)}) copy-start(f32[85,512]{1,0:T(8,128)} %small.1) | copy-start | bytes 522244
  619.3 633.4 %copy-start.1 = (f32[3,64,512]{2,1,0:T(8,128)S(1)}, f32[3,64,512]{2,1,0:T(8,128)}, u32[]{:S(2)}) copy-start(f32[3,64,512]{2,1,0:T(8,128)} %param.40) | copy-start | bytes 1179652
  619.3 633.4 %copy-start.5 = (f32[3,64,512]{2,1,0:T(8,128)S(1)}, f32[3,64,512]{2,1,0:T(8,128)}, u32[]{:S(2)}) copy-start(f32[3,64,512]{2,1,0:T(8,128)} %param.46) | copy-start | bytes 1179652
  619.3 633.4 %copy-start.6 = (f32[3,64,512]{2,1,0:T(8,128)S(1)}, f32[3,64,512]{2,1,0:T(8,128)}, u32[]{:S(2)}) copy-start(f32[3,64,512]{2,1,0:T(8,128)} %param.52) | copy-start | bytes 1179652
  619.3 635.8 %copy-start.2 = (f32[3,16,2048]{2,1,0:T(8,128)S(1)}, f32[3,16,2048]{2,1,0:T(8,128)}, u32[]{:S(2)}) copy-start(f32[3,16,2048]{2,1,0:T(8,128)} %param.39) | copy-start | bytes 1179652
  619.3 635.8 %copy-start.7 = (f32[3,16,2048]{2,1,0:T(8,128)S(1)}, f32[3,16,2048]{2,1,0:T(8,128)}, u32[]{:S(2)}) copy-start(f32[3,16,2048]{2,1,0:T(8,128)} %param.45) | copy-start | bytes 1179652
  619.3 635.7 %copy-start.8 = (f32[3,16,2048]{2,1,0:T(8,128)S(1)}, f32[3,16,2048]{2,1,0:T(8,128)}, u32[]{:S(2)}) copy-start(f32[3,16,2048]{2,1,0:T(8,128)} %param.51) | copy-start | bytes 1179652
  619.3 638.2 %copy-start.4 = (f32[3,16,512]{2,1,0:T(8,128)S(1)}, f32[3,16,512]{2,1,0:T(8,128)}, u32[]{:S(2)}) copy-start(f32[3,16,512]{2,1,0:T(8,128)} %param.38) | copy-start | bytes 294916
  619.4 639.9 %copy-start.3 = (f32[3,16,1536]{2,1,0:T(8,128)S(1)}, f32[3,16,1536]{2,1,0:T(8,128)}, u32[]{:S(2)}) copy-start(f32[3,16,1536]{2,1,0:T(8,128)} %param.37) | copy-start | bytes 884740
  619.4 639.9 %copy-start.9 = (f32[3,16,1536]{2,1,0:T(8,128)S(1)}, f32[3,16,1536]{2,1,0:T(8,128)}, u32[]{:S(2)}) copy-start(f32[3,16,1536]{2,1,0:T(8,128)} %param.43) | copy-start | bytes 884740
  619.4 639.9 %copy-start.10 = (f32[3,16,1536]{2,1,0:T(8,128)S(1)}, f32[3,16,1536]{2,1,0:T(8,128)}, u32[]{:S(2)}) copy-start(f32[3,16,1536]{2,1,0:T(8,128)} %param.49) | copy-start | bytes 884740
Sparse Core Ops, SparseCore 0:
  11.5 71.7 all-gather.6
  86.8 67.9 all-gather.8
  158.3 53.7 all-gather.10
  215.5 68.0 all-gather.12
  493.6 121.3 all-reduce.3
  617.1 139.9 reduce-scatter.6
  764.0 131.3 reduce-scatter.4
  897.8 155.8 reduce-scatter.8
  1056.0 152.7 reduce-scatter.10

commit v2 on v1

--- a/solution.py
+++ b/solution.py
@@ -111,7 +111,7 @@
         return self.lrows[l, k : k + 1, :]
 
     def w(self, l, first, count=16):
-        return self.wg[l, :, first : first + count, :].reshape(BLOCKS * count, D)
+        return self.wg[l, :, :, first : first + count, :].reshape(BLOCKS * count, D)
 
     def w_qkv(self, l, j):
         return self.w(l, 16 * j)
@@ -123,7 +123,7 @@
         return self.w(l, 64 + 16 * j)
 
     def w_down(self, l, j):
-        return self.wg[l, pl.ds(8 * j, 8), 128:192, :].reshape(D, D)
+        return self.wg[l, j, :, 128:192, :].reshape(D, D)
 
 
 def setup_stage(k):
@@ -315,7 +315,8 @@
 def store_blocks(k, slot, first_block, first_row, count, value):
     value = value.astype(LOWER)
     for n in range(value.shape[0] // count):
-        k.wg[slot, owner_place(first_block + n), first_row : first_row + count, :] = value[
+        place = owner_place(first_block + n)
+        k.wg[slot, place // 8, place % 8, first_row : first_row + count, :] = value[
             n * count : (n + 1) * count
         ]
 
@@ -446,7 +447,7 @@
 
 
 WORK_SHAPES = dict(
-    wg=((LAYERS + 1, BLOCKS, PACK, D), LOWER),
+    wg=((LAYERS + 1, BLOCKS // 8, 8, PACK, D), LOWER),
     xs=((LAYERS + 1, ROWS, D), WIDE),
     mid=((LAYERS, ROWS, D), WIDE),
     qkv=((LAYERS, ROWS, 3 * D), LOWER),
@@ -518,7 +519,7 @@
         compute_kernel,
         name="train_pass",
         out_shape=(
-            jax.ShapeDtypeStruct((LAYERS, BLOCKS, PACK, D), LOWER),
+            jax.ShapeDtypeStruct((LAYERS, BLOCKS // 8, 8, PACK, D), LOWER),
             jax.ShapeDtypeStruct((SMALL, D), WIDE),
         ),
         in_specs=[whole, whole, whole, scalars, scalars, anywhere],
@@ -540,7 +541,475 @@
     return meta, buf
 
 
-def adam_step(weight, grad, first, second, rate):
+MESH = pl.DeviceIdType.MESH
+NZ, NY, NX, NC = 4, 2, 2, 2
+NR = NY * NX * NC
+SHARD = PACK
+ATTN, FFN = (0, 64), (64, 128)
+
+
+class Place:
+    def __init__(self):
+        dp, fsdp = lax.axis_index("dp"), lax.axis_index("fsdp")
+        self.z, self.y = dp // NY, dp % NY
+        self.x, self.c = fsdp // NC, fsdp % NC
+        self.r = self.y * 4 + self.x * 2 + self.c
+        self.r_x = self.y * 4 + (1 - self.x) * 2 + self.c
+        self.r_y = (1 - self.y) * 4 + self.x * 2 + self.c
+        self.r_xy = (1 - self.y) * 4 + (1 - self.x) * 2 + self.c
+        self.to_x = (dp, (1 - self.x) * NC + self.c)
+        self.to_y = (self.z * NY + 1 - self.y, fsdp)
+        self.to_c = (dp, self.x * NC + 1 - self.c)
+        self.to_z = [(((self.z + d) % NZ) * NY + self.y, fsdp) for d in range(1, NZ)]
+
+    def barrier(self):
+        partners = [self.to_x, self.to_y, self.to_c] + self.to_z
+        sem = pltpu.get_barrier_semaphore()
+        for partner in partners:
+            pl.semaphore_signal(sem, inc=1, device_id=partner, device_id_type=MESH)
+        pl.semaphore_wait(sem, len(partners))
+
+
+class Gather:
+    COPIES = 11
+
+    def __init__(self, place, wg, send, recv):
+        self.at, self.wg, self.send, self.recv = place, wg, send, recv
+
+    def copy(self, l, part, n, z, r, rows, to):
+        q = 2 * l + part
+        ref = self.wg.at[l, z, r, pl.ds(*rows), :]
+        return pltpu.make_async_remote_copy(
+            src_ref=ref,
+            dst_ref=ref,
+            send_sem=self.send.at[q, n],
+            recv_sem=self.recv.at[q, n],
+            device_id=to,
+            device_id_type=MESH,
+        )
+
+    def copies(self, l, part):
+        at = self.at
+        first, count = (ATTN, FFN)[part]
+        rows, top, low = (first, count), (first, count // 2), (first + count // 2, count // 2)
+        column = pl.ds(0, NZ)
+        return (
+            [self.copy(l, part, n, at.z, at.r, rows, at.to_z[n]) for n in range(3)]
+            + [
+                self.copy(l, part, 3, column, at.r, rows, at.to_x),
+                self.copy(l, part, 4, column, at.r, rows, at.to_y),
+                self.copy(l, part, 5, column, at.r, rows, at.to_c),
+                self.copy(l, part, 6, column, at.r_x, top, at.to_y),
+                self.copy(l, part, 7, column, at.r_y, low, at.to_x),
+                self.copy(l, part, 8, column, at.r_x, rows, at.to_c),
+                self.copy(l, part, 9, column, at.r_y, rows, at.to_c),
+                self.copy(l, part, 10, column, at.r_xy, rows, at.to_c),
+            ]
+        )
+
+    def first(self, l, part):
+        for copy in self.copies(l, part)[0:3]:
+            copy.start()
+
+    def second(self, l, part):
+        c = self.copies(l, part)
+        for n in range(3):
+            c[n].wait_recv()
+        for n in (3, 4, 5):
+            c[n].start()
+
+    def third(self, l, part):
+        c = self.copies(l, part)
+        c[3].wait_recv()
+        c[6].start()
+        c[8].start()
+        c[4].wait_recv()
+        c[7].start()
+        c[9].start()
+
+    def fourth(self, l, part):
+        c = self.copies(l, part)
+        c[6].wait_recv()
+        c[7].wait_recv()
+        c[10].start()
+
+    def last(self, l, part):
+        c = self.copies(l, part)
+        for n in (5, 8, 9, 10):
+            c[n].wait_recv()
+
+    def sent(self, l, part):
+        for copy in self.copies(l, part):
+            copy.wait_send()
+
+
+def pack_rows(wg, l, z, r, mats):
+    qkv, out, up, down = mats
+    for j in range(3):
+        wg[l, z, r, 16 * j : 16 * j + 16, :] = qkv[l, :, j * D : (j + 1) * D].astype(LOWER)
+    wg[l, z, r, 48:64, :] = out[l].astype(LOWER)
+    for j in range(4):
+        wg[l, z, r, 64 + 16 * j : 80 + 16 * j, :] = up[l, :, j * D : (j + 1) * D].astype(LOWER)
+    wg[l, z, r, 128:192, :] = down[l].astype(LOWER)
+
+
+class Reduce:
+    COPIES = 8
+
+    def __init__(self, place, g, r0, r1a, r1b, r2, r3, send, recv):
+        self.at, self.g, self.r0, self.r1a, self.r1b = place, g, r0, r1a, r1b
+        self.r2, self.r3, self.send, self.recv = r2, r3, send, recv
+
+    def rows(self, part):
+        first, count = (ATTN, FFN)[part]
+        half = count // 2
+        return first, count, first, first + half, half, (0, 32)[part]
+
+    def copies(self, slot, buf, part):
+        at = self.at
+        first, count, top, low, half, one = self.rows(part)
+        rows, a, b, h = pl.ds(first, count), pl.ds(top, half), pl.ds(low, half), pl.ds(one, half)
+        q = 2 * slot + part
+        r0, r1a, r1b, r2, r3 = (
+            ref.at[buf] for ref in (self.r0, self.r1a, self.r1b, self.r2, self.r3)
+        )
+        other = pl.ds(4 * (1 - at.y), 4)
+
+        def copy(n, src, dst, to):
+            return pltpu.make_async_remote_copy(
+                src_ref=src,
+                dst_ref=dst,
+                send_sem=self.send.at[q, n],
+                recv_sem=self.recv.at[q, n],
+                device_id=to,
+                device_id_type=MESH,
+            )
+
+        return [
+            copy(0, self.g.at[slot, pl.ds(2 * (1 - at.c), 2), :, rows, :], r0.at[:, :, rows, :], at.to_c),
+            copy(1, r0.at[1 - at.x, :, a, :], r1a.at[:, h, :], at.to_x),
+            copy(2, r0.at[:, other, b, :], r1b.at[:, :, h, :], at.to_y),
+            copy(3, r1a.at[other, h, :], r2.at[:, a, :], at.to_y),
+            copy(4, r1b.at[1 - at.x, :, h, :], r2.at[:, b, :], at.to_x),
+        ] + [
+            copy(5 + n, r2.at[(at.z + n + 1) % NZ, rows, :], r3.at[n, rows, :], at.to_z[n])
+            for n in range(3)
+        ]
+
+    def start(self, slot, buf, part):
+        self.copies(slot, buf, part)[0].start()
+
+    def wide(self, ref, *index):
+        return ref[index].astype(WIDE)
+
+    def first(self, slot, buf, part):
+        at = self.at
+        c = self.copies(slot, buf, part)
+        _, _, top, low, half, _ = self.rows(part)
+        a, b = pl.ds(top, half), pl.ds(low, half)
+        c[0].wait_recv()
+
+        def along_x(n, carry):
+            total = self.wide(self.g, slot, 2 * at.c + 1 - at.x, n, a) + self.wide(
+                self.r0, buf, 1 - at.x, n, a
+            )
+            self.r0[buf, 1 - at.x, n, a] = total.astype(LOWER)
+            return carry
+
+        lax.fori_loop(0, NR, along_x, 0)
+        c[1].start()
+
+        def along_y(n, carry):
+            x, place = n // 4, 4 * (1 - at.y) + n % 4
+            total = self.wide(self.g, slot, 2 * at.c + x, place, b) + self.wide(
+                self.r0, buf, x, place, b
+            )
+            self.r0[buf, x, place, b] = total.astype(LOWER)
+            return carry
+
+        lax.fori_loop(0, NR, along_y, 0)
+        c[2].start()
+
+    def second(self, slot, buf, part):
+        at = self.at
+        c = self.copies(slot, buf, part)
+        _, _, top, low, half, one = self.rows(part)
+        a, b, h = pl.ds(top, half), pl.ds(low, half), pl.ds(one, half)
+        c[1].wait_recv()
+
+        def along_y(n, carry):
+            place = 4 * (1 - at.y) + n
+            total = (
+                self.wide(self.g, slot, 2 * at.c + at.x, place, a)
+                + self.wide(self.r0, buf, at.x, place, a)
+                + self.wide(self.r1a, buf, place, h)
+            )
+            self.r1a[buf, place, h] = total.astype(LOWER)
+            return carry
+
+        lax.fori_loop(0, NZ, along_y, 0)
+        c[3].start()
+        c[2].wait_recv()
+
+        def along_x(n, carry):
+            place, x = 4 * at.y + n, 1 - at.x
+            total = (
+                self.wide(self.g, slot, 2 * at.c + x, place, b)
+                + self.wide(self.r0, buf, x, place, b)
+                + self.wide(self.r1b, buf, x, n, h)
+            )
+            self.r1b[buf, x, n, h] = total.astype(LOWER)
+            return carry
+
+        lax.fori_loop(0, NZ, along_x, 0)
+        c[4].start()
+
+    def chip_sums(self, slot, buf, part, z):
+        at = self.at
+        _, _, top, low, half, one = self.rows(part)
+        a, b, h = pl.ds(top, half), pl.ds(low, half), pl.ds(one, half)
+        place = 4 * at.y + z
+        mine = 2 * at.c + at.x
+        return (
+            self.wide(self.g, slot, mine, place, a)
+            + self.wide(self.r0, buf, at.x, place, a)
+            + self.wide(self.r1a, buf, place, h)
+            + self.wide(self.r2, buf, z, a),
+            self.wide(self.g, slot, mine, place, b)
+            + self.wide(self.r0, buf, at.x, place, b)
+            + self.wide(self.r1b, buf, at.x, z, h)
+            + self.wide(self.r2, buf, z, b),
+        )
+
+    def third(self, slot, buf, part):
+        at = self.at
+        c = self.copies(slot, buf, part)
+        _, _, top, low, half, _ = self.rows(part)
+        c[3].wait_recv()
+        c[4].wait_recv()
+        for n in range(3):
+            z = (at.z + n + 1) % NZ
+            upper, lower = self.chip_sums(slot, buf, part, z)
+            self.r2[buf, z, pl.ds(top, half)] = upper.astype(LOWER)
+            self.r2[buf, z, pl.ds(low, half)] = lower.astype(LOWER)
+            c[5 + n].start()
+
+    def last(self, slot, buf, part, out):
+        c = self.copies(slot, buf, part)
+        _, _, top, low, half, _ = self.rows(part)
+        upper, lower = self.chip_sums(slot, buf, part, self.at.z)
+        for n in range(3):
+            c[5 + n].wait_recv()
+            upper = upper + self.wide(self.r3, buf, n, pl.ds(top, half))
+            lower = lower + self.wide(self.r3, buf, n, pl.ds(low, half))
+        out[pl.ds(top, half), :] = upper
+        out[pl.ds(low, half), :] = lower
+        return col_sum(upper * upper) + col_sum(lower * lower)
+
+    def sent(self, slot, buf, part):
+        for copy in self.copies(slot, buf, part):
+            copy.wait_send()
+
+
+class Total:
+    COPIES = 6
+
+    def __init__(self, place, own, got, send, recv):
+        self.at, self.own, self.got, self.send, self.recv = place, own, got, send, recv
+
+    def copies(self):
+        at = self.at
+
+        def copy(n, dst, to):
+            return pltpu.make_async_remote_copy(
+                src_ref=self.own.at[min(n, 3)],
+                dst_ref=self.got.at[dst],
+                send_sem=self.send.at[n],
+                recv_sem=self.recv.at[n],
+                device_id=to,
+                device_id_type=MESH,
+            )
+
+        return [copy(n, n, to) for n, to in enumerate((at.to_c, at.to_x, at.to_y))] + [
+            copy(3 + n, 3 + n, to) for n, to in enumerate(at.to_z)
+        ]
+
+    def start(self):
+        self.copies()[0].start()
+
+    def step(self, n):
+        c = self.copies()
+        c[n].wait_recv()
+        self.own[n + 1] = self.own[n] + self.got[n]
+        if n < 2:
+            c[n + 1].start()
+        else:
+            for m in (3, 4, 5):
+                c[m].start()
+
+    def last(self):
+        c = self.copies()
+        for m in (3, 4, 5):
+            c[m].wait_recv()
+        total = None
+        for z in range(NZ):
+            term = self.own[3]
+            for n in range(3):
+                from_z = (self.at.z + NZ - 1 - n) % NZ
+                term = jnp.where(from_z == z, self.got[3 + n], term)
+            total = term if total is None else total + term
+        return total
+
+    def sent(self):
+        for copy in self.copies():
+            copy.wait_send()
+
+
+def gather_kernel(qkv, out, up, down, packed, wg, send, recv, store):
+    place = Place()
+    net = Gather(place, wg, send, recv)
+    for l in range(LAYERS):
+        pack_rows(wg, l, place.z, place.r, (qkv, out, up, down))
+    place.barrier()
+    parts = [(l, part) for l in range(LAYERS) for part in (0, 1)]
+
+    def keep(l, part):
+        rows = pl.ds(*(ATTN, FFN)[part])
+        return pltpu.make_async_copy(
+            wg.at[l, :, :, rows, :], packed.at[l, :, :, rows, :], store.at[2 * l + part]
+        )
+
+    for l, part in parts[:2]:
+        net.first(l, part)
+    for t in range(len(parts) + 3):
+        if t < len(parts):
+            net.second(*parts[t])
+        if t + 2 < len(parts):
+            net.first(*parts[t + 2])
+        if 0 <= t - 1 < len(parts):
+            net.third(*parts[t - 1])
+        if 0 <= t - 2 < len(parts):
+            net.fourth(*parts[t - 2])
+        if 0 <= t - 3 < len(parts):
+            net.last(*parts[t - 3])
+            keep(*parts[t - 3]).start()
+    for l, part in parts:
+        net.sent(l, part)
+        keep(l, part).wait()
+
+
+def gather_all(mats):
+    whole = pl.BlockSpec(memory_space=pltpu.VMEM)
+    count = 2 * LAYERS
+    return pl.pallas_call(
+        gather_kernel,
+        name="gather",
+        out_shape=jax.ShapeDtypeStruct((LAYERS, NZ, NR, PACK, D), LOWER),
+        in_specs=[whole] * 4,
+        out_specs=pl.BlockSpec(memory_space=pl.ANY),
+        scratch_shapes=[
+            pltpu.VMEM((LAYERS, NZ, NR, PACK, D), LOWER),
+            pltpu.SemaphoreType.DMA((count, Gather.COPIES)),
+            pltpu.SemaphoreType.DMA((count, Gather.COPIES)),
+            pltpu.SemaphoreType.DMA((count,)),
+        ],
+        compiler_params=pltpu.CompilerParams(
+            collective_id=0, has_side_effects=True, vmem_limit_bytes=40 * 1024 * 1024
+        ),
+        cost_estimate=pl.CostEstimate(flops=0, bytes_accessed=4 * 10**7, transcendentals=0),
+    )(*mats)
+
+
+REDUCE_SHAPES = dict(
+    r0=(NX, NR, PACK, D),
+    r1a=(NR, PACK // 2, D),
+    r1b=(NX, NZ, PACK // 2, D),
+    r2=(NZ, PACK, D),
+    r3=(3, PACK, D),
+)
+
+
+def reduce_kernel(grads, small, shard, totals, squares, g, *scratch):
+    refs = scratch[: len(REDUCE_SHAPES)]
+    send, recv, load, own_s, got_s, send_s, recv_s, own_n, got_n, send_n, recv_n = scratch[
+        len(REDUCE_SHAPES) :
+    ]
+    place = Place()
+    net = Reduce(place, g, *refs, send, recv)
+    sums = Total(place, own_s, got_s, send_s, recv_s)
+    norm = Total(place, own_n, got_n, send_n, recv_n)
+    parts = [(l, part) for l in reversed(range(LAYERS)) for part in (1, 0)]
+
+    def fetch(l, part):
+        rows = pl.ds(*(ATTN, FFN)[part])
+        return pltpu.make_async_copy(
+            grads.at[l, :, :, rows, :], g.at[l, :, :, rows, :], load.at[2 * l + part]
+        )
+
+    for l, part in parts:
+        fetch(l, part).start()
+    own_s[0] = small[...]
+    place.barrier()
+    sums.start()
+    square = jnp.zeros((1, D), WIDE)
+    for t in range(len(parts) + 4):
+        if t < len(parts):
+            l, part = parts[t]
+            fetch(l, part).wait()
+            net.start(l, l, part)
+        if 0 <= t - 1 < len(parts):
+            l, part = parts[t - 1]
+            net.first(l, l, part)
+        if 0 <= t - 2 < len(parts):
+            l, part = parts[t - 2]
+            net.second(l, l, part)
+        if 0 <= t - 3 < len(parts):
+            l, part = parts[t - 3]
+            net.third(l, l, part)
+        if 0 <= t - 4 < len(parts):
+            l, part = parts[t - 4]
+            square = square + net.last(l, l, part, shard.at[l])
+        if 1 <= t <= 3:
+            sums.step(t - 1)
+    own_n[0] = jnp.broadcast_to(square, own_n.shape[1:])
+    norm.start()
+    totals[...] = sums.last()
+    for n in range(3):
+        norm.step(n)
+    squares[...] = norm.last()
+    for l, part in parts:
+        net.sent(l, l, part)
+    sums.sent()
+    norm.sent()
+
+
+def reduce_all(grads, small):
+    whole = pl.BlockSpec(memory_space=pltpu.VMEM)
+    count = 2 * LAYERS
+    dma = pltpu.SemaphoreType.DMA
+    return pl.pallas_call(
+        reduce_kernel,
+        name="reduce",
+        out_shape=(
+            jax.ShapeDtypeStruct((LAYERS, PACK, D), WIDE),
+            jax.ShapeDtypeStruct((SMALL, D), WIDE),
+            jax.ShapeDtypeStruct((8, D), WIDE),
+        ),
+        in_specs=[pl.BlockSpec(memory_space=pl.ANY), whole],
+        out_specs=(whole,) * 3,
+        scratch_shapes=[pltpu.VMEM((LAYERS, NZ, NR, PACK, D), LOWER)]
+        + [pltpu.VMEM((LAYERS,) + shape, LOWER) for shape in REDUCE_SHAPES.values()]
+        + [dma((count, Reduce.COPIES)), dma((count, Reduce.COPIES)), dma((count,))]
+        + [pltpu.VMEM((4, SMALL, D), WIDE), pltpu.VMEM((6, SMALL, D), WIDE), dma((6,)), dma((6,))]
+        + [pltpu.VMEM((4, 8, D), WIDE), pltpu.VMEM((6, 8, D), WIDE), dma((6,)), dma((6,))],
+        compiler_params=pltpu.CompilerParams(
+            collective_id=1, has_side_effects=True, vmem_limit_bytes=56 * 1024 * 1024
+        ),
+        cost_estimate=pl.CostEstimate(flops=0, bytes_accessed=4 * 10**7, transcendentals=0),
+    )(grads, small)
+
+
+def adam_parts(weight, grad, first, second, rate):
     first = BETA_ONE * first + (1.0 - BETA_ONE) * grad
     second = BETA_TWO * second + (1.0 - BETA_TWO) * grad * grad
     fix_one = 1.0 - BETA_ONE**STEP
@@ -548,7 +1017,123 @@
     fresh = weight - rate * (
         first / fix_one / (jnp.sqrt(second / fix_two) + ADAM_EPS) + DECAY * weight
     )
-    return (fresh, first, second)
+    return fresh, first, second
+
+
+def adam_kernel(*refs):
+    shard, small_grad, squares, groups, log_temp = refs[:5]
+    small, small_first, small_second, bias, bias_first, bias_second = refs[5:11]
+    mats, firsts, seconds = refs[11:15], refs[15:19], refs[19:23]
+    totals, norm, next_temp, s_next, s_first, s_second, b_next, b_first, b_second = refs[23:32]
+    m_next, m_copy, m_first, m_second = refs[32:36], refs[36:40], refs[40:44], refs[44:48]
+    l = pl.program_id(0)
+    extra = small_grad[NROWS : NROWS + 3, 0:128]
+    lane = iota((1, 128), 1)
+    bias_mean = jnp.where(lane < A, extra[1:2], 0.0)
+    bias_spread = jnp.where(lane < A, extra[2:3], 0.0)
+
+    def all_sum(v):
+        return jnp.sum(jnp.sum(v, 0, keepdims=True), 1, keepdims=True)
+
+    grads = small_grad[0:NROWS, :]
+    square = (
+        all_sum(squares[0:1, :])
+        + all_sum(grads * grads)
+        + all_sum(bias_mean * bias_mean)
+        + all_sum(bias_spread * bias_spread)
+    )
+    length = jnp.sqrt(square)
+    clip = jnp.minimum(1.0, CLIP / (length + 1e-06))
+
+    def rate_of(kind):
+        group = jnp.full((1, 1), groups[l, kind], jnp.int32).astype(WIDE)
+        return LEARN * jnp.exp2(-group)
+
+    def update(kind, rows, cols, grad):
+        at = (0, rows, cols)
+        fresh, first, second = adam_parts(
+            mats[kind][at], clip * grad, firsts[kind][at], seconds[kind][at], rate_of(kind)
+        )
+        m_next[kind][at] = fresh
+        m_copy[kind][at] = fresh.astype(LOWER)
+        m_first[kind][at] = first
+        m_second[kind][at] = second
+
+    every = slice(0, 16)
+    for j in range(3):
+        update(0, every, slice(j * D, (j + 1) * D), shard[0, 16 * j : 16 * j + 16, :])
+    update(1, every, slice(0, D), shard[0, 48:64, :])
+    for j in range(4):
+        update(2, every, slice(j * D, (j + 1) * D), shard[0, 64 + 16 * j : 80 + 16 * j, :])
+    update(3, slice(0, 64), slice(0, D), shard[0, 128:192, :])
+
+    @pl.when(l == 0)
+    def _():
+        s_next[...], s_first[...], s_second[...] = adam_parts(
+            small[...], clip * grads, small_first[...], small_second[...], LEARN
+        )
+
+        def scalar(v, n):
+            return jnp.sum(jnp.where(lane == n, v, 0.0))
+
+        def row(ref):
+            v = jnp.zeros((1, 128), WIDE)
+            for n in range(2 * A):
+                v = jnp.where(lane == n, ref[n], v)
+            return v
+
+        grad = bias_mean + pltpu.roll(bias_spread, A, 1)
+        results = adam_parts(row(bias), clip * grad, row(bias_first), row(bias_second), LEARN)
+        for ref, result in zip((b_next, b_first, b_second), results):
+            for n in range(2 * A):
+                ref[n] = scalar(result, n)
+        sums = extra[0:1]
+        for n in range(3):
+            totals[n] = scalar(sums, n)
+        norm[0] = jnp.sum(length)
+        logs = jnp.full((1, 1), log_temp[0], WIDE)
+        ratio = jnp.full((1, 1), scalar(sums, 1), WIDE) / jnp.full((1, 1), scalar(sums, 2), WIDE)
+        next_temp[0] = jnp.sum(logs - TEMP_RATE * jnp.exp(logs) * (ratio + A))
+
+
+def adam_all(shard, small_grad, squares, groups, log_temp, smalls, biases, mats, firsts, seconds):
+    scalars = pl.BlockSpec(memory_space=pltpu.SMEM)
+
+    def fixed(array):
+        return pl.BlockSpec(array.shape, lambda l: (0,) * array.ndim)
+
+    def layer(array):
+        return pl.BlockSpec((1,) + array.shape[1:], lambda l: (l, 0, 0))
+
+    def like(array, dtype=WIDE):
+        return jax.ShapeDtypeStruct(array.shape, dtype)
+
+    stacks = list(mats) + list(firsts) + list(seconds)
+    small, bias = smalls[0], biases[0]
+    return pl.pallas_call(
+        adam_kernel,
+        name="adam",
+        grid=(LAYERS,),
+        out_shape=(
+            (jax.ShapeDtypeStruct((3,), WIDE),)
+            + (jax.ShapeDtypeStruct((1,), WIDE),) * 2
+            + (like(small),) * 3
+            + (like(bias),) * 3
+            + tuple(like(m) for m in mats)
+            + tuple(like(m, LOWER) for m in mats)
+            + tuple(like(m) for m in mats) * 2
+        ),
+        in_specs=[layer(shard), fixed(small_grad), fixed(squares), scalars, scalars]
+        + [fixed(small)] * 3
+        + [scalars] * 3
+        + [layer(m) for m in stacks],
+        out_specs=(scalars,) * 3
+        + (fixed(small),) * 3
+        + (scalars,) * 3
+        + tuple(layer(m) for m in mats) * 4,
+        compiler_params=pltpu.CompilerParams(vmem_limit_bytes=40 * 1024 * 1024),
+        cost_estimate=pl.CostEstimate(flops=10**7, bytes_accessed=8 * 10**6, transcendentals=10**6),
+    )(shard, small_grad, squares, groups, log_temp, *smalls, *biases, *stacks)
 
 
 def gather_packed(mats, axes, count):
@@ -560,12 +1145,12 @@
         piece = lax.all_gather(piece, axes, axis=1, tiled=True)
         piece = piece.reshape(LAYERS, BLOCKS, group * rows, wide, D).transpose(0, 1, 3, 2, 4)
         pieces.append(piece.reshape(LAYERS, BLOCKS, wide * group * rows, D))
-    return jnp.concatenate(pieces, 2)
+    return jnp.concatenate(pieces, 2).reshape(LAYERS, BLOCKS // 8, 8, PACK, D)
 
 
 def scatter_packed(grads, mats, axes):
     order = [owner_place(i) for i in range(BLOCKS)]
-    grads = grads[:, jnp.array(order)].astype(WIDE)
+    grads = grads.reshape(LAYERS, BLOCKS, PACK, D)[:, jnp.array(order)].astype(WIDE)
     results, first = [], 0
     for mat in mats:
         rows, wide = mat.shape[1], mat.shape[2] // D
@@ -614,6 +1199,22 @@
     meta, buf = small_inputs(
         buf_states, buf_actions, buf_returns, window_starts, window_repeats, valid_steps
     )
+    if FF // down_weight.shape[1] == BLOCKS and lax.psum(1, "fsdp") == NX * NC:
+        packed = gather_all(mats)
+        grads, small = compute(meta, buf, small_rows, head_bias, log_temp, packed)
+        shard, small, squares = reduce_all(grads, small)
+        return adam_all(
+            shard,
+            small,
+            squares,
+            matrix_groups,
+            log_temp,
+            (small_rows, small_first, small_second),
+            (head_bias, bias_first, bias_second),
+            mats,
+            firsts,
+            seconds,
+        )
     packed = gather_packed(mats, axes, FF // down_weight.shape[1])
     grads, small = compute(meta, buf, small_rows, head_bias, log_temp, packed)
     big = scatter_packed(grads, mats, axes)
@@ -628,13 +1229,13 @@
     clip = jnp.minimum(1.0, CLIP / (grad_norm + 1e-06))
     rates = LEARN * jnp.exp2(-matrix_groups.astype(WIDE))
     results = [
-        adam_step(
+        adam_parts(
             mats[kind], clip * big[kind], firsts[kind], seconds[kind], rates[:, kind][:, None, None]
         )
         for kind in range(4)
     ]
-    small_new = adam_step(small_rows, clip * small_grad, small_first, small_second, LEARN)
-    bias_new = adam_step(head_bias, clip * bias_grad, bias_first, bias_second, LEARN)
+    small_new = adam_parts(small_rows, clip * small_grad, small_first, small_second, LEARN)
+    bias_new = adam_parts(head_bias, clip * bias_grad, bias_first, bias_second, LEARN)
     next_temp = log_temp - TEMP_RATE * jnp.exp(log_temp) * (totals[1] / totals[2] + A)
     return (
         (totals, grad_norm[None], next_temp)

time: 1270 us -> 429 us (0.34)
  waiting for transfers between devices: 824 us -> 0 us
  Pallas kernels: 194 us -> 416 us
  local copies, waits for them, and re-layouts: 136 us -> 9.69 us
  other arithmetic: 55.6 us -> 1.51 us
  blocking collectives: 36.9 us -> 0 us
  between operations: 23 us -> 1.83 us
    reduce_scatter x4 -> x0, waiting for transfers between devices: 575 us -> none  [scatter_packed(): lax.psum_scatter(piece, axes, scatter_dimension=1, tiled=True)]
    all_gather x4 -> x0, waiting for transfers between devices: 249 us -> none  [gather_packed(): piece = lax.all_gather(piece, axes, axis=1, tiled=True)]
    pallas_call x0 -> x3, Pallas kernels: none -> 222 us  [the longest x1 119 us: reduce_all(): pl.pallas_call(reduce_kernel, name='reduce', out_shape=(jax.ShapeDtypeStr...]
    reshape x5 -> x0, local copies, waits for them, and re-layouts: 44.3 us -> none  [the longest x2 31.8 us: scatter_packed(): piece = piece.reshape(LAYERS, total, wide * D)]
    psum x1 -> x0, blocking collectives: 36.9 us -> none  [local(): lax.psum(square, axes) + jnp.sum(small_grad * small_grad)]
    slice x8 -> x0, local copies, waits for them, and re-layouts: 34.8 us -> none  [the longest x6 33.1 us: scatter_packed(): piece = grads[:, :, first:first + wide * deep]]
    convert_element_type x9 -> x0, other arithmetic: 25.2 us -> none  [the longest x1 11.2 us: scatter_packed(): grads = grads[:, jnp.array(order)].astype(WIDE)]
    transpose x3 -> x0, local copies, waits for them, and re-layouts: 17.2 us -> none  [the longest x1 11.1 us: scatter_packed(): piece.reshape(LAYERS, BLOCKS, wide, deep, D).transpose(0, 1, 3, 2, 4)]
  transfers between devices with their start and end apart: 9 -> 0, of which waited for: 8 -> 0; matrix products, arithmetic and copies ran while one was open for 11% -> 0% of each run, Pallas kernels for 0% -> 0%
where the time goes in v2:
time: 429 us
  Pallas kernels  416 us (97%)
  local copies, waits for them, and re-layouts  9.69 us (2%)
    pallas_call x1, Pallas kernels, compute(): pl.pallas_call(compute_kernel, name='train_pass', out_shape=(jax.ShapeDty...  194 us
    pallas_call x1, Pallas kernels, reduce_all(): pl.pallas_call(reduce_kernel, name='reduce', out_shape=(jax.ShapeDtypeStr...  119 us
    pallas_call x1, Pallas kernels, gather_all(): pl.pallas_call(gather_kernel, name='gather', out_shape=jax.ShapeDtypeStru...  98.2 us

profile of v2, /device:TPU:0, one launch (start us, length us, event | category | flops | bytes accessed | tf_op | source)
XLA Modules:
  0.0 428.8 jit_solution(4109879936731086407)
XLA Ops:
  1.3 0.7 pad_maximum_fusion
  2.1 0.7 copy.56
  2.8 0.7 copy.57
  3.5 0.8 add_convert_fusion
  4.3 0.1 copy.58
  4.4 0.6 pad.9.buf
  5.0 0.6 pad.8.meta
  5.7 1.0 copy-done
  6.7 1.0 copy-done.2
  7.7 1.0 copy-done.5
  8.6 0.9 copy-done.7
  9.5 98.2 %gather.1.packed = bf16[3,4,8,192,512]{4,3,2,1,0:T(8,128)(2,1)} custom-call(f32[3,16,1536]{2,1,0:T(8,128)S(1)} %copy-done.5, f32[3,16,512]{2,1,0:T(8,128)S(1)} %copy-done.7, f32[3,16,2048]{2,1,0:T(8,128)S(1)} %copy-done, f32[3,64,512]{2,1,0:T(8,128)S(1)} %copy-done.2), custom_call_target="tpu_custom_call" | custom-call | bytes 40000000 | tf_op jit(solution)/shard_map/gather/pallas_call | solution.py:904
  107.8 193.6 %train_pass.1 = (bf16[3,4,8,192,512]{4,3,2,1,0:T(8,128)(2,1)}, f32[88,512]{1,0:T(8,128)}) custom-call(f32[128,128]{1,0:T(8,128)} %pad.8.meta, f32[128,128]{1,0:T(8,128)} %pad.9.buf, f32[85,512]{1,0:T(8,128)} %refs_5_.1, f32[6]{0:T(128)} %refs_8_.1, f32[1]{0:T(128)S(6)} %copy.59.log_temp.refs_4_, bf16[3,4,8,192,512]{4,3,2,1,0:T(8,128)(2,1)} %gather.1.packed), custom_call_target="tpu_custom_call" | custom-call | flops 60000002048 | bytes 40000000 | tf_op jit(solution)/shard_map/train_pass/pallas_call | solution.py:518
  301.4 0.0 copy-start.1
  301.4 0.0 copy-start.3
  301.4 0.0 copy-start.6
  301.5 0.0 copy-start.8
  301.5 0.0 copy-start.9
  301.5 0.0 copy-start.10
  301.5 0.0 copy-start.11
  301.5 0.0 copy-start.12
  301.5 0.0 copy-start.13
  301.5 0.0 copy-start.14
  301.5 0.0 copy-start.15
  301.5 0.0 copy-start.16
  301.6 0.0 copy-start.17
  301.6 0.0 copy-start.19
  301.6 0.0 copy-start.20
  301.6 0.0 copy-start.22
  301.6 0.0 copy-start.23
  301.6 0.0 copy-start.24
  301.6 0.0 copy-start.25
  301.6 119.4 %reduce.1 = (f32[3,192,512]{2,1,0:T(8,128)}, f32[88,512]{1,0:T(8,128)}, f32[8,512]{1,0:T(8,128)}) custom-call(bf16[3,4,8,192,512]{4,3,2,1,0:T(8,128)(2,1)} %get-tuple-element.30.grads, f32[88,512]{1,0:T(8,128)} %get-tuple-element.31.small), custom_call_target="tpu_custom_call" | custom-call | bytes 40000000 | tf_op jit(solution)/shard_map/reduce/pallas_call | solution.py:990
  421.0 0.0 copy-done.1
  421.0 0.0 copy-done.3
  421.0 0.0 copy-done.6
  421.0 0.0 copy-done.8
  421.0 0.0 copy-done.9
  421.1 0.0 copy-done.10
  421.1 0.0 copy-done.11
  421.1 0.0 copy-done.12
  421.1 0.0 copy-done.13
  421.1 0.0 copy-done.14
  421.1 0.0 copy-done.15
  421.2 1.3 copy-done.4
  422.5 0.9 copy-done.18
  423.4 0.7 copy-done.21
  424.1 4.5 %adam.1 = (f32[3]{0:T(128)}, f32[1]{0:T(128)}, f32[1]{0:T(128)}, f32[85,512]{1,0:T(8,128)}, f32[85,512]{1,0:T(8,128)}, /*index=5*/f32[85,512]{1,0:T(8,128)}, f32...) custom-call(f32[3,192,512]{2,1,0:T(8,128)S(1)} %copy-done.4, ...), custom_call_target="tpu_custom_call" | custom-call | flops 10000000 | bytes 8000000 | tf_op jit(solution)/shard_map/adam/pallas_call | solution.py:1113
  (15 shorter events, 0.0 us)
Async XLA Ops:
  5.7 1.0 copy-start
  6.7 1.0 copy-start.2
  7.6 1.0 copy-start.5
  8.6 0.9 copy-start.7
  301.4 119.6 %copy-start.1 = (f32[3,16,2048]{2,1,0:T(8,128)S(1)}, f32[3,16,2048]{2,1,0:T(8,128)}, u32[]{:S(2)}) copy-start(f32[3,16,2048]{2,1,0:T(8,128)} %refs_13_.1) | copy-start | bytes 1179652
  301.4 119.6 %copy-start.3 = (f32[3,64,512]{2,1,0:T(8,128)S(1)}, f32[3,64,512]{2,1,0:T(8,128)}, u32[]{:S(2)}) copy-start(f32[3,64,512]{2,1,0:T(8,128)} %refs_14_.1) | copy-start | bytes 1179652
  301.4 119.6 %copy-start.6 = (f32[3,16,1536]{2,1,0:T(8,128)S(1)}, f32[3,16,1536]{2,1,0:T(8,128)}, u32[]{:S(2)}) copy-start(f32[3,16,1536]{2,1,0:T(8,128)} %refs_11_.1) | copy-start | bytes 884740
  301.5 119.6 %copy-start.8 = (f32[3,16,512]{2,1,0:T(8,128)S(1)}, f32[3,16,512]{2,1,0:T(8,128)}, u32[]{:S(2)}) copy-start(f32[3,16,512]{2,1,0:T(8,128)} %refs_12_.1) | copy-start | bytes 294916
  301.5 119.6 %copy-start.9 = (f32[3,16,2048]{2,1,0:T(8,128)S(1)}, f32[3,16,2048]{2,1,0:T(8,128)}, u32[]{:S(2)}) copy-start(f32[3,16,2048]{2,1,0:T(8,128)} %refs_17_.1) | copy-start | bytes 1179652
  301.5 119.6 %copy-start.10 = (f32[3,64,512]{2,1,0:T(8,128)S(1)}, f32[3,64,512]{2,1,0:T(8,128)}, u32[]{:S(2)}) copy-start(f32[3,64,512]{2,1,0:T(8,128)} %refs_18_.1) | copy-start | bytes 1179652
  301.5 119.6 %copy-start.11 = (f32[3,16,2048]{2,1,0:T(8,128)S(1)}, f32[3,16,2048]{2,1,0:T(8,128)}, u32[]{:S(2)}) copy-start(f32[3,16,2048]{2,1,0:T(8,128)} %refs_21_.1) | copy-start | bytes 1179652
  301.5 119.6 %copy-start.12 = (f32[3,64,512]{2,1,0:T(8,128)S(1)}, f32[3,64,512]{2,1,0:T(8,128)}, u32[]{:S(2)}) copy-start(f32[3,64,512]{2,1,0:T(8,128)} %refs_22_.1) | copy-start | bytes 1179652
  301.5 119.6 %copy-start.13 = (f32[3,16,1536]{2,1,0:T(8,128)S(1)}, f32[3,16,1536]{2,1,0:T(8,128)}, u32[]{:S(2)}) copy-start(f32[3,16,1536]{2,1,0:T(8,128)} %refs_15_.1) | copy-start | bytes 884740
  301.5 119.6 %copy-start.14 = (f32[3,16,1536]{2,1,0:T(8,128)S(1)}, f32[3,16,1536]{2,1,0:T(8,128)}, u32[]{:S(2)}) copy-start(f32[3,16,1536]{2,1,0:T(8,128)} %refs_19_.1) | copy-start | bytes 884740
  301.5 119.6 %copy-start.15 = (f32[85,512]{1,0:T(8,128)S(1)}, f32[85,512]{1,0:T(8,128)}, u32[]{:S(2)}) copy-start(f32[85,512]{1,0:T(8,128)} %refs_5_.1) | copy-start | bytes 522244
  301.5 119.6 %copy-start.16 = (f32[85,512]{1,0:T(8,128)S(1)}, f32[85,512]{1,0:T(8,128)}, u32[]{:S(2)}) copy-start(f32[85,512]{1,0:T(8,128)} %refs_6_.1) | copy-start | bytes 522244
  301.6 119.6 %copy-start.17 = (f32[85,512]{1,0:T(8,128)S(1)}, f32[85,512]{1,0:T(8,128)}, u32[]{:S(2)}) copy-start(f32[85,512]{1,0:T(8,128)} %refs_7_.1) | copy-start | bytes 522244
  301.6 119.6 %copy-start.19 = (f32[3,16,512]{2,1,0:T(8,128)S(1)}, f32[3,16,512]{2,1,0:T(8,128)}, u32[]{:S(2)}) copy-start(f32[3,16,512]{2,1,0:T(8,128)} %refs_16_.1) | copy-start | bytes 294916
  301.6 119.6 %copy-start.20 = (f32[3,16,512]{2,1,0:T(8,128)S(1)}, f32[3,16,512]{2,1,0:T(8,128)}, u32[]{:S(2)}) copy-start(f32[3,16,512]{2,1,0:T(8,128)} %refs_20_.1) | copy-start | bytes 294916
  301.6 119.6 %copy-start.22 = (s32[3,4]{1,0:T(4,128)S(1)}, s32[3,4]{1,0:T(4,128)}, u32[]{:S(2)}) copy-start(s32[3,4]{1,0:T(4,128)} %refs_3_.1) | copy-start | bytes 148
  301.6 119.6 %copy-start.23 = (f32[6]{0:T(128)S(1)}, f32[6]{0:T(128)}, u32[]{:S(2)}) copy-start(f32[6]{0:T(128)} %refs_8_.1) | copy-start | bytes 76
  301.6 119.6 %copy-start.24 = (f32[6]{0:T(128)S(1)}, f32[6]{0:T(128)}, u32[]{:S(2)}) copy-start(f32[6]{0:T(128)} %refs_9_.1) | copy-start | bytes 76
  301.6 119.6 %copy-start.25 = (f32[6]{0:T(128)S(1)}, f32[6]{0:T(128)}, u32[]{:S(2)}) copy-start(f32[6]{0:T(128)} %refs_10_.1) | copy-start | bytes 76
  421.2 1.3 copy-start.4
  422.5 0.9 copy-start.18
  423.4 0.7 copy-start.21

commit v3 on v1

v3 whole, which is shorter than its diff:
```python
import functools
import math

import jax
import jax.numpy as jnp
from jax import lax
from jax.experimental import pallas as pl
from jax.experimental.pallas import tpu as pltpu
from jax.sharding import PartitionSpec as P

D = 512
H = 8
HD = 64
FF = 2048
S = 11
A = 3
K = 20
STEP = 10

EPS = 1e-05
CLIP = 1.0
LEARN = 0.03
BETA_ONE = 0.5
BETA_TWO = 0.7
DECAY = 0.01
ADAM_EPS = 1e-08
TEMP_RATE = 0.1
MASKED = -1e30
HALF_LOG_TAU = 0.5 * math.log(2.0 * math.pi)
GELU_C = math.sqrt(2.0 / math.pi)
GELU_A = 0.044715
HIGH = lax.Precision.HIGHEST
LOWER = jnp.bfloat16
WIDE = jnp.float32

LAYERS = 3
WINS = 16
SLOT = 64
ROWS = WINS * SLOT
CHUNK = 256
CHUNKS = ROWS // CHUNK
UNROLL = 2
BLOCKS = 32
PACK = 192
ATTN, FFN = 64, 128
EMB = S + A + 1 + K + 3
FIN = EMB
HEADW = EMB + 2
BASE = EMB + 2 + 2 * A
PER = 9 + FF // D
NROWS = BASE + LAYERS * PER
SMALL = 88
VMEM_BYTES = 64 * 1024 * 1024


def dot(a, b, precision=None):
    return lax.dot_general(
        a, b, (((1,), (0,)), ((), ())), precision=precision, preferred_element_type=WIDE
    )


def dot_nt(a, b, precision=None):
    return lax.dot_general(
        a, b, (((1,), (1,)), ((), ())), precision=precision, preferred_element_type=WIDE
    )


def dot_tn(a, b, precision=None):
    return lax.dot_general(
        a, b, (((0,), (0,)), ((), ())), precision=precision, preferred_element_type=WIDE
    )


def iota(shape, dim):
    return lax.broadcasted_iota(jnp.int32, shape, dim)


def col_sum(v):
    return jnp.sum(v, 0, keepdims=True)


def row_mean(v):
    return jnp.mean(v, -1, keepdims=True)


def norm_parts(x):
    center = x - row_mean(x)
    scale = lax.rsqrt(row_mean(center * center) + EPS)
    return center * scale, scale


def norm_back(xhat, scale, gain, grad):
    scaled = grad * gain
    return scale * (scaled - row_mean(scaled) - xhat * row_mean(scaled * xhat))


def token_rows(at, count):
    row = at + iota((count, 128), 0)
    place = row & (SLOT - 1)
    step = (place * 21846) >> 16
    return row >> 6, step, place - 3 * step, place < 3 * K


def chunk_rows(c):
    return pl.ds(pl.multiple_of(c * CHUNK, CHUNK), CHUNK)


def owner_place(i):
    z, y, x, c = i // 8, (i // 4) % 2, (i // 2) % 2, i % 2
    return 2 * c + x, 4 * y + z


class Kit:
    def __init__(self, **refs):
        self.__dict__.update(refs)

    def row(self, l, k):
        return self.lrows[l, k : k + 1, :]

    def blocks(self, ref, l, first, count, owners):
        places = [owner_place(i) for i in owners]
        return jnp.concatenate([ref[l, a, b, first : first + count, :] for a, b in places], 0)

    def w_qkv(self, l, j):
        return self.blocks(self.wa, l, 16 * j, 16, range(BLOCKS))

    def w_out(self, l):
        return self.blocks(self.wa, l, 48, 16, range(BLOCKS))

    def w_up(self, l, j):
        return self.blocks(self.wf, l, 16 * j, 16, range(BLOCKS))

    def w_down(self, l, j):
        return self.blocks(self.wf, l, 64, 64, range(8 * j, 8 * j + 8))


def slot(l):
    return l % 2


def setup_stage(k):
    k.emb[...] = jnp.zeros_like(k.emb)
    k.emb[0:EMB, :] = k.small[0:EMB, :]
    k.headw[...] = jnp.zeros_like(k.headw)
    k.headw[0, 0:A, :] = k.small[HEADW : HEADW + A, :].astype(LOWER)
    k.headw[1, 0:A, :] = k.small[HEADW + A : HEADW + 2 * A, :].astype(LOWER)
    for l in range(LAYERS):
        k.lrows[l, 0:PER, :] = k.small[BASE + l * PER : BASE + (l + 1) * PER, :]
    k.sgl[...] = jnp.zeros_like(k.sgl)
    k.sgh[...] = jnp.zeros_like(k.sgh)
    k.sgw[...] = jnp.zeros_like(k.sgw)

    meta = k.meta[...].astype(LOWER)

    def chunk(c, carry):
        rows = chunk_rows(c)
        win, step, kind, real = token_rows(c * CHUNK, CHUNK)
        lane = iota((CHUNK, 128), 1)
        tok = dot((lane == win).astype(WIDE).astype(LOWER), meta)
        start, repeat = tok[:, 0:1], tok[:, 1:2]
        valid = jnp.sum(jnp.where(lane == step + 2, tok, 0.0), -1, keepdims=True)
        key = iota((CHUNK, 128), 0) & (SLOT - 1)
        query = lane & (SLOT - 1)
        allowed = (key <= query) & (((valid > 0.5) & real) | (key == query))
        k.bias[rows, :] = jnp.where(allowed, 0.0, MASKED)
        place = start.astype(jnp.int32) + step
        source = ((lane == place) & real).astype(WIDE)
        raw = dot(source, k.buf[...], HIGH)
        mine = (
            ((lane < S) & (kind == 1))
            | ((lane >= S) & (lane < S + A) & (kind == 2))
            | ((lane == S + A) & (kind == 0))
        )
        marks = ((lane == S + A + 1 + step) | (lane == S + A + 1 + K + kind)) & real
        feats = jnp.where(mine, raw, 0.0) + marks.astype(WIDE)
        k.feats[rows, :] = feats
        weight = jnp.where((kind == 1) & real, repeat * valid, 0.0)
        acts = pltpu.roll(raw, 128 - S, 1)
        k.acts[rows, :] = jnp.where(lane < A, acts, jnp.where(lane == A, weight, 0.0))
        k.xs[0, rows, :] = dot(feats, k.emb[...], HIGH)
        return carry

    lax.fori_loop(0, CHUNKS, chunk, 0)


def stack_pair(v, first):
    zero = jnp.zeros_like(v)
    return jnp.concatenate([jnp.where(first, v, zero), jnp.where(first, zero, v)], 0)


def join_pair(v, first):
    return jnp.where(first, v[:SLOT], v[SLOT:])


def window_rows(w):
    return pl.ds(pl.multiple_of(w * SLOT, SLOT), SLOT)


def each_chunk(body):
    def some(n, carry):
        for c in range(UNROLL):
            body(UNROLL * n + c, chunk_rows(UNROLL * n + c))
        return carry

    lax.fori_loop(0, CHUNKS // UNROLL, some, 0)


def each_window(body):
    def pair(n, carry):
        body(2 * n)
        body(2 * n + 1)
        return carry

    lax.fori_loop(0, WINS // 2, pair, 0)


def forward_attn(k, l):
    def chunk(c, rows):
        xhat, _ = norm_parts(k.xs[slot(l), rows, :])
        normed = (xhat * k.row(l, 0) + k.row(l, 1)).astype(LOWER)
        k.normed_t[slot(l), :, rows] = normed.T
        for j in range(3):
            part = dot(normed, k.w_qkv(l, j)) + k.row(l, 4 + j)
            k.qkv[slot(l), rows, j * D : (j + 1) * D] = part.astype(LOWER)

    each_chunk(chunk)
    first = iota((SLOT, 128), 1) < HD

    def window(w):
        rows = window_rows(w)
        bias = k.bias[rows, :]
        scores = []
        for p in range(H // 2):
            at = p * 128
            query = stack_pair(k.qkv[slot(l), rows, at : at + 128] * jnp.asarray(HD**-0.5, LOWER), first)
            scores.append(dot_nt(k.qkv[slot(l), rows, D + at : D + at + 128], query) + bias)
        for p in range(H // 2):
            at = p * 128
            peak = jnp.max(scores[p], 0, keepdims=True)
            expo = jnp.exp(scores[p] - peak)
            total = jnp.sum(expo, 0, keepdims=True)
            probs = (expo * (1.0 / total)).astype(LOWER)
            k.logs[l, w, p : p + 1, :] = peak + jnp.log(total)
            out = dot_tn(probs, k.qkv[slot(l), rows, 2 * D + at : 2 * D + at + 128])
            k.left[rows, at : at + 128] = join_pair(out, first).astype(LOWER)

    each_window(window)


def gelu_parts(h):
    square = h * h
    t = jnp.tanh(GELU_C * (h + GELU_A * h * square))
    return t, square


def forward_ffn(k, l, dest):
    def chunk(c, rows):
        mixed = k.left[rows, :]
        k.mixed_t[slot(l), :, rows] = mixed.T
        mid = k.xs[slot(l), rows, :] + dot(mixed, k.w_out(l)) + k.row(l, 7)
        k.mid[slot(l), rows, :] = mid
        xhat, _ = norm_parts(mid)
        second = (xhat * k.row(l, 2) + k.row(l, 3)).astype(LOWER)
        out = mid + k.row(l, 12)
        for j in range(4):
            h = dot(second, k.w_up(l, j)) + k.row(l, 8 + j)
            t, _ = gelu_parts(h)
            acted = (0.5 * h * (1.0 + t)).astype(LOWER)
            out = out + dot(acted, k.w_down(l, j))
        k.xs[dest, rows, :] = out

    each_chunk(chunk)


def head_stage(k, at):
    gain, bias = k.small[FIN : FIN + 1, :], k.small[FIN + 1 : FIN + 2, :]
    lane = iota((CHUNK, 128), 1)
    keep = lane < A

    def bias_row(first):
        row = jnp.zeros((1, 128), WIDE)
        at = iota((1, 128), 1)
        for a in range(A):
            row = jnp.where(at == a, k.head_bias[first + a], row)
        return row

    bias_mean, bias_spread = bias_row(0), bias_row(A)
    temp = jnp.exp(jnp.full((1, 128), k.log_temp[0], WIDE))

    def chunk(c, carry):
        rows = chunk_rows(c)
        xhat, scale = norm_parts(k.xs[at, rows, :])
        feats = (xhat * gain + bias).astype(LOWER)
        mean = dot_nt(feats, k.headw[0]) + bias_mean
        spread = jnp.tanh(dot_nt(feats, k.headw[1]) + bias_spread)
        acts = k.acts[rows, :]
        weight = acts[:, A : A + 1]
        acts = jnp.where(keep, acts, 0.0)
        target = 0.5 * (jnp.log(1.0 + acts) - jnp.log(1.0 - acts))
        shrink = jnp.exp(-spread)
        zed = (target - mean) * shrink
        terms = 0.5 * zed * zed + spread + HALF_LOG_TAU + jnp.log(1.0 - acts * acts)
        nll = jnp.sum(jnp.where(keep, terms, 0.0), -1, keepdims=True)
        entropy = jnp.sum(jnp.where(keep, spread, 0.0), -1, keepdims=True) + A * (0.5 + HALF_LOG_TAU)
        loss = weight * (nll - temp * entropy)
        sums = jnp.where(lane == 0, loss, jnp.where(lane == 1, weight * entropy, jnp.where(lane == 2, weight, 0.0)))
        d_mean = jnp.where(keep, weight * (-zed * shrink), 0.0).astype(LOWER)
        d_spread = weight * (1.0 - zed * zed - temp) * (1.0 - spread * spread)
        d_spread = jnp.where(keep, d_spread, 0.0).astype(LOWER)
        k.sgh[2:3, 0:128] += col_sum(sums)
        k.sgh[3:4, 0:128] += col_sum(d_mean.astype(WIDE))
        k.sgh[4:5, 0:128] += col_sum(d_spread.astype(WIDE))
        k.sgw[0] += dot_tn(d_mean, feats)[0:8]
        k.sgw[1] += dot_tn(d_spread, feats)[0:8]
        d_feats = dot(d_mean, k.headw[0]) + dot(d_spread, k.headw[1])
        k.sgh[0:1, :] += col_sum(d_feats * xhat)
        k.sgh[1:2, :] += col_sum(d_feats)
        k.xs[at, rows, :] = norm_back(xhat, scale, gain, d_feats)
        return carry

    lax.fori_loop(0, CHUNKS, chunk, 0)


def store_blocks(ref, l, owners, first, count, value):
    value = value.astype(LOWER)
    for n, i in enumerate(owners):
        a, b = owner_place(i)
        ref[l, a, b, first : first + count, :] = value[n * count : (n + 1) * count]


def backward_ffn_start(k, l, grad):
    def before(c, rows):
        d_down = k.xs[grad, rows, :].astype(LOWER)
        k.dout[rows, :] = d_down
        k.sgl[l, 12:13, :] += col_sum(d_down.astype(WIDE))
        xhat, _ = norm_parts(k.mid[slot(l), rows, :])
        second = (xhat * k.row(l, 2) + k.row(l, 3)).astype(LOWER)
        k.left[rows, :] = second
        k.left_t[:, rows] = second.T
        k.dsec[rows, :] = jnp.zeros((CHUNK, D), WIDE)

    each_chunk(before)


def backward_ffn_block(k, l, j):
    def chunk(c, rows):
        h = dot(k.left[rows, :], k.w_up(l, j)) + k.row(l, 8 + j)
        t, square = gelu_parts(h)
        half, over = 0.5 * h, 1.0 + t
        k.act_t[:, rows] = (half * over).astype(LOWER).T
        slope = over * (0.5 + half * (2.0 - over) * (GELU_C + 3.0 * GELU_A * GELU_C * square))
        d_acted = dot_nt(k.dout[rows, :], k.w_down(l, j))
        d_hidden = (d_acted * slope).astype(LOWER)
        k.work[rows, 0:D] = d_hidden
        k.sgl[l, 8 + j : 9 + j, :] += col_sum(d_hidden.astype(WIDE))
        k.dsec[rows, :] += dot_nt(d_hidden, k.w_up(l, j))

    each_chunk(chunk)
    store_blocks(k.wf, l, range(BLOCKS), 16 * j, 16, dot(k.left_t[...], k.work[:, 0:D]))
    store_blocks(k.wf, l, range(8 * j, 8 * j + 8), 64, 64, dot(k.act_t[...], k.dout[...]))


def backward_ffn_end(k, l, grad):
    def after(c, rows):
        xhat, scale = norm_parts(k.mid[slot(l), rows, :])
        d_second = k.dsec[rows, :]
        k.sgl[l, 2:3, :] += col_sum(d_second * xhat)
        k.sgl[l, 3:4, :] += col_sum(d_second)
        k.xs[grad, rows, :] += norm_back(xhat, scale, k.row(l, 2), d_second)

    each_chunk(after)


def backward_attn(k, l, grad):
    def before(c, rows):
        d_branch = k.xs[grad, rows, :].astype(LOWER)
        k.left[rows, :] = d_branch
        k.sgl[l, 7:8, :] += col_sum(d_branch.astype(WIDE))
        k.dout[rows, :] = dot_nt(d_branch, k.w_out(l)).astype(LOWER)

    each_chunk(before)
    store_blocks(k.wa, l + 1, range(BLOCKS), 48, 16, dot(k.mixed_t[slot(l)], k.left[...]))
    first = iota((SLOT, 128), 1) < HD
    scale = HD**-0.5

    def window(w):
        rows = window_rows(w)
        bias = k.bias[rows, :]
        for p in range(H // 2):
            at = p * 128
            query = stack_pair(k.qkv[slot(l), rows, at : at + 128] * jnp.asarray(scale, LOWER), first)
            keyed = k.qkv[slot(l), rows, D + at : D + at + 128]
            values = k.qkv[slot(l), rows, 2 * D + at : 2 * D + at + 128]
            d_mixed = stack_pair(k.dout[rows, at : at + 128], first)
            probs = jnp.exp(dot_nt(keyed, query) + bias - k.logs[l, w, p : p + 1, :])
            d_probs = dot_nt(values, d_mixed)
            d_values = dot(probs.astype(LOWER), d_mixed)
            inner = probs * d_probs
            d_scores = (inner - probs * jnp.sum(inner, 0, keepdims=True)).astype(LOWER)
            d_keyed = dot(d_scores, query)
            d_query = join_pair(dot_tn(d_scores, keyed), first) * scale
            k.work[rows, at : at + 128] = d_query.astype(LOWER)
            k.work[rows, D + at : D + at + 128] = d_keyed.astype(LOWER)
            k.work[rows, 2 * D + at : 2 * D + at + 128] = d_values.astype(LOWER)

    each_window(window)
    for j in range(3):
        store_blocks(k.wa, l + 1, range(BLOCKS), 16 * j, 16, dot(k.normed_t[slot(l)], k.work[:, j * D : (j + 1) * D]))


def backward_input(k, l, grad):
    def chunk(c, rows):
        d_normed = jnp.zeros((CHUNK, D), WIDE)
        for j in range(3):
            d_part = k.work[rows, j * D : (j + 1) * D]
            k.sgl[l, 4 + j : 5 + j, :] += col_sum(d_part.astype(WIDE))
            d_normed = d_normed + dot_nt(d_part, k.w_qkv(l, j))
        xhat, scale = norm_parts(k.xs[slot(l), rows, :])
        k.sgl[l, 0:1, :] += col_sum(d_normed * xhat)
        k.sgl[l, 1:2, :] += col_sum(d_normed)
        k.xs[grad, rows, :] += norm_back(xhat, scale, k.row(l, 0), d_normed)

    each_chunk(chunk)


def small_stage(k, out, grad):
    out[...] = jnp.zeros_like(out)
    out[0:EMB, :] = dot_tn(k.feats[...], k.xs[grad], HIGH)[0:EMB]
    out[FIN : FIN + 2, :] = k.sgh[0:2, :]
    out[HEADW : HEADW + A, :] = k.sgw[0, 0:A, :]
    out[HEADW + A : HEADW + 2 * A, :] = k.sgw[1, 0:A, :]
    for l in range(LAYERS):
        out[BASE + l * PER : BASE + (l + 1) * PER, :] = k.sgl[l, 0:PER, :]
    out[NROWS : NROWS + 3, :] = k.sgh[2:5, :]


WORK_SHAPES = dict(
    wa=((LAYERS + 1, 4, 8, ATTN, D), LOWER),
    wf=((LAYERS, 4, 8, FFN, D), LOWER),
    xs=((3, ROWS, D), WIDE),
    mid=((2, ROWS, D), WIDE),
    qkv=((2, ROWS, 3 * D), LOWER),
    normed_t=((2, D, ROWS), LOWER),
    mixed_t=((2, D, ROWS), LOWER),
    logs=((LAYERS, WINS, 8, 128), WIDE),
    work=((ROWS, 3 * D), LOWER),
    left=((ROWS, D), LOWER),
    left_t=((D, ROWS), LOWER),
    act_t=((D, ROWS), LOWER),
    dout=((ROWS, D), LOWER),
    dsec=((ROWS, D), WIDE),
    feats=((ROWS, 128), WIDE),
    acts=((ROWS, 128), WIDE),
    bias=((ROWS, 128), WIDE),
    emb=((128, D), WIDE),
    headw=((2, 128, D), LOWER),
    lrows=((LAYERS, 16, D), WIDE),
    sgl=((LAYERS, 16, D), WIDE),
    sgh=((8, D), WIDE),
    sgw=((2, 8, D), WIDE),
)
SAVED = ("xs", "mid", "qkv", "normed_t", "mixed_t")


MESH = pl.DeviceIdType.MESH
NZ, NY, NX, NC = 4, 2, 2, 2
NR = NY * NX * NC
SHARD = PACK
PART = (ATTN, FFN)


class Place:
    def __init__(self):
        dp, fsdp = lax.axis_index("dp"), lax.axis_index("fsdp")
        self.z, self.y = dp // NY, dp % NY
        self.x, self.c = fsdp // NC, fsdp % NC
        self.a, self.b = 2 * self.c + self.x, 4 * self.y + self.z
        self.to_x = (dp, (1 - self.x) * NC + self.c)
        self.to_y = (self.z * NY + 1 - self.y, fsdp)
        self.to_c = (dp, self.x * NC + 1 - self.c)
        self.to_z = [(((self.z + d) % NZ) * NY + self.y, fsdp) for d in range(1, NZ)]
        self.partners = [self.to_c, self.to_x, self.to_y] + self.to_z

    def barrier(self):
        sem = pltpu.get_barrier_semaphore()
        for partner in self.partners:
            pl.semaphore_signal(sem, inc=1, device_id=partner, device_id_type=MESH)
        pl.semaphore_wait(sem, len(self.partners))


def remote(src, dst, send, recv, to):
    return pltpu.make_async_remote_copy(
        src_ref=src, dst_ref=dst, send_sem=send, recv_sem=recv, device_id=to, device_id_type=MESH
    )


class Gather:
    COPIES = 11

    def __init__(self, place, weights, send, recv):
        self.at, self.weights, self.send, self.recv = place, weights, send, recv

    def copy(self, l, part, n):
        at, count = self.at, PART[part]
        half = count // 2
        a, b, rows, to = at.a, pl.ds(4 * at.y, 4), pl.ds(0, count), at.to_c
        if n < 3:
            b, to = at.b, at.to_z[n]
        elif n < 5:
            to = (at.to_x, at.to_y)[n - 3]
        if n in (6, 8, 10):
            a = 2 * at.c + 1 - at.x
        if n in (7, 9, 10):
            b = pl.ds(4 * (1 - at.y), 4)
        if n in (6, 7):
            rows, to = pl.ds((n - 6) * half, half), (at.to_y, at.to_x)[n - 6]
        ref = self.weights[part].at[l, a, b, rows, :]
        q = 2 * l + part
        return remote(ref, ref, self.send.at[q, n], self.recv.at[q, n], to)

    def start(self, l, part, *ns):
        for n in ns:
            self.copy(l, part, n).start()

    def wait(self, l, part, *ns):
        for n in ns:
            self.copy(l, part, n).wait_recv()

    def first(self, l, part):
        self.start(l, part, 0, 1, 2)

    def second(self, l, part):
        self.wait(l, part, 0, 1, 2)
        self.start(l, part, 3, 4, 5)

    def third(self, l, part):
        self.wait(l, part, 3)
        self.start(l, part, 6, 8)
        self.wait(l, part, 4)
        self.start(l, part, 7, 9)

    def fourth(self, l, part):
        self.wait(l, part, 6, 7)
        self.start(l, part, 10)

    def last(self, l, part):
        self.wait(l, part, 5, 8, 9, 10)

    def sent(self, l, part):
        for n in range(self.COPIES):
            self.copy(l, part, n).wait_send()


class Reduce:
    COPIES = 8

    def __init__(self, place, grads, landing, send, recv, credit):
        self.at, self.grads, self.landing = place, grads, landing
        self.send, self.recv, self.credit = send, recv, credit

    def refs(self, l, part):
        grads = self.grads[part].at[l + 1 - part]
        r0, r1a, r1b, r2, r3 = self.landing[part]
        return grads, r0, r1a, r1b, r2, r3

    def copy(self, l, part, n):
        at, half = self.at, PART[part] // 2
        g, r0, r1a, r1b, r2, r3 = self.refs(l, part)
        top, low, other = pl.ds(0, half), pl.ds(half, half), pl.ds(4 * (1 - at.y), 4)
        if n == 0:
            src, dst, to = g.at[pl.ds(2 * (1 - at.c), 2)], r0, at.to_c
        elif n == 1:
            src, dst, to = r0.at[1 - at.x, :, top, :], r1a, at.to_x
        elif n == 2:
            src, dst, to = r0.at[:, other, low, :], r1b, at.to_y
        elif n == 3:
            src, dst, to = r1a.at[other], r2.at[:, top, :], at.to_y
        elif n == 4:
            src, dst, to = r1b.at[1 - at.x], r2.at[:, low, :], at.to_x
        else:
            src, dst, to = r2.at[(at.z + n - 4) % NZ], r3.at[n - 5], at.to_z[n - 5]
        q = 2 * l + part
        return remote(src, dst, self.send.at[q, n], self.recv.at[q, n], to)

    def may_send(self, l, part, *partners):
        @pl.when(l < LAYERS - 1)
        def _():
            for n in partners:
                pl.semaphore_wait(self.credit.at[part, n], 1)

    def start(self, l, part):
        self.may_send(l, part, 0)
        self.copy(l, part, 0).start()

    def first(self, l, part):
        at, half = self.at, PART[part] // 2
        g, r0, _, _, _, _ = self.refs(l, part)
        top, low = pl.ds(0, half), pl.ds(half, half)
        self.copy(l, part, 0).wait_recv()

        def along_x(n, carry):
            x = 1 - at.x
            total = g[2 * at.c + x, n, top].astype(WIDE) + r0[x, n, top].astype(WIDE)
            r0[x, n, top] = total.astype(LOWER)
            return carry

        def along_y(n, carry):
            x, b = n // 4, 4 * (1 - at.y) + n % 4
            total = g[2 * at.c + x, b, low].astype(WIDE) + r0[x, b, low].astype(WIDE)
            r0[x, b, low] = total.astype(LOWER)
            return carry

        lax.fori_loop(0, 8, along_x, 0)
        self.may_send(l, part, 1, 2)
        self.copy(l, part, 1).start()
        lax.fori_loop(0, 8, along_y, 0)
        self.copy(l, part, 2).start()

    def second(self, l, part):
        at, half = self.at, PART[part] // 2
        g, r0, r1a, r1b, _, _ = self.refs(l, part)
        top, low = pl.ds(0, half), pl.ds(half, half)

        def along_y(n, carry):
            b = 4 * (1 - at.y) + n
            total = g[at.a, b, top].astype(WIDE) + r0[at.x, b, top].astype(WIDE)
            r1a[b] = (total + r1a[b].astype(WIDE)).astype(LOWER)
            return carry

        def along_x(n, carry):
            x, b = 1 - at.x, 4 * at.y + n
            total = g[2 * at.c + x, b, low].astype(WIDE) + r0[x, b, low].astype(WIDE)
            r1b[x, n] = (total + r1b[x, n].astype(WIDE)).astype(LOWER)
            return carry

        self.copy(l, part, 1).wait_recv()
        lax.fori_loop(0, NZ, along_y, 0)
        self.copy(l, part, 3).start()
        self.copy(l, part, 2).wait_recv()
        lax.fori_loop(0, NZ, along_x, 0)
        self.copy(l, part, 4).start()

    def chip_sums(self, l, part, z):
        at, half = self.at, PART[part] // 2
        g, r0, r1a, r1b, r2, _ = self.refs(l, part)
        top, low, b = pl.ds(0, half), pl.ds(half, half), 4 * at.y + z
        upper = g[at.a, b, top].astype(WIDE) + r0[at.x, b, top].astype(WIDE)
        lower = g[at.a, b, low].astype(WIDE) + r0[at.x, b, low].astype(WIDE)
        return (
            upper + r1a[b].astype(WIDE) + r2[z, top].astype(WIDE),
            lower + r1b[at.x, z].astype(WIDE) + r2[z, low].astype(WIDE),
        )

    def third(self, l, part):
        half = PART[part] // 2
        r2 = self.landing[part][3]
        for n in (3, 4):
            self.copy(l, part, n).wait_recv()
        self.may_send(l, part, 3, 4, 5)
        for n in range(3):
            z = (self.at.z + n + 1) % NZ
            upper, lower = self.chip_sums(l, part, z)
            r2[z, pl.ds(0, half)] = upper.astype(LOWER)
            r2[z, pl.ds(half, half)] = lower.astype(LOWER)
            self.copy(l, part, 5 + n).start()

    def last(self, l, part, out, squares):
        half, row = PART[part] // 2, (0, ATTN)[part]
        r3 = self.landing[part][4]
        upper, lower = self.chip_sums(l, part, self.at.z)
        for n in range(3):
            self.copy(l, part, 5 + n).wait_recv()
            upper = upper + r3[n, pl.ds(0, half)].astype(WIDE)
            lower = lower + r3[n, pl.ds(half, half)].astype(WIDE)
        out[l, row : row + half, :] = upper
        out[l, row + half : row + 2 * half, :] = lower
        squares[0:1, :] += col_sum(upper * upper) + col_sum(lower * lower)
        for n in range(self.COPIES):
            self.copy(l, part, n).wait_send()

        @pl.when(l > 0)
        def _():
            for n, to in zip((0, 1, 2, 5, 4, 3), self.at.partners):
                pl.semaphore_signal(
                    self.credit.at[part, n], inc=1, device_id=to, device_id_type=MESH
                )


class Total:
    COPIES = 6

    def __init__(self, place, own, got, send, recv):
        self.at, self.own, self.got, self.send, self.recv = place, own, got, send, recv

    def copy(self, n):
        src = self.own.at[min(n, 3)]
        return remote(src, self.got.at[n], self.send.at[n], self.recv.at[n], self.at.partners[n])

    def start(self):
        self.copy(0).start()

    def step(self, n):
        self.copy(n).wait_recv()
        self.own[n + 1] = self.own[n] + self.got[n]
        for m in ((1,), (2,), (3, 4, 5))[n]:
            self.copy(m).start()

    def last(self):
        for m in (3, 4, 5):
            self.copy(m).wait_recv()
        total = None
        for z in range(NZ):
            term = self.own[3]
            for n in range(3):
                from_z = (self.at.z + NZ - 1 - n) % NZ
                term = jnp.where(from_z == z, self.got[3 + n], term)
            total = term if total is None else total + term
        return total

    def sent(self):
        for n in range(self.COPIES):
            self.copy(n).wait_send()


def landing_shapes(count):
    half = count // 2
    return [
        (NX, 8, count, D),
        (8, half, D),
        (NX, NZ, half, D),
        (NZ, count, D),
        (3, count, D),
    ]


def stage_rows(qkv, out, up, down, l):
    return (
        [(qkv.at[l, :, pl.ds(j * D, D)], 16 * j, 16) for j in range(3)]
        + [(out.at[l], 48, 16)]
        + [(up.at[l, :, pl.ds(j * D, D)], 64 + 16 * j, 16) for j in range(4)]
        + [(down.at[l], 128, 64)]
    )


def train_kernel(refs, alone):
    k = Kit(**refs)

    def saved(back):
        copies = []
        for n, name in enumerate(SAVED):
            here, there = refs[name].at[0], refs["save_" + name]
            src, dst = (there, here) if back else (here, there)
            copies.append(pltpu.make_async_copy(src, dst, k.save_sem.at[n]))
        return copies

    parts = [(l, part) for l in range(LAYERS) for part in (0, 1)]
    weights = (k.wa, k.wf)
    if alone:
        loads = [
            pltpu.make_async_copy(ref, weights[part].at[l], k.load_sem.at[2 * l + part])
            for l, part in parts
            for ref in [(k.all_a, k.all_f)[part].at[l]]
        ]
        stores = [
            pltpu.make_async_copy(
                weights[part].at[l + 1 - part],
                (k.grad_a, k.grad_f)[part].at[l],
                k.load_sem.at[2 * l + part],
            )
            for l, part in parts
        ]
        for copy in loads:
            copy.start()
    else:
        place = Place()
        gather = Gather(place, weights, k.gather_send, k.gather_recv)
        reduce = Reduce(
            place, weights, (k.land_a, k.land_f), k.reduce_send, k.reduce_recv, k.credit
        )
        sums = Total(place, k.sum_own, k.sum_got, k.sum_send, k.sum_recv)
        norm = Total(place, k.norm_own, k.norm_got, k.norm_send, k.norm_recv)
        staged = []
        for l in range(LAYERS):
            for n, (src, row, count) in enumerate(stage_rows(k.qkv_w, k.out_w, k.up_w, k.down_w, l)):
                dst = k.dsec.at[pl.ds(l * PACK + row, count), :]
                staged.append(pltpu.make_async_copy(src, dst, k.stage_sem.at[l, n]))
        for copy in staged:
            copy.start()
        place.barrier()
        for l in range(LAYERS):
            for copy in staged[9 * l : 9 * l + 9]:
                copy.wait()
            row = l * PACK
            k.wa[l, place.a, place.b] = k.dsec[row : row + ATTN, :].astype(LOWER)
            gather.first(l, 0)
            k.wf[l, place.a, place.b] = k.dsec[row + ATTN : row + PACK, :].astype(LOWER)
            if l < LAYERS - 1:
                gather.first(l, 1)
        k.squares_sum[...] = jnp.zeros_like(k.squares_sum)

    setup_stage(k)
    if not alone:
        gather.second(0, 0)
        gather.second(0, 1)
        gather.third(0, 0)
        gather.second(1, 0)
        gather.third(0, 1)
        gather.fourth(0, 0)

    def forward(l, carry):
        def ahead(n, *stages):
            for stage, part in stages:

                @pl.when(l + n < LAYERS)
                def _(stage=stage, part=part):
                    stage(l + n, part)

        if alone:
            pltpu.make_async_copy(k.all_a.at[l], k.wa.at[l], k.load_sem.at[2 * l]).wait()
        else:
            ahead(1, (gather.second, 1))
            ahead(2, (gather.first, 1))
            ahead(1, (gather.third, 0))
            gather.fourth(l, 1)
            gather.last(l, 0)
        forward_attn(k, l)

        @pl.when(l == 1)
        def _():
            for copy in saved(False):
                copy.wait()

        if alone:
            pltpu.make_async_copy(k.all_f.at[l], k.wf.at[l], k.load_sem.at[2 * l + 1]).wait()
        else:
            ahead(2, (gather.second, 0))
            ahead(1, (gather.third, 1), (gather.fourth, 0))
            gather.last(l, 1)
        forward_ffn(k, l, (l + 1) % 2 + l // 2)

        @pl.when(l == 0)
        def _():
            for copy in saved(False):
                copy.start()

        return carry

    lax.fori_loop(0, LAYERS, forward, 0)
    if not alone:
        for l, part in parts:
            gather.sent(l, part)
    grad = 2
    head_stage(k, grad)

    def backward(n, carry):
        l = LAYERS - 1 - n

        def behind(*stages):
            if alone:
                return

            @pl.when(n > 0)
            def _():
                for stage, part, *more in stages:
                    stage(l + 1, part, *more)

        def now(*stages):
            if not alone:
                for stage, part in stages:
                    stage(l, part)

        finish = () if alone else (k.shard, k.squares_sum)

        @pl.when(n == 2)
        def _():
            for copy in saved(True):
                copy.wait()

        backward_ffn_start(k, l, grad)
        backward_ffn_block(k, l, 0)
        backward_ffn_block(k, l, 1)
        if not alone:
            behind((reduce.third, 1), (reduce.second, 0))
        backward_ffn_block(k, l, 2)
        backward_ffn_block(k, l, 3)
        if not alone:
            behind((reduce.last, 1, *finish), (reduce.third, 0))
            now((reduce.start, 1))
        backward_ffn_end(k, l, grad)
        backward_attn(k, l, grad)
        if not alone:
            behind((reduce.last, 0, *finish))
            now((reduce.first, 1), (reduce.start, 0))
        backward_input(k, l, grad)

        @pl.when(n == 0)
        def _():
            for copy in saved(True):
                copy.start()

        if not alone:
            now((reduce.second, 1), (reduce.first, 0))
        return carry

    lax.fori_loop(0, LAYERS, backward, 0)
    if alone:
        for copy in stores:
            copy.start()
        small_stage(k, k.small_out, grad)
        for copy in stores:
            copy.wait()
        return
    reduce.third(0, 1)
    small_stage(k, k.sum_own.at[0], grad)
    sums.start()
    reduce.second(0, 0)
    reduce.last(0, 1, k.shard, k.squares_sum)
    sums.step(0)
    reduce.third(0, 0)
    sums.step(1)
    reduce.last(0, 0, k.shard, k.squares_sum)
    k.norm_own[0] = k.squares_sum[...]
    norm.start()
    sums.step(2)
    norm.step(0)
    norm.step(1)
    k.small_out[...] = sums.last()
    norm.step(2)
    k.squares[...] = norm.last()
    sums.sent()
    norm.sent()


def train_pass(meta, buf, small, head_bias, log_temp, weights, alone):
    whole = pl.BlockSpec(memory_space=pltpu.VMEM)
    scalars = pl.BlockSpec(memory_space=pltpu.SMEM)
    anywhere = pl.BlockSpec(memory_space=pl.ANY)
    dma = pltpu.SemaphoreType.DMA
    count = 2 * LAYERS
    names = ["meta", "buf", "small", "head_bias", "log_temp"]
    out_shape = {"small_out": ((SMALL, D), WIDE)}
    for name in SAVED:
        shape, dtype = WORK_SHAPES[name]
        out_shape["save_" + name] = (shape[1:], dtype)
    scratch = {name: pltpu.VMEM(*shape) for name, shape in WORK_SHAPES.items()}
    scratch["save_sem"] = dma((len(SAVED),))
    if alone:
        names += ["all_a", "all_f"]
        out_shape["grad_a"] = ((LAYERS, 4, 8, ATTN, D), LOWER)
        out_shape["grad_f"] = ((LAYERS, 4, 8, FFN, D), LOWER)
        scratch["load_sem"] = dma((count,))
    else:
        names += ["qkv_w", "out_w", "up_w", "down_w"]
        out_shape["shard"] = ((LAYERS, PACK, D), WIDE)
        out_shape["squares"] = ((8, D), WIDE)
        for part, name in enumerate("af"):
            for n, shape in enumerate(landing_shapes(PART[part])):
                scratch["land_%s%d" % (name, n)] = pltpu.VMEM(shape, LOWER)
        scratch["stage_sem"] = dma((LAYERS, 9))
        scratch["squares_sum"] = pltpu.VMEM((8, D), WIDE)
        for name, copies in (("gather", Gather.COPIES), ("reduce", Reduce.COPIES)):
            scratch[name + "_send"] = dma((count, copies))
            scratch[name + "_recv"] = dma((count, copies))
        scratch["credit"] = pltpu.SemaphoreType.REGULAR((2, 6))
        for name, rows in (("sum", SMALL), ("norm", 8)):
            scratch[name + "_own"] = pltpu.VMEM((4, rows, D), WIDE)
            scratch[name + "_got"] = pltpu.VMEM((6, rows, D), WIDE)
            scratch[name + "_send"] = dma((6,))
            scratch[name + "_recv"] = dma((6,))
    spaces = dict(head_bias=scalars, log_temp=scalars)
    for name in ("all_a", "all_f", "grad_a", "grad_f", "qkv_w", "out_w", "up_w", "down_w"):
        spaces[name] = anywhere
    for name in SAVED:
        spaces["save_" + name] = anywhere
    every = names + list(out_shape) + list(scratch)

    def kernel(*given):
        refs = dict(zip(every, given))
        for name in "af":
            refs["land_" + name] = [refs.get("land_%s%d" % (name, n)) for n in range(5)]
        train_kernel(refs, alone)

    results = pl.pallas_call(
        kernel,
        name="train_pass",
        out_shape=tuple(jax.ShapeDtypeStruct(*shape) for shape in out_shape.values()),
        in_specs=[spaces.get(name, whole) for name in names],
        out_specs=tuple(spaces.get(name, whole) for name in out_shape),
        scratch_shapes=list(scratch.values()),
        compiler_params=pltpu.CompilerParams(
            vmem_limit_bytes=VMEM_BYTES,
            collective_id=None if alone else 0,
            has_side_effects=not alone,
        ),
        cost_estimate=pl.CostEstimate(
            flops=6 * 10**10, bytes_accessed=4 * 10**7, transcendentals=10**7
        ),
    )(meta, buf, small, head_bias, log_temp, *weights)
    return dict(zip(out_shape, results))


def small_inputs(buf_states, buf_actions, buf_returns, window_starts, window_repeats, valid_steps):
    meta = jnp.concatenate(
        [window_starts[:, None], window_repeats[:, None], valid_steps], 1
    ).astype(WIDE)
    meta = jnp.pad(meta, ((0, 128 - meta.shape[0]), (0, 128 - meta.shape[1])))
    buf = jnp.concatenate([buf_states, buf_actions, buf_returns[:, None]], 1)
    buf = jnp.pad(buf, ((0, 128 - buf.shape[0]), (0, 128 - buf.shape[1])))
    return meta, buf


def adam_parts(weight, grad, first, second, rate):
    first = BETA_ONE * first + (1.0 - BETA_ONE) * grad
    second = BETA_TWO * second + (1.0 - BETA_TWO) * grad * grad
    fix_one = 1.0 - BETA_ONE**STEP
    fix_two = 1.0 - BETA_TWO**STEP
    fresh = weight - rate * (
        first / fix_one / (jnp.sqrt(second / fix_two) + ADAM_EPS) + DECAY * weight
    )
    return fresh, first, second


def adam_kernel(*refs):
    shard, small_grad, squares, groups, log_temp = refs[:5]
    small, small_first, small_second, bias, bias_first, bias_second = refs[5:11]
    mats, firsts, seconds = refs[11:15], refs[15:19], refs[19:23]
    totals, norm, next_temp, s_next, s_first, s_second, b_next, b_first, b_second = refs[23:32]
    m_next, m_copy, m_first, m_second = refs[32:36], refs[36:40], refs[40:44], refs[44:48]
    l = pl.program_id(0)
    extra = small_grad[NROWS : NROWS + 3, 0:128]
    lane = iota((1, 128), 1)
    bias_mean = jnp.where(lane < A, extra[1:2], 0.0)
    bias_spread = jnp.where(lane < A, extra[2:3], 0.0)

    def all_sum(v):
        return jnp.sum(jnp.sum(v, 0, keepdims=True), 1, keepdims=True)

    grads = small_grad[0:NROWS, :]
    square = (
        all_sum(squares[0:1, :])
        + all_sum(grads * grads)
        + all_sum(bias_mean * bias_mean)
        + all_sum(bias_spread * bias_spread)
    )
    length = jnp.sqrt(square)
    clip = jnp.minimum(1.0, CLIP / (length + 1e-06))

    def rate_of(kind):
        group = jnp.full((1, 1), groups[l, kind], jnp.int32).astype(WIDE)
        return LEARN * jnp.exp2(-group)

    def update(kind, rows, cols, grad):
        at = (0, rows, cols)
        fresh, first, second = adam_parts(
            mats[kind][at], clip * grad, firsts[kind][at], seconds[kind][at], rate_of(kind)
        )
        m_next[kind][at] = fresh
        m_copy[kind][at] = fresh.astype(LOWER)
        m_first[kind][at] = first
        m_second[kind][at] = second

    every = slice(0, 16)
    for j in range(3):
        update(0, every, slice(j * D, (j + 1) * D), shard[0, 16 * j : 16 * j + 16, :])
    update(1, every, slice(0, D), shard[0, 48:64, :])
    for j in range(4):
        update(2, every, slice(j * D, (j + 1) * D), shard[0, 64 + 16 * j : 80 + 16 * j, :])
    update(3, slice(0, 64), slice(0, D), shard[0, 128:192, :])

    @pl.when(l == 0)
    def _():
        s_next[...], s_first[...], s_second[...] = adam_parts(
            small[...], clip * grads, small_first[...], small_second[...], LEARN
        )

        def scalar(v, n):
            return jnp.sum(jnp.where(lane == n, v, 0.0))

        def row(ref):
            v = jnp.zeros((1, 128), WIDE)
            for n in range(2 * A):
                v = jnp.where(lane == n, ref[n], v)
            return v

        grad = bias_mean + pltpu.roll(bias_spread, A, 1)
        results = adam_parts(row(bias), clip * grad, row(bias_first), row(bias_second), LEARN)
        for ref, result in zip((b_next, b_first, b_second), results):
            for n in range(2 * A):
                ref[n] = scalar(result, n)
        sums = extra[0:1]
        for n in range(3):
            totals[n] = scalar(sums, n)
        norm[0] = jnp.sum(length)
        logs = jnp.full((1, 1), log_temp[0], WIDE)
        ratio = jnp.full((1, 1), scalar(sums, 1), WIDE) / jnp.full((1, 1), scalar(sums, 2), WIDE)
        next_temp[0] = jnp.sum(logs - TEMP_RATE * jnp.exp(logs) * (ratio + A))


def adam_all(shard, small_grad, squares, groups, log_temp, smalls, biases, mats, firsts, seconds):
    scalars = pl.BlockSpec(memory_space=pltpu.SMEM)

    def fixed(array):
        return pl.BlockSpec(array.shape, lambda l: (0,) * array.ndim)

    def layer(array):
        return pl.BlockSpec((1,) + array.shape[1:], lambda l: (l, 0, 0))

    def like(array, dtype=WIDE):
        return jax.ShapeDtypeStruct(array.shape, dtype)

    stacks = list(mats) + list(firsts) + list(seconds)
    small, bias = smalls[0], biases[0]
    return pl.pallas_call(
        adam_kernel,
        name="adam",
        grid=(LAYERS,),
        out_shape=(
            (jax.ShapeDtypeStruct((3,), WIDE),)
            + (jax.ShapeDtypeStruct((1,), WIDE),) * 2
            + (like(small),) * 3
            + (like(bias),) * 3
            + tuple(like(m) for m in mats)
            + tuple(like(m, LOWER) for m in mats)
            + tuple(like(m) for m in mats) * 2
        ),
        in_specs=[layer(shard), fixed(small_grad), fixed(squares), scalars, scalars]
        + [fixed(small)] * 3
        + [scalars] * 3
        + [layer(m) for m in stacks],
        out_specs=(scalars,) * 3
        + (fixed(small),) * 3
        + (scalars,) * 3
        + tuple(layer(m) for m in mats) * 4,
        compiler_params=pltpu.CompilerParams(vmem_limit_bytes=40 * 1024 * 1024),
        cost_estimate=pl.CostEstimate(flops=10**7, bytes_accessed=8 * 10**6, transcendentals=10**6),
    )(shard, small_grad, squares, groups, log_temp, *smalls, *biases, *stacks)


def gather_packed(mats, axes, count):
    group = count // BLOCKS
    pieces = []
    for mat in mats:
        rows, wide = mat.shape[1], mat.shape[2] // D
        piece = mat.astype(LOWER).reshape(LAYERS, rows, wide, D)
        piece = lax.all_gather(piece, axes, axis=1, tiled=True)
        piece = piece.reshape(LAYERS, NZ, NY, NX, NC, group * rows, wide, D)
        piece = piece.transpose(0, 4, 3, 2, 1, 6, 5, 7)
        pieces.append(piece.reshape(LAYERS, 4, 8, wide * group * rows, D))
    return jnp.concatenate(pieces[:2], 3), jnp.concatenate(pieces[2:], 3)


def scatter_packed(grads, mats, axes):
    results, first = [], 0
    for n, mat in enumerate(mats):
        rows, wide = mat.shape[1], mat.shape[2] // D
        total = lax.psum(1, axes) * rows
        deep = total // BLOCKS
        first = 0 if n % 2 == 0 else first
        piece = grads[n // 2][:, :, :, first : first + wide * deep].astype(WIDE)
        first += wide * deep
        piece = piece.reshape(LAYERS, NC, NX, NY, NZ, wide, deep, D)
        piece = piece.transpose(0, 4, 3, 2, 1, 6, 5, 7).reshape(LAYERS, total, wide * D)
        results.append(lax.psum_scatter(piece, axes, scatter_dimension=1, tiled=True))
    return results


def local(
    buf_states,
    buf_actions,
    buf_returns,
    window_starts,
    window_repeats,
    valid_steps,
    matrix_groups,
    log_temp,
    small_rows,
    head_bias,
    qkv_weight,
    out_weight,
    up_weight,
    down_weight,
    small_first,
    bias_first,
    qkv_first,
    out_first,
    up_first,
    down_first,
    small_second,
    bias_second,
    qkv_second,
    out_second,
    up_second,
    down_second,
):
    axes = ("dp", "fsdp")
    mats = (qkv_weight, out_weight, up_weight, down_weight)
    firsts = (qkv_first, out_first, up_first, down_first)
    seconds = (qkv_second, out_second, up_second, down_second)
    meta, buf = small_inputs(
        buf_states, buf_actions, buf_returns, window_starts, window_repeats, valid_steps
    )
    pass_inputs = (meta, buf, small_rows, head_bias, log_temp)
    if FF // down_weight.shape[1] == BLOCKS and lax.psum(1, "fsdp") == NX * NC:
        made = train_pass(*pass_inputs, mats, False)
        return adam_all(
            made["shard"],
            made["small_out"],
            made["squares"],
            matrix_groups,
            log_temp,
            (small_rows, small_first, small_second),
            (head_bias, bias_first, bias_second),
            mats,
            firsts,
            seconds,
        )
    packed = gather_packed(mats, axes, FF // down_weight.shape[1])
    made = train_pass(*pass_inputs, packed, True)
    big = scatter_packed((made["grad_a"], made["grad_f"]), mats, axes)
    small = made["small_out"]
    small = lax.psum(small, axes)
    small_grad, totals = small[:NROWS], small[NROWS, :3]
    bias_grad = jnp.concatenate([small[NROWS + 1, :A], small[NROWS + 2, :A]])
    square = sum((jnp.sum(piece * piece) for piece in big))
    square = (
        lax.psum(square, axes) + jnp.sum(small_grad * small_grad) + jnp.sum(bias_grad * bias_grad)
    )
    grad_norm = jnp.sqrt(square)
    clip = jnp.minimum(1.0, CLIP / (grad_norm + 1e-06))
    rates = LEARN * jnp.exp2(-matrix_groups.astype(WIDE))
    results = [
        adam_parts(
            mats[kind], clip * big[kind], firsts[kind], seconds[kind], rates[:, kind][:, None, None]
        )
        for kind in range(4)
    ]
    small_new = adam_parts(small_rows, clip * small_grad, small_first, small_second, LEARN)
    bias_new = adam_parts(head_bias, clip * bias_grad, bias_first, bias_second, LEARN)
    next_temp = log_temp - TEMP_RATE * jnp.exp(log_temp) * (totals[1] / totals[2] + A)
    return (
        (totals, grad_norm[None], next_temp)
        + small_new
        + bias_new
        + tuple(r[0] for r in results)
        + tuple(r[0].astype(LOWER) for r in results)
        + tuple(r[1] for r in results)
        + tuple(r[2] for r in results)
    )


def solution(mesh):
    rows = P(("dp", "fsdp"), None)
    vector = P(("dp", "fsdp"))
    stack = P(None, ("dp", "fsdp"), None)
    same = P()
    in_specs = (
        (rows, rows, vector, vector, vector, rows)
        + (same,) * 4
        + (stack,) * 4
        + (same,) * 2
        + (stack,) * 4
        + (same,) * 2
        + (stack,) * 4
    )
    out_specs = (same,) * 9 + (stack,) * 16
    return jax.shard_map(local, mesh=mesh, in_specs=in_specs, out_specs=out_specs, check_vma=False)
```

time: 1270 us -> 379 us (0.30)
  waiting for transfers between devices: 824 us -> 0 us
  Pallas kernels: 194 us -> 353 us
  local copies, waits for them, and re-layouts: 136 us -> 22.7 us
  other arithmetic: 55.6 us -> 1.51 us
  blocking collectives: 36.9 us -> 0 us
  between operations: 23 us -> 1.53 us
    reduce_scatter x4 -> x0, waiting for transfers between devices: 575 us -> none  [scatter_packed(): lax.psum_scatter(piece, axes, scatter_dimension=1, tiled=True)]
    all_gather x4 -> x0, waiting for transfers between devices: 249 us -> none  [gather_packed(): piece = lax.all_gather(piece, axes, axis=1, tiled=True)]
    pallas_call x1 -> x2, Pallas kernels: 194 us -> 353 us  [the longest x1 348 us: train_pass(): pl.pallas_call(kernel, name='train_pass', out_shape=tuple((jax.ShapeDtype...]
    reshape x5 -> x0, local copies, waits for them, and re-layouts: 44.3 us -> none  [the longest x2 31.8 us: scatter_packed(): piece = piece.reshape(LAYERS, total, wide * D)]
    psum x1 -> x0, blocking collectives: 36.9 us -> none  [local(): lax.psum(square, axes) + jnp.sum(small_grad * small_grad)]
    slice x8 -> x0, local copies, waits for them, and re-layouts: 34.8 us -> none  [the longest x6 33.1 us: scatter_packed(): piece = grads[:, :, first:first + wide * deep]]
    convert_element_type x9 -> x0, other arithmetic: 25.2 us -> none  [the longest x1 11.2 us: scatter_packed(): grads = grads[:, jnp.array(order)].astype(WIDE)]
    transpose x3 -> x0, local copies, waits for them, and re-layouts: 17.2 us -> none  [the longest x1 11.1 us: scatter_packed(): piece.reshape(LAYERS, BLOCKS, wide, deep, D).transpose(0, 1, 3, 2, 4)]
  transfers between devices with their start and end apart: 9 -> 0, of which waited for: 8 -> 0; matrix products, arithmetic and copies ran while one was open for 11% -> 0% of each run, Pallas kernels for 0% -> 0%
where the time goes in v3:
time: 379 us
  Pallas kernels  353 us (93%)
  local copies, waits for them, and re-layouts  22.7 us (6%)
    pallas_call x1, Pallas kernels, train_pass(): pl.pallas_call(kernel, name='train_pass', out_shape=tuple((jax.ShapeDtype...  348 us
    unnamed x44, local copies, waits for them, and re-layouts  19.8 us

profile of v3, /device:TPU:0, one launch (start us, length us, event | category | flops | bytes accessed | tf_op | source)
XLA Modules:
  0.0 378.5 jit_solution(14294590644153398318)
XLA Ops:
  1.3 0.7 pad_maximum_fusion
  2.1 0.7 copy.56
  2.8 0.7 copy.57
  3.5 0.8 add_convert_fusion
  4.3 0.1 copy.58
  4.4 0.6 pad.9.given_1_
  5.0 0.6 pad.8.given_0_
  5.7 348.3 %train_pass.1 = (f32[88,512]{1,0:T(8,128)}, f32[1024,512]{1,0:T(8,128)}, f32[1024,512]{1,0:T(8,128)}, bf16[1024,1536]{1,0:T(8,128)(2,1)}, bf16[512,1024]{1,0:T(8...) custom-call(f32[128,128]{1,0:T(8,128)} %pad.8.given_0_, f32[128,128]{1,0:T(8,128)} %pad.9.given_1_, ...), custom_call_target="tpu_custom_call" | custom-call | flops 60000002048 | bytes 40000000 | tf_op jit(solution)/shard_map/train_pass/pallas_call | solution.py:983
  353.9 0.0 copy-start
  354.0 1.3 copy-done
  355.2 0.0 copy-start.1
  355.2 1.0 copy-done.1
  356.2 0.0 copy-start.2
  356.2 1.0 copy-done.2
  357.2 0.0 copy-start.3
  357.2 1.0 copy-done.3
  358.2 0.0 copy-start.4
  358.2 1.0 copy-done.4
  359.2 0.0 copy-start.5
  359.2 1.0 copy-done.5
  360.2 0.0 copy-start.6
  360.2 1.0 copy-done.6
  361.2 0.0 copy-start.7
  361.2 1.0 copy-done.7
  362.2 0.0 copy-start.8
  362.2 1.0 copy-done.8
  363.1 0.0 copy-start.9
  363.1 1.0 copy-done.9
  364.1 0.0 copy-start.10
  364.1 0.9 copy-done.10
  365.0 0.0 copy-start.11
  365.0 0.9 copy-done.11
  365.9 0.0 copy-start.12
  365.9 0.9 copy-done.12
  366.8 0.0 copy-start.13
  366.8 0.9 copy-done.13
  367.8 0.0 copy-start.14
  367.8 0.9 copy-done.14
  368.7 0.0 copy-start.15
  368.7 0.9 copy-done.15
  369.6 0.0 copy-start.16
  369.6 0.9 copy-done.16
  370.4 0.7 copy-done.17
  371.2 0.7 copy-done.18
  371.8 0.7 copy-done.19
  372.5 0.7 copy-done.20
  373.2 0.7 copy-done.21
  373.8 4.6 %adam.1 = (f32[3]{0:T(128)}, f32[1]{0:T(128)}, f32[1]{0:T(128)}, f32[85,512]{1,0:T(8,128)}, f32[85,512]{1,0:T(8,128)}, /*index=5*/f32[85,512]{1,0:T(8,128)}, f32...) custom-call(f32[3,192,512]{2,1,0:T(8,128)S(1)} %copy-done, ...), custom_call_target="tpu_custom_call" | custom-call | flops 10000000 | bytes 8000000 | tf_op jit(solution)/shard_map/adam/pallas_call | solution.py:1113
  (5 shorter events, 0.0 us)
Async XLA Ops:
  353.9 1.3 copy-start
  355.2 1.0 copy-start.1
  356.2 1.0 copy-start.2
  357.2 1.0 copy-start.3
  358.2 1.0 copy-start.4
  359.2 1.0 copy-start.5
  360.2 1.0 copy-start.6
  361.2 1.0 copy-start.7
  362.2 1.0 copy-start.8
  363.1 1.0 copy-start.9
  364.1 0.9 copy-start.10
  365.0 0.9 copy-start.11
  365.9 0.9 copy-start.12
  366.8 0.9 copy-start.13
  367.8 0.9 copy-start.14
  368.7 0.9 copy-start.15
  369.6 0.9 copy-start.16
  370.4 0.7 copy-start.17
  371.2 0.7 copy-start.18
  371.8 0.7 copy-start.19
  372.5 0.7 copy-start.20
  373.2 0.7 copy-start.21

commit v4 on v3

--- a/solution.py
+++ b/solution.py
@@ -560,8 +560,10 @@
 
     def refs(self, l, part):
         grads = self.grads[part].at[l + 1 - part]
-        r0, r1a, r1b, r2, r3 = self.landing[part]
-        return grads, r0, r1a, r1b, r2, r3
+        landing = self.landing[part]
+        if self.credit is None:
+            landing = [ref.at[l] for ref in landing]
+        return (grads, *landing)
 
     def copy(self, l, part, n):
         at, half = self.at, PART[part] // 2
@@ -583,6 +585,9 @@
         return remote(src, dst, self.send.at[q, n], self.recv.at[q, n], to)
 
     def may_send(self, l, part, *partners):
+        if self.credit is None:
+            return
+
         @pl.when(l < LAYERS - 1)
         def _():
             for n in partners:
@@ -653,7 +658,7 @@
 
     def third(self, l, part):
         half = PART[part] // 2
-        r2 = self.landing[part][3]
+        r2 = self.refs(l, part)[4]
         for n in (3, 4):
             self.copy(l, part, n).wait_recv()
         self.may_send(l, part, 3, 4, 5)
@@ -666,7 +671,7 @@
 
     def last(self, l, part, out, squares):
         half, row = PART[part] // 2, (0, ATTN)[part]
-        r3 = self.landing[part][4]
+        r3 = self.refs(l, part)[5]
         upper, lower = self.chip_sums(l, part, self.at.z)
         for n in range(3):
             self.copy(l, part, 5 + n).wait_recv()
@@ -677,6 +682,8 @@
         squares[0:1, :] += col_sum(upper * upper) + col_sum(lower * lower)
         for n in range(self.COPIES):
             self.copy(l, part, n).wait_send()
+        if self.credit is None:
+            return
 
         @pl.when(l > 0)
         def _():
@@ -999,6 +1006,166 @@
     return dict(zip(out_shape, results))
 
 
+def packed_shape(part, layers=LAYERS):
+    return (layers, 4, 8, PART[part], D)
+
+
+def gather_kernel(qkv, out, up, down, all_a, all_f, wa, wf, stage, send, recv, stage_sem, store):
+    place = Place()
+    weights, results = (wa, wf), (all_a, all_f)
+    net = Gather(place, weights, send, recv)
+    staged = []
+    for l in range(LAYERS):
+        for n, (src, row, count) in enumerate(stage_rows(qkv, out, up, down, l)):
+            dst = stage.at[pl.ds(l * PACK + row, count), :]
+            staged.append(pltpu.make_async_copy(src, dst, stage_sem.at[l, n]))
+    for copy in staged:
+        copy.start()
+    place.barrier()
+    parts = [(l, part) for l in range(LAYERS) for part in (0, 1)]
+    for l in range(LAYERS):
+        for copy in staged[9 * l : 9 * l + 9]:
+            copy.wait()
+        row = l * PACK
+        wa[l, place.a, place.b] = stage[row : row + ATTN, :].astype(LOWER)
+        wf[l, place.a, place.b] = stage[row + ATTN : row + PACK, :].astype(LOWER)
+
+    def keep(l, part):
+        return pltpu.make_async_copy(
+            weights[part].at[l], results[part].at[l], store.at[2 * l + part]
+        )
+
+    for l, part in parts[:3]:
+        net.first(l, part)
+    for t in range(len(parts) + 3):
+        if t < len(parts):
+            net.second(*parts[t])
+        if t + 3 < len(parts):
+            net.first(*parts[t + 3])
+        if 0 <= t - 1 < len(parts):
+            net.third(*parts[t - 1])
+        if 0 <= t - 2 < len(parts):
+            net.fourth(*parts[t - 2])
+        if 0 <= t - 3 < len(parts):
+            net.last(*parts[t - 3])
+            keep(*parts[t - 3]).start()
+    for l, part in parts:
+        net.sent(l, part)
+        keep(l, part).wait()
+
+
+def gather_all(mats):
+    anywhere = pl.BlockSpec(memory_space=pl.ANY)
+    dma = pltpu.SemaphoreType.DMA
+    count = 2 * LAYERS
+    return pl.pallas_call(
+        gather_kernel,
+        name="gather",
+        out_shape=tuple(jax.ShapeDtypeStruct(packed_shape(part), LOWER) for part in (0, 1)),
+        in_specs=[anywhere] * 4,
+        out_specs=(anywhere,) * 2,
+        scratch_shapes=[pltpu.VMEM(packed_shape(part), LOWER) for part in (0, 1)]
+        + [pltpu.VMEM((LAYERS * PACK, D), WIDE)]
+        + [dma((count, Gather.COPIES))] * 2
+        + [dma((LAYERS, 9)), dma((count,))],
+        compiler_params=pltpu.CompilerParams(
+            collective_id=0, has_side_effects=True, vmem_limit_bytes=VMEM_BYTES
+        ),
+        cost_estimate=pl.CostEstimate(flops=0, bytes_accessed=4 * 10**7, transcendentals=0),
+    )(*mats)
+
+
+def reduce_kernel(refs):
+    k = Kit(**refs)
+    place = Place()
+    net = Reduce(place, (k.wa, k.wf), (k.land_a, k.land_f), k.send, k.recv, None)
+    sums = Total(place, k.sum_own, k.sum_got, k.sum_send, k.sum_recv)
+    norm = Total(place, k.norm_own, k.norm_got, k.norm_send, k.norm_recv)
+    parts = [(l, part) for l in reversed(range(LAYERS)) for part in (1, 0)]
+
+    def fetch(l, part):
+        return pltpu.make_async_copy(
+            (k.grad_a, k.grad_f)[part].at[l],
+            (k.wa, k.wf)[part].at[l + 1 - part],
+            k.load.at[2 * l + part],
+        )
+
+    for l, part in parts:
+        fetch(l, part).start()
+    k.sum_own[0] = k.small[...]
+    k.squares_sum[...] = jnp.zeros_like(k.squares_sum)
+    place.barrier()
+    sums.start()
+    stages = (net.first, net.second, net.third)
+    for t in range(len(parts) + 4):
+        if t >= 4:
+            net.last(*parts[t - 4], k.shard, k.squares_sum)
+        if t < len(parts):
+            fetch(*parts[t]).wait()
+            net.start(*parts[t])
+        for n, stage in enumerate(stages):
+            if 0 <= t - 1 - n < len(parts):
+                stage(*parts[t - 1 - n])
+        if 1 <= t <= 3:
+            sums.step(t - 1)
+    k.norm_own[0] = k.squares_sum[...]
+    norm.start()
+    k.small_out[...] = sums.last()
+    for n in range(3):
+        norm.step(n)
+    k.squares[...] = norm.last()
+    sums.sent()
+    norm.sent()
+
+
+def reduce_all(grad_a, grad_f, small):
+    whole = pl.BlockSpec(memory_space=pltpu.VMEM)
+    anywhere = pl.BlockSpec(memory_space=pl.ANY)
+    dma = pltpu.SemaphoreType.DMA
+    count = 2 * LAYERS
+    out_shape = {
+        "shard": (LAYERS, PACK, D),
+        "small_out": (SMALL, D),
+        "squares": (8, D),
+    }
+    scratch = dict(
+        wa=pltpu.VMEM(packed_shape(0, LAYERS + 1), LOWER),
+        wf=pltpu.VMEM(packed_shape(1), LOWER),
+        squares_sum=pltpu.VMEM((8, D), WIDE),
+        send=dma((count, Reduce.COPIES)),
+        recv=dma((count, Reduce.COPIES)),
+        load=dma((count,)),
+    )
+    for part, name in enumerate("af"):
+        for n, shape in enumerate(landing_shapes(PART[part])):
+            scratch["land_%s%d" % (name, n)] = pltpu.VMEM((LAYERS,) + shape, LOWER)
+    for name, rows in (("sum", SMALL), ("norm", 8)):
+        scratch[name + "_own"] = pltpu.VMEM((4, rows, D), WIDE)
+        scratch[name + "_got"] = pltpu.VMEM((6, rows, D), WIDE)
+        scratch[name + "_send"] = dma((6,))
+        scratch[name + "_recv"] = dma((6,))
+    every = ["grad_a", "grad_f", "small"] + list(out_shape) + list(scratch)
+
+    def kernel(*given):
+        refs = dict(zip(every, given))
+        for name in "af":
+            refs["land_" + name] = [refs["land_%s%d" % (name, n)] for n in range(5)]
+        reduce_kernel(refs)
+
+    return pl.pallas_call(
+        kernel,
+        name="reduce",
+        out_shape=tuple(jax.ShapeDtypeStruct(shape, WIDE) for shape in out_shape.values()),
+        in_specs=[anywhere, anywhere, whole],
+        out_specs=(whole,) * 3,
+        scratch_shapes=list(scratch.values()),
+        compiler_params=pltpu.CompilerParams(
+            collective_id=1, has_side_effects=True, vmem_limit_bytes=VMEM_BYTES
+        ),
+        cost_estimate=pl.CostEstimate(flops=0, bytes_accessed=4 * 10**7, transcendentals=0),
+    )(grad_a, grad_f, small)
+
+
 def small_inputs(buf_states, buf_actions, buf_returns, window_starts, window_repeats, valid_steps):
     meta = jnp.concatenate(
         [window_starts[:, None], window_repeats[:, None], valid_steps], 1
@@ -1131,7 +1298,7 @@
         + (fixed(small),) * 3
         + (scalars,) * 3
         + tuple(layer(m) for m in mats) * 4,
-        compiler_params=pltpu.CompilerParams(vmem_limit_bytes=40 * 1024 * 1024),
+        compiler_params=pltpu.CompilerParams(vmem_limit_bytes=VMEM_BYTES),
         cost_estimate=pl.CostEstimate(flops=10**7, bytes_accessed=8 * 10**6, transcendentals=10**6),
     )(shard, small_grad, squares, groups, log_temp, *smalls, *biases, *stacks)
 
@@ -1201,11 +1368,12 @@
     )
     pass_inputs = (meta, buf, small_rows, head_bias, log_temp)
     if FF // down_weight.shape[1] == BLOCKS and lax.psum(1, "fsdp") == NX * NC:
-        made = train_pass(*pass_inputs, mats, False)
+        made = train_pass(*pass_inputs, gather_all(mats), True)
+        shard, small, squares = reduce_all(made["grad_a"], made["grad_f"], made["small_out"])
         return adam_all(
-            made["shard"],
-            made["small_out"],
-            made["squares"],
+            shard,
+            small,
+            squares,
             matrix_groups,
             log_temp,
             (small_rows, small_first, small_second),

time: 379 us -> 443 us (1.17)
  Pallas kernels: 353 us -> 436 us
  local copies, waits for them, and re-layouts: 22.7 us -> 2.83 us
    pallas_call x0 -> x2, Pallas kernels: none -> 234 us  [the longest x1 133 us: reduce_all(): pl.pallas_call(kernel, name='reduce', out_shape=tuple((jax.ShapeDtypeStru...]
    pallas_call x1, Pallas kernels: 348 us -> 195 us  [train_pass(): pl.pallas_call(kernel, name='train_pass', out_shape=tuple((jax.ShapeDtype...]
    unnamed x44 -> x0, local copies, waits for them, and re-layouts: 19.8 us -> none
where the time goes in v4:
time: 443 us; the launch traced here: 442 us
  Pallas kernels  436 us (98%)
    pallas_call x1, Pallas kernels, train_pass(): pl.pallas_call(kernel, name='train_pass', out_shape=tuple((jax.ShapeDtype...  195 us
    pallas_call x1, Pallas kernels, reduce_all(): pl.pallas_call(kernel, name='reduce', out_shape=tuple((jax.ShapeDtypeStru...  133 us
    pallas_call x1, Pallas kernels, gather_all(): pl.pallas_call(gather_kernel, name='gather', out_shape=tuple((jax.ShapeDt...  101 us

profile of v4, /device:TPU:0, one launch (start us, length us, event | category | flops | bytes accessed | tf_op | source)
XLA Modules:
  0.0 442.3 jit_solution(5651954684015053140)
XLA Ops:
  1.3 0.7 pad_maximum_fusion
  2.1 0.7 copy.56
  2.8 0.7 copy.57
  3.5 0.8 add_convert_fusion
  4.3 0.1 copy.58
  4.4 0.6 pad.9.given_1_
  5.0 0.6 pad.8.given_0_
  5.7 101.0 %gather.1 = (bf16[3,4,8,64,512]{4,3,2,1,0:T(8,128)(2,1)}, bf16[3,4,8,128,512]{4,3,2,1,0:T(8,128)(2,1)}) custom-call(f32[3,16,1536]{2,1,0:T(8,128)} %refs_11_.1, f32[3,16,512]{2,1,0:T(8,128)} %refs_12_.1, f32[3,16,2048]{2,1,0:T(8,128)} %refs_13_.1, f32[3,64,512]{2,1,0:T(8,128)} %refs_14_.1), custom_call_target="tpu_custom_call" | custom-call | bytes 40000000 | tf_op jit(solution)/shard_map/gather/pallas_call | solution.py:1061
  106.6 195.4 %train_pass.1 = (f32[88,512]{1,0:T(8,128)}, f32[1024,512]{1,0:T(8,128)}, f32[1024,512]{1,0:T(8,128)}, bf16[1024,1536]{1,0:T(8,128)(2,1)}, bf16[512,1024]{1,0:T(8...) custom-call(f32[128,128]{1,0:T(8,128)} %pad.8.given_0_, ...), custom_call_target="tpu_custom_call" | custom-call | flops 60000002048 | bytes 40000000 | tf_op jit(solution)/shard_map/train_pass/pallas_call | solution.py:990
  302.0 132.9 %reduce.1 = (f32[3,192,512]{2,1,0:T(8,128)}, f32[88,512]{1,0:T(8,128)}, f32[8,512]{1,0:T(8,128)}) custom-call(bf16[3,4,8,64,512]{4,3,2,1,0:T(8,128)(2,1)} %get-tuple-element.35.given_0_, bf16[3,4,8,128,512]{4,3,2,1,0:T(8,128)(2,1)} %get-tuple-element.36.given_1_, f32[88,512]{1,0:T(8,128)} %get-tuple-element.37.given_2_), custom_call_target="tpu_custom_call" | custom-call | bytes 40000000 | tf_op jit(solution)/shard_map/reduce/pallas_call | solution.py:1155
  435.0 7.2 %adam.1 = (f32[3]{0:T(128)}, f32[1]{0:T(128)}, f32[1]{0:T(128)}, f32[85,512]{1,0:T(8,128)}, f32[85,512]{1,0:T(8,128)}, /*index=5*/f32[85,512]{1,0:T(8,128)}, f32...) custom-call(f32[3,192,512]{2,1,0:T(8,128)} %get-tuple-element.38.ref, ...), custom_call_target="tpu_custom_call" | custom-call | flops 10000000 | bytes 8000000 | tf_op jit(solution)/shard_map/adam/pallas_call | solution.py:1280

commit v5 on v3

--- a/solution.py
+++ b/solution.py
@@ -37,9 +37,8 @@
 WINS = 16
 SLOT = 64
 ROWS = WINS * SLOT
-CHUNK = 256
+CHUNK = 512
 CHUNKS = ROWS // CHUNK
-UNROLL = 2
 BLOCKS = 32
 PACK = 192
 ATTN, FFN = 64, 128
@@ -50,6 +49,8 @@
 PER = 9 + FF // D
 NROWS = BASE + LAYERS * PER
 SMALL = 88
+HEAD_AT = 64
+EMB_AT = ROWS - 128
 VMEM_BYTES = 64 * 1024 * 1024
 
 
@@ -139,8 +140,8 @@
 
 
 def setup_stage(k):
-    k.emb[...] = jnp.zeros_like(k.emb)
-    k.emb[0:EMB, :] = k.small[0:EMB, :]
+    k.xs[2, EMB_AT:ROWS, :] = jnp.zeros((128, D), WIDE)
+    k.xs[2, EMB_AT : EMB_AT + EMB, :] = k.small[0:EMB, :]
     k.headw[...] = jnp.zeros_like(k.headw)
     k.headw[0, 0:A, :] = k.small[HEADW : HEADW + A, :].astype(LOWER)
     k.headw[1, 0:A, :] = k.small[HEADW + A : HEADW + 2 * A, :].astype(LOWER)
@@ -173,11 +174,12 @@
         )
         marks = ((lane == S + A + 1 + step) | (lane == S + A + 1 + K + kind)) & real
         feats = jnp.where(mine, raw, 0.0) + marks.astype(WIDE)
+        weight = jnp.where((kind == 1) & real, repeat * valid, 0.0)
+        acts = pltpu.roll(raw, HEAD_AT - S, 1)
+        ours = (lane >= HEAD_AT) & (lane < HEAD_AT + A)
+        feats = jnp.where(ours, acts, jnp.where(lane == HEAD_AT + A, weight, feats))
         k.feats[rows, :] = feats
-        weight = jnp.where((kind == 1) & real, repeat * valid, 0.0)
-        acts = pltpu.roll(raw, 128 - S, 1)
-        k.acts[rows, :] = jnp.where(lane < A, acts, jnp.where(lane == A, weight, 0.0))
-        k.xs[0, rows, :] = dot(feats, k.emb[...], HIGH)
+        k.xs[0, rows, :] = dot(feats, k.xs[2, EMB_AT:ROWS, :], HIGH)
         return carry
 
     lax.fori_loop(0, CHUNKS, chunk, 0)
@@ -196,34 +198,44 @@
     return pl.ds(pl.multiple_of(w * SLOT, SLOT), SLOT)
 
 
-def each_chunk(body):
-    def some(n, carry):
-        for c in range(UNROLL):
-            body(UNROLL * n + c, chunk_rows(UNROLL * n + c))
+def each_chunk(body, between=None):
+    def step(c, carry):
+        body(c, chunk_rows(c))
+        if between is not None:
+
+            @pl.when(c < CHUNKS - 1)
+            def _():
+                between()
+
         return carry
 
-    lax.fori_loop(0, CHUNKS // UNROLL, some, 0)
-
-
-def each_window(body):
+    lax.fori_loop(0, CHUNKS, step, 0)
+
+
+def each_window(body, after=None):
     def pair(n, carry):
         body(2 * n)
         body(2 * n + 1)
+        if after is not None:
+            after(pl.ds(pl.multiple_of(n * 128, 128), 128))
         return carry
 
     lax.fori_loop(0, WINS // 2, pair, 0)
 
 
-def forward_attn(k, l):
+def forward_qkv(k, l):
     def chunk(c, rows):
         xhat, _ = norm_parts(k.xs[slot(l), rows, :])
         normed = (xhat * k.row(l, 0) + k.row(l, 1)).astype(LOWER)
-        k.normed_t[slot(l), :, rows] = normed.T
+        k.normed_t[:, rows] = normed.T
         for j in range(3):
             part = dot(normed, k.w_qkv(l, j)) + k.row(l, 4 + j)
-            k.qkv[slot(l), rows, j * D : (j + 1) * D] = part.astype(LOWER)
+            k.qkv[rows, j * D : (j + 1) * D] = part.astype(LOWER)
 
     each_chunk(chunk)
+
+
+def forward_windows(k, l):
     first = iota((SLOT, 128), 1) < HD
 
     def window(w):
@@ -232,8 +244,8 @@
         scores = []
         for p in range(H // 2):
             at = p * 128
-            query = stack_pair(k.qkv[slot(l), rows, at : at + 128] * jnp.asarray(HD**-0.5, LOWER), first)
-            scores.append(dot_nt(k.qkv[slot(l), rows, D + at : D + at + 128], query) + bias)
+            query = stack_pair(k.qkv[rows, at : at + 128] * jnp.asarray(HD**-0.5, LOWER), first)
+            scores.append(dot_nt(k.qkv[rows, D + at : D + at + 128], query) + bias)
         for p in range(H // 2):
             at = p * 128
             peak = jnp.max(scores[p], 0, keepdims=True)
@@ -241,35 +253,37 @@
             total = jnp.sum(expo, 0, keepdims=True)
             probs = (expo * (1.0 / total)).astype(LOWER)
             k.logs[l, w, p : p + 1, :] = peak + jnp.log(total)
-            out = dot_tn(probs, k.qkv[slot(l), rows, 2 * D + at : 2 * D + at + 128])
+            out = dot_tn(probs, k.qkv[rows, 2 * D + at : 2 * D + at + 128])
             k.left[rows, at : at + 128] = join_pair(out, first).astype(LOWER)
 
-    each_window(window)
-
-
-def gelu_parts(h):
-    square = h * h
-    t = jnp.tanh(GELU_C * (h + GELU_A * h * square))
-    return t, square
-
-
-def forward_ffn(k, l, dest):
+    def turn(rows):
+        k.mixed_t[:, rows] = k.left[rows, :].T
+
+    each_window(window, turn)
+
+
+def forward_ffn(k, l, dest, between=None):
     def chunk(c, rows):
-        mixed = k.left[rows, :]
-        k.mixed_t[slot(l), :, rows] = mixed.T
-        mid = k.xs[slot(l), rows, :] + dot(mixed, k.w_out(l)) + k.row(l, 7)
-        k.mid[slot(l), rows, :] = mid
+        mid = k.xs[slot(l), rows, :] + dot(k.left[rows, :], k.w_out(l)) + k.row(l, 7)
+        k.mid[rows, :] = mid
         xhat, _ = norm_parts(mid)
         second = (xhat * k.row(l, 2) + k.row(l, 3)).astype(LOWER)
+        k.second_t[:, rows] = second.T
         out = mid + k.row(l, 12)
         for j in range(4):
+            cols = slice(j * D, (j + 1) * D)
             h = dot(second, k.w_up(l, j)) + k.row(l, 8 + j)
-            t, _ = gelu_parts(h)
-            acted = (0.5 * h * (1.0 + t)).astype(LOWER)
+            square = h * h
+            over = 1.0 + jnp.tanh(h * (GELU_C + GELU_C * GELU_A * square))
+            half = 0.5 * h
+            acted = (half * over).astype(LOWER)
+            slope = over * (0.5 + half * (2.0 - over) * (GELU_C + 3.0 * GELU_A * GELU_C * square))
+            k.slope[rows, cols] = slope.astype(LOWER)
+            k.act_t[cols, rows] = acted.T
             out = out + dot(acted, k.w_down(l, j))
         k.xs[dest, rows, :] = out
 
-    each_chunk(chunk)
+    each_chunk(chunk, between)
 
 
 def head_stage(k, at):
@@ -293,7 +307,7 @@
         feats = (xhat * gain + bias).astype(LOWER)
         mean = dot_nt(feats, k.headw[0]) + bias_mean
         spread = jnp.tanh(dot_nt(feats, k.headw[1]) + bias_spread)
-        acts = k.acts[rows, :]
+        acts = pltpu.roll(k.feats[rows, :], 128 - HEAD_AT, 1)
         weight = acts[:, A : A + 1]
         acts = jnp.where(keep, acts, 0.0)
         target = 0.5 * (jnp.log(1.0 + acts) - jnp.log(1.0 - acts))
@@ -328,47 +342,32 @@
         ref[l, a, b, first : first + count, :] = value[n * count : (n + 1) * count]
 
 
-def backward_ffn_start(k, l, grad):
-    def before(c, rows):
+def backward_ffn(k, l, grad, between=None):
+    def chunk(c, rows):
         d_down = k.xs[grad, rows, :].astype(LOWER)
         k.dout[rows, :] = d_down
         k.sgl[l, 12:13, :] += col_sum(d_down.astype(WIDE))
-        xhat, _ = norm_parts(k.mid[slot(l), rows, :])
-        second = (xhat * k.row(l, 2) + k.row(l, 3)).astype(LOWER)
-        k.left[rows, :] = second
-        k.left_t[:, rows] = second.T
-        k.dsec[rows, :] = jnp.zeros((CHUNK, D), WIDE)
-
-    each_chunk(before)
-
-
-def backward_ffn_block(k, l, j):
-    def chunk(c, rows):
-        h = dot(k.left[rows, :], k.w_up(l, j)) + k.row(l, 8 + j)
-        t, square = gelu_parts(h)
-        half, over = 0.5 * h, 1.0 + t
-        k.act_t[:, rows] = (half * over).astype(LOWER).T
-        slope = over * (0.5 + half * (2.0 - over) * (GELU_C + 3.0 * GELU_A * GELU_C * square))
-        d_acted = dot_nt(k.dout[rows, :], k.w_down(l, j))
-        d_hidden = (d_acted * slope).astype(LOWER)
-        k.work[rows, 0:D] = d_hidden
-        k.sgl[l, 8 + j : 9 + j, :] += col_sum(d_hidden.astype(WIDE))
-        k.dsec[rows, :] += dot_nt(d_hidden, k.w_up(l, j))
-
-    each_chunk(chunk)
-    store_blocks(k.wf, l, range(BLOCKS), 16 * j, 16, dot(k.left_t[...], k.work[:, 0:D]))
-    store_blocks(k.wf, l, range(8 * j, 8 * j + 8), 64, 64, dot(k.act_t[...], k.dout[...]))
-
-
-def backward_ffn_end(k, l, grad):
-    def after(c, rows):
-        xhat, scale = norm_parts(k.mid[slot(l), rows, :])
-        d_second = k.dsec[rows, :]
+        d_second = jnp.zeros((CHUNK, D), WIDE)
+        for j in range(4):
+            cols = slice(j * D, (j + 1) * D)
+            d_acted = dot_nt(d_down, k.w_down(l, j))
+            d_hidden = (d_acted * k.slope[rows, cols].astype(WIDE)).astype(LOWER)
+            k.work[rows, cols] = d_hidden
+            k.sgl[l, 8 + j : 9 + j, :] += col_sum(d_hidden.astype(WIDE))
+            d_second = d_second + dot_nt(d_hidden, k.w_up(l, j))
+        xhat, scale = norm_parts(k.mid[rows, :])
         k.sgl[l, 2:3, :] += col_sum(d_second * xhat)
         k.sgl[l, 3:4, :] += col_sum(d_second)
         k.xs[grad, rows, :] += norm_back(xhat, scale, k.row(l, 2), d_second)
 
-    each_chunk(after)
+    each_chunk(chunk, between)
+
+
+def backward_ffn_grads(k, l):
+    for j in range(4):
+        cols = slice(j * D, (j + 1) * D)
+        store_blocks(k.wf, l, range(BLOCKS), 16 * j, 16, dot(k.second_t[...], k.work[:, cols]))
+        store_blocks(k.wf, l, range(8 * j, 8 * j + 8), 64, 64, dot(k.act_t[cols, :], k.dout[...]))
 
 
 def backward_attn(k, l, grad):
@@ -379,7 +378,7 @@
         k.dout[rows, :] = dot_nt(d_branch, k.w_out(l)).astype(LOWER)
 
     each_chunk(before)
-    store_blocks(k.wa, l + 1, range(BLOCKS), 48, 16, dot(k.mixed_t[slot(l)], k.left[...]))
+    store_blocks(k.wa, l + 1, range(BLOCKS), 48, 16, dot(k.mixed_t[...], k.left[...]))
     first = iota((SLOT, 128), 1) < HD
     scale = HD**-0.5
 
@@ -388,9 +387,9 @@
         bias = k.bias[rows, :]
         for p in range(H // 2):
             at = p * 128
-            query = stack_pair(k.qkv[slot(l), rows, at : at + 128] * jnp.asarray(scale, LOWER), first)
-            keyed = k.qkv[slot(l), rows, D + at : D + at + 128]
-            values = k.qkv[slot(l), rows, 2 * D + at : 2 * D + at + 128]
+            query = stack_pair(k.qkv[rows, at : at + 128] * jnp.asarray(scale, LOWER), first)
+            keyed = k.qkv[rows, D + at : D + at + 128]
+            values = k.qkv[rows, 2 * D + at : 2 * D + at + 128]
             d_mixed = stack_pair(k.dout[rows, at : at + 128], first)
             probs = jnp.exp(dot_nt(keyed, query) + bias - k.logs[l, w, p : p + 1, :])
             d_probs = dot_nt(values, d_mixed)
@@ -404,8 +403,12 @@
             k.work[rows, 2 * D + at : 2 * D + at + 128] = d_values.astype(LOWER)
 
     each_window(window)
+
+
+def backward_attn_grads(k, l):
     for j in range(3):
-        store_blocks(k.wa, l + 1, range(BLOCKS), 16 * j, 16, dot(k.normed_t[slot(l)], k.work[:, j * D : (j + 1) * D]))
+        part = dot(k.normed_t[...], k.work[:, j * D : (j + 1) * D])
+        store_blocks(k.wa, l + 1, range(BLOCKS), 16 * j, 16, part)
 
 
 def backward_input(k, l, grad):
@@ -438,28 +441,28 @@
     wa=((LAYERS + 1, 4, 8, ATTN, D), LOWER),
     wf=((LAYERS, 4, 8, FFN, D), LOWER),
     xs=((3, ROWS, D), WIDE),
-    mid=((2, ROWS, D), WIDE),
-    qkv=((2, ROWS, 3 * D), LOWER),
-    normed_t=((2, D, ROWS), LOWER),
-    mixed_t=((2, D, ROWS), LOWER),
+    qkv=((ROWS, 3 * D), LOWER),
+    normed_t=((D, ROWS), LOWER),
+    mixed_t=((D, ROWS), LOWER),
+    slope=((ROWS, FF), LOWER),
+    act_t=((FF, ROWS), LOWER),
+    second_t=((D, ROWS), LOWER),
+    mid=((ROWS, D), WIDE),
     logs=((LAYERS, WINS, 8, 128), WIDE),
-    work=((ROWS, 3 * D), LOWER),
+    work=((ROWS, FF), LOWER),
     left=((ROWS, D), LOWER),
-    left_t=((D, ROWS), LOWER),
-    act_t=((D, ROWS), LOWER),
     dout=((ROWS, D), LOWER),
-    dsec=((ROWS, D), WIDE),
     feats=((ROWS, 128), WIDE),
-    acts=((ROWS, 128), WIDE),
     bias=((ROWS, 128), WIDE),
-    emb=((128, D), WIDE),
     headw=((2, 128, D), LOWER),
     lrows=((LAYERS, 16, D), WIDE),
     sgl=((LAYERS, 16, D), WIDE),
     sgh=((8, D), WIDE),
     sgw=((2, 8, D), WIDE),
 )
-SAVED = ("xs", "mid", "qkv", "normed_t", "mixed_t")
+KEEP_ATTN = ("qkv", "normed_t", "mixed_t")
+KEEP_FFN = ("slope", "act_t", "second_t", "mid")
+KEEP = KEEP_ATTN + KEEP_FFN
 
 
 MESH = pl.DeviceIdType.MESH
@@ -588,6 +591,16 @@
             for n in partners:
                 pl.semaphore_wait(self.credit.at[part, n], 1)
 
+    def allow(self, l, part, *credits):
+        at = self.at
+
+        @pl.when(l > 0)
+        def _():
+            for n, to in credits:
+                pl.semaphore_signal(
+                    self.credit.at[part, n], inc=1, device_id=to, device_id_type=MESH
+                )
+
     def start(self, l, part):
         self.may_send(l, part, 0)
         self.copy(l, part, 0).start()
@@ -635,6 +648,7 @@
 
         self.copy(l, part, 1).wait_recv()
         lax.fori_loop(0, NZ, along_y, 0)
+        self.may_send(l, part, 6, 7)
         self.copy(l, part, 3).start()
         self.copy(l, part, 2).wait_recv()
         lax.fori_loop(0, NZ, along_x, 0)
@@ -651,57 +665,64 @@
             lower + r1b[at.x, z].astype(WIDE) + r2[z, low].astype(WIDE),
         )
 
-    def third(self, l, part):
-        half = PART[part] // 2
+    def third(self, l, part, out):
+        at, half, row = self.at, PART[part] // 2, (0, ATTN)[part]
         r2 = self.landing[part][3]
         for n in (3, 4):
             self.copy(l, part, n).wait_recv()
         self.may_send(l, part, 3, 4, 5)
         for n in range(3):
-            z = (self.at.z + n + 1) % NZ
+            z = (at.z + n + 1) % NZ
             upper, lower = self.chip_sums(l, part, z)
             r2[z, pl.ds(0, half)] = upper.astype(LOWER)
             r2[z, pl.ds(half, half)] = lower.astype(LOWER)
             self.copy(l, part, 5 + n).start()
+        upper, lower = self.chip_sums(l, part, at.z)
+        out[l, row : row + half, :] = upper
+        out[l, row + half : row + 2 * half, :] = lower
+        for n in range(5):
+            self.copy(l, part, n).wait_send()
+        self.allow(l, part, (0, at.to_c), (1, at.to_x), (2, at.to_y))
 
     def last(self, l, part, out, squares):
-        half, row = PART[part] // 2, (0, ATTN)[part]
+        at, row = self.at, (0, ATTN)[part]
         r3 = self.landing[part][4]
-        upper, lower = self.chip_sums(l, part, self.at.z)
+        rows = slice(row, row + PART[part])
+        total = out[l, rows, :]
         for n in range(3):
             self.copy(l, part, 5 + n).wait_recv()
-            upper = upper + r3[n, pl.ds(0, half)].astype(WIDE)
-            lower = lower + r3[n, pl.ds(half, half)].astype(WIDE)
-        out[l, row : row + half, :] = upper
-        out[l, row + half : row + 2 * half, :] = lower
-        squares[0:1, :] += col_sum(upper * upper) + col_sum(lower * lower)
-        for n in range(self.COPIES):
+            total = total + r3[n].astype(WIDE)
+        out[l, rows, :] = total
+        squares[0:1, :] += col_sum(total * total)
+        for n in range(5, self.COPIES):
             self.copy(l, part, n).wait_send()
-
-        @pl.when(l > 0)
-        def _():
-            for n, to in zip((0, 1, 2, 5, 4, 3), self.at.partners):
-                pl.semaphore_signal(
-                    self.credit.at[part, n], inc=1, device_id=to, device_id_type=MESH
-                )
+        late = [(6, at.to_x), (7, at.to_y)] + [(5 - n, at.to_z[n]) for n in range(3)]
+        self.allow(l, part, *late)
 
 
 class Total:
     COPIES = 6
 
-    def __init__(self, place, own, got, send, recv):
-        self.at, self.own, self.got, self.send, self.recv = place, own, got, send, recv
+    def __init__(self, place, ref, first, rows, send, recv):
+        self.at, self.ref, self.first, self.rows = place, ref, first, rows
+        self.send, self.recv = send, recv
+
+    def own(self, n):
+        return self.ref.at[pl.ds(self.first + n * self.rows, self.rows), :]
+
+    def got(self, n):
+        return self.own(4 + n)
 
     def copy(self, n):
-        src = self.own.at[min(n, 3)]
-        return remote(src, self.got.at[n], self.send.at[n], self.recv.at[n], self.at.partners[n])
+        src, dst = self.own(min(n, 3)), self.got(n)
+        return remote(src, dst, self.send.at[n], self.recv.at[n], self.at.partners[n])
 
     def start(self):
         self.copy(0).start()
 
     def step(self, n):
         self.copy(n).wait_recv()
-        self.own[n + 1] = self.own[n] + self.got[n]
+        self.own(n + 1)[...] = self.own(n)[...] + self.got(n)[...]
         for m in ((1,), (2,), (3, 4, 5))[n]:
             self.copy(m).start()
 
@@ -710,10 +731,10 @@
             self.copy(m).wait_recv()
         total = None
         for z in range(NZ):
-            term = self.own[3]
+            term = self.own(3)[...]
             for n in range(3):
                 from_z = (self.at.z + NZ - 1 - n) % NZ
-                term = jnp.where(from_z == z, self.got[3 + n], term)
+                term = jnp.where(from_z == z, self.got(3 + n)[...], term)
             total = term if total is None else total + term
         return total
 
@@ -742,16 +763,45 @@
     )
 
 
+GATHER_PLAN = {
+    (-1, "start"): [("first", 0, 0), ("first", 0, 1), ("first", 1, 0), ("first", 1, 1)],
+    (-1, "setup"): [("second", 0, 0), ("third", 0, 0), ("fourth", 0, 0), ("last", 0, 0)],
+    (0, "qkv"): [("second", 0, 1), ("first", 2, 0), ("second", 1, 0)],
+    (0, "windows"): [("third", 0, 1), ("first", 2, 1), ("fourth", 0, 1), ("last", 0, 1)],
+    (0, "half"): [("third", 1, 0), ("second", 1, 1)],
+    (0, "ffn"): [("fourth", 1, 0), ("second", 2, 0), ("last", 1, 0)],
+    (1, "qkv"): [("third", 1, 1), ("fourth", 1, 1)],
+    (1, "windows"): [("third", 2, 0), ("second", 2, 1), ("last", 1, 1)],
+    (1, "half"): [("fourth", 2, 0)],
+    (1, "ffn"): [("last", 2, 0), ("third", 2, 1)],
+    (2, "qkv"): [("fourth", 2, 1)],
+    (2, "windows"): [("last", 2, 1)],
+}
+
+
 def train_kernel(refs, alone):
     k = Kit(**refs)
 
-    def saved(back):
+    def kept(names, l, back):
         copies = []
-        for n, name in enumerate(SAVED):
-            here, there = refs[name].at[0], refs["save_" + name]
+        for name in names:
+            here, there = refs[name], refs["keep_" + name].at[l]
             src, dst = (there, here) if back else (here, there)
-            copies.append(pltpu.make_async_copy(src, dst, k.save_sem.at[n]))
+            copies.append(pltpu.make_async_copy(src, dst, k.keep_sem.at[KEEP.index(name)]))
         return copies
+
+    def start(copies):
+        for copy in copies:
+            copy.start()
+
+    def wait(copies):
+        for copy in copies:
+            copy.wait()
+
+    def kept_x(back):
+        here, there = k.xs.at[0], k.keep_x
+        src, dst = (there, here) if back else (here, there)
+        return [pltpu.make_async_copy(src, dst, k.keep_sem.at[len(KEEP)])]
 
     parts = [(l, part) for l in range(LAYERS) for part in (0, 1)]
     weights = (k.wa, k.wf)
@@ -769,80 +819,87 @@
             )
             for l, part in parts
         ]
-        for copy in loads:
-            copy.start()
+        start(loads)
     else:
         place = Place()
         gather = Gather(place, weights, k.gather_send, k.gather_recv)
         reduce = Reduce(
             place, weights, (k.land_a, k.land_f), k.reduce_send, k.reduce_recv, k.credit
         )
-        sums = Total(place, k.sum_own, k.sum_got, k.sum_send, k.sum_recv)
-        norm = Total(place, k.norm_own, k.norm_got, k.norm_send, k.norm_recv)
+        sums = Total(place, k.mid, 0, SMALL, k.sum_send, k.sum_recv)
+        norm = Total(place, k.mid, 10 * SMALL, 8, k.norm_send, k.norm_recv)
+
+    def run(plan):
+        for stage, l, part in plan:
+            getattr(gather, stage)(l, part)
+
+    def poll(l, point):
+        if alone:
+            return
+        for layer in range(LAYERS):
+            plan = GATHER_PLAN.get((layer, point))
+            if plan:
+
+                @pl.when(l == layer)
+                def _(plan=plan):
+                    run(plan)
+
+    if not alone:
         staged = []
         for l in range(LAYERS):
             for n, (src, row, count) in enumerate(stage_rows(k.qkv_w, k.out_w, k.up_w, k.down_w, l)):
-                dst = k.dsec.at[pl.ds(l * PACK + row, count), :]
+                dst = k.xs.at[2, pl.ds(l * PACK + row, count), :]
                 staged.append(pltpu.make_async_copy(src, dst, k.stage_sem.at[l, n]))
-        for copy in staged:
-            copy.start()
+        start(staged)
         place.barrier()
         for l in range(LAYERS):
-            for copy in staged[9 * l : 9 * l + 9]:
-                copy.wait()
+            wait(staged[9 * l : 9 * l + 9])
             row = l * PACK
-            k.wa[l, place.a, place.b] = k.dsec[row : row + ATTN, :].astype(LOWER)
-            gather.first(l, 0)
-            k.wf[l, place.a, place.b] = k.dsec[row + ATTN : row + PACK, :].astype(LOWER)
-            if l < LAYERS - 1:
-                gather.first(l, 1)
+            for part, (low, high) in enumerate(((0, ATTN), (ATTN, PACK))):
+                weights[part][l, place.a, place.b] = k.xs[2, row + low : row + high, :].astype(LOWER)
+                if ("first", l, part) in GATHER_PLAN[-1, "start"]:
+                    gather.first(l, part)
         k.squares_sum[...] = jnp.zeros_like(k.squares_sum)
 
     setup_stage(k)
+    start(kept_x(False))
     if not alone:
-        gather.second(0, 0)
-        gather.second(0, 1)
-        gather.third(0, 0)
-        gather.second(1, 0)
-        gather.third(0, 1)
-        gather.fourth(0, 0)
+        run(GATHER_PLAN[-1, "setup"])
 
     def forward(l, carry):
-        def ahead(n, *stages):
-            for stage, part in stages:
-
-                @pl.when(l + n < LAYERS)
-                def _(stage=stage, part=part):
-                    stage(l + n, part)
-
         if alone:
             pltpu.make_async_copy(k.all_a.at[l], k.wa.at[l], k.load_sem.at[2 * l]).wait()
-        else:
-            ahead(1, (gather.second, 1))
-            ahead(2, (gather.first, 1))
-            ahead(1, (gather.third, 0))
-            gather.fourth(l, 1)
-            gather.last(l, 0)
-        forward_attn(k, l)
+
+        @pl.when(l > 0)
+        def _():
+            wait(kept(KEEP_ATTN, l - 1, False))
+
+        forward_qkv(k, l)
+        poll(l, "qkv")
+        forward_windows(k, l)
+
+        @pl.when(l < LAYERS - 1)
+        def _():
+            start(kept(KEEP_ATTN, l, False))
+
+        @pl.when(l > 0)
+        def _():
+            wait(kept(KEEP_FFN, l - 1, False))
 
         @pl.when(l == 1)
         def _():
-            for copy in saved(False):
-                copy.wait()
+            wait(kept_x(False))
 
         if alone:
             pltpu.make_async_copy(k.all_f.at[l], k.wf.at[l], k.load_sem.at[2 * l + 1]).wait()
-        else:
-            ahead(2, (gather.second, 0))
-            ahead(1, (gather.third, 1), (gather.fourth, 0))
-            gather.last(l, 1)
-        forward_ffn(k, l, (l + 1) % 2 + l // 2)
-
-        @pl.when(l == 0)
+        poll(l, "windows")
+        forward_ffn(k, l, (l + 1) % 2 + l // 2, lambda: poll(l, "half"))
+
+        @pl.when(l < LAYERS - 1)
         def _():
-            for copy in saved(False):
-                copy.start()
-
+            start(kept(KEEP_FFN, l, False))
+
+        poll(l, "ffn")
         return carry
 
     lax.fori_loop(0, LAYERS, forward, 0)
@@ -864,62 +921,71 @@
                 for stage, part, *more in stages:
                     stage(l + 1, part, *more)
 
-        def now(*stages):
-            if not alone:
-                for stage, part in stages:
-                    stage(l, part)
-
-        finish = () if alone else (k.shard, k.squares_sum)
-
-        @pl.when(n == 2)
+        @pl.when(n > 0)
         def _():
-            for copy in saved(True):
-                copy.wait()
-
-        backward_ffn_start(k, l, grad)
-        backward_ffn_block(k, l, 0)
-        backward_ffn_block(k, l, 1)
+            wait(kept(KEEP_FFN, l, True))
+
+        backward_ffn(k, l, grad)
         if not alone:
-            behind((reduce.third, 1), (reduce.second, 0))
-        backward_ffn_block(k, l, 2)
-        backward_ffn_block(k, l, 3)
+            behind((reduce.second, 1), (reduce.second, 0))
+        backward_ffn_grads(k, l)
+
+        @pl.when(n < LAYERS - 1)
+        def _():
+            start(kept(KEEP_FFN, l - 1, True))
+
         if not alone:
-            behind((reduce.last, 1, *finish), (reduce.third, 0))
-            now((reduce.start, 1))
-        backward_ffn_end(k, l, grad)
+            behind((reduce.third, 1, k.shard), (reduce.third, 0, k.shard))
+            reduce.start(l, 1)
+
+        @pl.when(n > 0)
+        def _():
+            wait(kept(KEEP_ATTN, l, True))
+
         backward_attn(k, l, grad)
         if not alone:
-            behind((reduce.last, 0, *finish))
-            now((reduce.first, 1), (reduce.start, 0))
+            reduce.first(l, 1)
+        backward_attn_grads(k, l)
+
+        @pl.when(n < LAYERS - 1)
+        def _():
+            start(kept(KEEP_ATTN, l - 1, True))
+
+        if not alone:
+            reduce.start(l, 0)
+            behind((reduce.last, 1, k.shard, k.squares_sum), (reduce.last, 0, k.shard, k.squares_sum))
+
+        @pl.when(n == LAYERS - 1)
+        def _():
+            wait(kept_x(True))
+
         backward_input(k, l, grad)
 
         @pl.when(n == 0)
         def _():
-            for copy in saved(True):
-                copy.start()
+            start(kept_x(True))
 
         if not alone:
-            now((reduce.second, 1), (reduce.first, 0))
+            reduce.first(l, 0)
         return carry
 
     lax.fori_loop(0, LAYERS, backward, 0)
     if alone:
-        for copy in stores:
-            copy.start()
+        start(stores)
         small_stage(k, k.small_out, grad)
-        for copy in stores:
-            copy.wait()
+        wait(stores)
         return
-    reduce.third(0, 1)
-    small_stage(k, k.sum_own.at[0], grad)
+    small_stage(k, sums.own(0), grad)
     sums.start()
+    reduce.second(0, 1)
     reduce.second(0, 0)
+    sums.step(0)
+    reduce.third(0, 1, k.shard)
+    reduce.third(0, 0, k.shard)
+    sums.step(1)
     reduce.last(0, 1, k.shard, k.squares_sum)
-    sums.step(0)
-    reduce.third(0, 0)
-    sums.step(1)
     reduce.last(0, 0, k.shard, k.squares_sum)
-    k.norm_own[0] = k.squares_sum[...]
+    norm.own(0)[...] = k.squares_sum[...]
     norm.start()
     sums.step(2)
     norm.step(0)
@@ -939,11 +1005,12 @@
     count = 2 * LAYERS
     names = ["meta", "buf", "small", "head_bias", "log_temp"]
     out_shape = {"small_out": ((SMALL, D), WIDE)}
-    for name in SAVED:
+    for name in KEEP:
         shape, dtype = WORK_SHAPES[name]
-        out_shape["save_" + name] = (shape[1:], dtype)
+        out_shape["keep_" + name] = ((LAYERS - 1,) + shape, dtype)
+    out_shape["keep_x"] = ((ROWS, D), WIDE)
     scratch = {name: pltpu.VMEM(*shape) for name, shape in WORK_SHAPES.items()}
-    scratch["save_sem"] = dma((len(SAVED),))
+    scratch["keep_sem"] = dma((len(KEEP) + 1,))
     if alone:
         names += ["all_a", "all_f"]
         out_shape["grad_a"] = ((LAYERS, 4, 8, ATTN, D), LOWER)
@@ -961,17 +1028,15 @@
         for name, copies in (("gather", Gather.COPIES), ("reduce", Reduce.COPIES)):
             scratch[name + "_send"] = dma((count, copies))
             scratch[name + "_recv"] = dma((count, copies))
-        scratch["credit"] = pltpu.SemaphoreType.REGULAR((2, 6))
-        for name, rows in (("sum", SMALL), ("norm", 8)):
-            scratch[name + "_own"] = pltpu.VMEM((4, rows, D), WIDE)
-            scratch[name + "_got"] = pltpu.VMEM((6, rows, D), WIDE)
+        scratch["credit"] = pltpu.SemaphoreType.REGULAR((2, 8))
+        for name in ("sum", "norm"):
             scratch[name + "_send"] = dma((6,))
             scratch[name + "_recv"] = dma((6,))
     spaces = dict(head_bias=scalars, log_temp=scalars)
     for name in ("all_a", "all_f", "grad_a", "grad_f", "qkv_w", "out_w", "up_w", "down_w"):
         spaces[name] = anywhere
-    for name in SAVED:
-        spaces["save_" + name] = anywhere
+    for name in KEEP + ("x",):
+        spaces["keep_" + name] = anywhere
     every = names + list(out_shape) + list(scratch)
 
     def kernel(*given):
@@ -1131,7 +1196,7 @@
         + (fixed(small),) * 3
         + (scalars,) * 3
         + tuple(layer(m) for m in mats) * 4,
-        compiler_params=pltpu.CompilerParams(vmem_limit_bytes=40 * 1024 * 1024),
+        compiler_params=pltpu.CompilerParams(vmem_limit_bytes=VMEM_BYTES),
         cost_estimate=pl.CostEstimate(flops=10**7, bytes_accessed=8 * 10**6, transcendentals=10**6),
     )(shard, small_grad, squares, groups, log_temp, *smalls, *biases, *stacks)
 

time: 379 us -> 339 us (0.89)
  Pallas kernels: 353 us -> 332 us
  local copies, waits for them, and re-layouts: 22.7 us -> 2.83 us
    pallas_call x1, Pallas kernels: 348 us -> 325 us  [train_pass(): pl.pallas_call(kernel, name='train_pass', out_shape=tuple((jax.ShapeDtype...]
    unnamed x44 -> x0, local copies, waits for them, and re-layouts: 19.8 us -> none
where the time goes in v5:
time: 339 us; the launch traced here: 338 us
  Pallas kernels  332 us (98%)
    pallas_call x1, Pallas kernels, train_pass(): pl.pallas_call(kernel, name='train_pass', out_shape=tuple((jax.ShapeDtype...  325 us
    pallas_call x1, Pallas kernels, adam_all(): pl.pallas_call(adam_kernel, name='adam', grid=(LAYERS,), out_shape=(jax.S...  7.17 us

profile of v5, /device:TPU:0, one launch (start us, length us, event | category | flops | bytes accessed | tf_op | source)
XLA Modules:
  0.0 338.2 jit_solution(8215786779477859806)
XLA Ops:
  1.3 0.7 pad_maximum_fusion
  2.1 0.7 copy.56
  2.8 0.7 copy.57
  3.5 0.8 add_convert_fusion
  4.3 0.1 copy.58
  4.4 0.6 pad.9.given_1_
  5.0 0.6 pad.8.given_0_
  5.7 325.2 %train_pass.1 = (f32[88,512]{1,0:T(8,128)}, bf16[2,1024,1536]{2,1,0:T(8,128)(2,1)}, bf16[2,512,1024]{2,1,0:T(8,128)(2,1)}, bf16[2,512,1024]{2,1,0:T(8,128)(2,1)}...) custom-call(f32[128,128]{1,0:T(8,128)} %pad.8.given_0_, ...), custom_call_target="tpu_custom_call" | custom-call | flops 60000002048 | bytes 40000000 | tf_op jit(solution)/shard_map/train_pass/pallas_call | solution.py:1048
  330.9 7.2 %adam.1 = (f32[3]{0:T(128)}, f32[1]{0:T(128)}, f32[1]{0:T(128)}, f32[85,512]{1,0:T(8,128)}, f32[85,512]{1,0:T(8,128)}, /*index=5*/f32[85,512]{1,0:T(8,128)}, f32...) custom-call(f32[3,192,512]{2,1,0:T(8,128)} %get-tuple-element.28.ref, ...), custom_call_target="tpu_custom_call" | custom-call | flops 10000000 | bytes 8000000 | tf_op jit(solution)/shard_map/adam/pallas_call | solution.py:1178

commit v6 on v5

--- a/solution.py
+++ b/solution.py
@@ -35,6 +35,7 @@
 
 LAYERS = 3
 WINS = 16
+BUF_DEV = 64
 SLOT = 64
 ROWS = WINS * SLOT
 CHUNK = 512
@@ -151,31 +152,45 @@
     k.sgh[...] = jnp.zeros_like(k.sgh)
     k.sgw[...] = jnp.zeros_like(k.sgw)
 
+    lane, sub = iota((WINS, 128), 1), iota((WINS, 128), 0)
+    k.meta[...] = jnp.zeros_like(k.meta)
+    k.meta[0:WINS, 0:K] = k.valid[...].astype(WIDE)
+    meta = k.meta[0:WINS, :]
+    for w in range(WINS):
+        for n, ref in enumerate((k.starts, k.repeats)):
+            meta = jnp.where((sub == w) & (lane == K + n), ref[w].astype(WIDE), meta)
+    k.meta[0:WINS, :] = meta
     meta = k.meta[...].astype(LOWER)
+    k.buf[...] = jnp.zeros_like(k.buf)
+    k.buf[0, 0:S, 0:BUF_DEV] = k.states[...]
+    k.buf[0, S + A : S + A + 1, 0:BUF_DEV] = k.returns[...]
+    k.buf[1, 0:A, 0:BUF_DEV] = k.actions[...]
 
     def chunk(c, carry):
         rows = chunk_rows(c)
         win, step, kind, real = token_rows(c * CHUNK, CHUNK)
         lane = iota((CHUNK, 128), 1)
         tok = dot((lane == win).astype(WIDE).astype(LOWER), meta)
-        start, repeat = tok[:, 0:1], tok[:, 1:2]
-        valid = jnp.sum(jnp.where(lane == step + 2, tok, 0.0), -1, keepdims=True)
+        start, repeat = tok[:, K : K + 1], tok[:, K + 1 : K + 2]
+        valid = jnp.sum(jnp.where(lane == step, tok, 0.0), -1, keepdims=True)
         key = iota((CHUNK, 128), 0) & (SLOT - 1)
         query = lane & (SLOT - 1)
         allowed = (key <= query) & (((valid > 0.5) & real) | (key == query))
         k.bias[rows, :] = jnp.where(allowed, 0.0, MASKED)
         place = start.astype(jnp.int32) + step
         source = ((lane == place) & real).astype(WIDE)
-        raw = dot(source, k.buf[...], HIGH)
+        raw = dot_nt(source, k.buf[0], HIGH)
+        acts = dot_nt(source, k.buf[1], HIGH)
         mine = (
             ((lane < S) & (kind == 1))
             | ((lane >= S) & (lane < S + A) & (kind == 2))
             | ((lane == S + A) & (kind == 0))
         )
+        raw = raw + pltpu.roll(acts, S, 1)
         marks = ((lane == S + A + 1 + step) | (lane == S + A + 1 + K + kind)) & real
         feats = jnp.where(mine, raw, 0.0) + marks.astype(WIDE)
         weight = jnp.where((kind == 1) & real, repeat * valid, 0.0)
-        acts = pltpu.roll(raw, HEAD_AT - S, 1)
+        acts = pltpu.roll(acts, HEAD_AT, 1)
         ours = (lane >= HEAD_AT) & (lane < HEAD_AT + A)
         feats = jnp.where(ours, acts, jnp.where(lane == HEAD_AT + A, weight, feats))
         k.feats[rows, :] = feats
@@ -212,10 +227,16 @@
     lax.fori_loop(0, CHUNKS, step, 0)
 
 
-def each_window(body, after=None):
+def each_window(body, after=None, between=None):
     def pair(n, carry):
         body(2 * n)
         body(2 * n + 1)
+        if between is not None:
+
+            @pl.when(n == WINS // 4 - 1)
+            def _():
+                between()
+
         if after is not None:
             after(pl.ds(pl.multiple_of(n * 128, 128), 128))
         return carry
@@ -370,7 +391,7 @@
         store_blocks(k.wf, l, range(8 * j, 8 * j + 8), 64, 64, dot(k.act_t[cols, :], k.dout[...]))
 
 
-def backward_attn(k, l, grad):
+def backward_attn(k, l, grad, between=None):
     def before(c, rows):
         d_branch = k.xs[grad, rows, :].astype(LOWER)
         k.left[rows, :] = d_branch
@@ -402,7 +423,7 @@
             k.work[rows, D + at : D + at + 128] = d_keyed.astype(LOWER)
             k.work[rows, 2 * D + at : 2 * D + at + 128] = d_values.astype(LOWER)
 
-    each_window(window)
+    each_window(window, None, between)
 
 
 def backward_attn_grads(k, l):
@@ -459,6 +480,8 @@
     sgl=((LAYERS, 16, D), WIDE),
     sgh=((8, D), WIDE),
     sgw=((2, 8, D), WIDE),
+    meta=((128, 128), WIDE),
+    buf=((2, 128, 128), WIDE),
 )
 KEEP_ATTN = ("qkv", "normed_t", "mixed_t")
 KEEP_FFN = ("slope", "act_t", "second_t", "mid")
@@ -842,7 +865,8 @@
 
                 @pl.when(l == layer)
                 def _(plan=plan):
-                    run(plan)
+                    with jax.named_scope("gather_" + point):
+                        run(plan)
 
     if not alone:
         staged = []
@@ -861,10 +885,12 @@
                     gather.first(l, part)
         k.squares_sum[...] = jnp.zeros_like(k.squares_sum)
 
-    setup_stage(k)
+    with jax.named_scope("embedding"):
+        setup_stage(k)
     start(kept_x(False))
     if not alone:
-        run(GATHER_PLAN[-1, "setup"])
+        with jax.named_scope("gather_setup"):
+            run(GATHER_PLAN[-1, "setup"])
 
     def forward(l, carry):
         if alone:
@@ -874,9 +900,11 @@
         def _():
             wait(kept(KEEP_ATTN, l - 1, False))
 
-        forward_qkv(k, l)
+        with jax.named_scope("qkv"):
+            forward_qkv(k, l)
         poll(l, "qkv")
-        forward_windows(k, l)
+        with jax.named_scope("attention"):
+            forward_windows(k, l)
 
         @pl.when(l < LAYERS - 1)
         def _():
@@ -893,7 +921,8 @@
         if alone:
             pltpu.make_async_copy(k.all_f.at[l], k.wf.at[l], k.load_sem.at[2 * l + 1]).wait()
         poll(l, "windows")
-        forward_ffn(k, l, (l + 1) % 2 + l // 2, lambda: poll(l, "half"))
+        with jax.named_scope("ffn"):
+            forward_ffn(k, l, (l + 1) % 2 + l // 2, lambda: poll(l, "half"))
 
         @pl.when(l < LAYERS - 1)
         def _():
@@ -907,66 +936,85 @@
         for l, part in parts:
             gather.sent(l, part)
     grad = 2
-    head_stage(k, grad)
+    with jax.named_scope("head"):
+        head_stage(k, grad)
 
     def backward(n, carry):
         l = LAYERS - 1 - n
 
-        def behind(*stages):
-            if alone:
-                return
-
+        def behind(name, *stages):
             @pl.when(n > 0)
             def _():
-                for stage, part, *more in stages:
-                    stage(l + 1, part, *more)
+                with jax.named_scope(name):
+                    for stage, part, *more in stages:
+                        stage(l + 1, part, *more)
 
         @pl.when(n > 0)
         def _():
             wait(kept(KEEP_FFN, l, True))
 
-        backward_ffn(k, l, grad)
+        finish = () if alone else (k.shard, k.squares_sum)
+
+        def ffn_between():
+            if not alone:
+                behind("reduce_third", (reduce.third, 1, k.shard))
+
+        def attn_between():
+            if not alone:
+                with jax.named_scope("reduce_first"):
+                    reduce.first(l, 1)
+                behind("reduce_last", (reduce.last, 1, *finish))
+
+        with jax.named_scope("ffn_back"):
+            backward_ffn(k, l, grad, ffn_between)
         if not alone:
-            behind((reduce.second, 1), (reduce.second, 0))
-        backward_ffn_grads(k, l)
+            behind("reduce_second", (reduce.second, 0))
+        with jax.named_scope("ffn_grads"):
+            backward_ffn_grads(k, l)
 
         @pl.when(n < LAYERS - 1)
         def _():
             start(kept(KEEP_FFN, l - 1, True))
 
         if not alone:
-            behind((reduce.third, 1, k.shard), (reduce.third, 0, k.shard))
-            reduce.start(l, 1)
+            with jax.named_scope("reduce_start"):
+                reduce.start(l, 1)
+            behind("reduce_third", (reduce.third, 0, k.shard))
 
         @pl.when(n > 0)
         def _():
             wait(kept(KEEP_ATTN, l, True))
 
-        backward_attn(k, l, grad)
-        if not alone:
-            reduce.first(l, 1)
-        backward_attn_grads(k, l)
+        with jax.named_scope("attention_back"):
+            backward_attn(k, l, grad, attn_between)
+        with jax.named_scope("qkv_grads"):
+            backward_attn_grads(k, l)
 
         @pl.when(n < LAYERS - 1)
         def _():
             start(kept(KEEP_ATTN, l - 1, True))
 
         if not alone:
-            reduce.start(l, 0)
-            behind((reduce.last, 1, k.shard, k.squares_sum), (reduce.last, 0, k.shard, k.squares_sum))
+            with jax.named_scope("reduce_start"):
+                reduce.start(l, 0)
+            behind("reduce_last", (reduce.last, 0, *finish))
 
         @pl.when(n == LAYERS - 1)
         def _():
             wait(kept_x(True))
 
-        backward_input(k, l, grad)
+        with jax.named_scope("qkv_back"):
+            backward_input(k, l, grad)
 
         @pl.when(n == 0)
         def _():
             start(kept_x(True))
 
         if not alone:
-            reduce.first(l, 0)
+            with jax.named_scope("reduce_second"):
+                reduce.second(l, 1)
+            with jax.named_scope("reduce_first"):
+                reduce.first(l, 0)
         return carry
 
     lax.fori_loop(0, LAYERS, backward, 0)
@@ -975,35 +1023,41 @@
         small_stage(k, k.small_out, grad)
         wait(stores)
         return
-    small_stage(k, sums.own(0), grad)
+    with jax.named_scope("small_grads"):
+        small_stage(k, sums.own(0), grad)
     sums.start()
-    reduce.second(0, 1)
-    reduce.second(0, 0)
+    with jax.named_scope("reduce_third"):
+        reduce.third(0, 1, k.shard)
+    with jax.named_scope("reduce_second"):
+        reduce.second(0, 0)
     sums.step(0)
-    reduce.third(0, 1, k.shard)
-    reduce.third(0, 0, k.shard)
+    with jax.named_scope("reduce_third"):
+        reduce.third(0, 0, k.shard)
     sums.step(1)
-    reduce.last(0, 1, k.shard, k.squares_sum)
-    reduce.last(0, 0, k.shard, k.squares_sum)
-    norm.own(0)[...] = k.squares_sum[...]
-    norm.start()
-    sums.step(2)
-    norm.step(0)
-    norm.step(1)
-    k.small_out[...] = sums.last()
-    norm.step(2)
-    k.squares[...] = norm.last()
+    with jax.named_scope("reduce_last"):
+        reduce.last(0, 1, k.shard, k.squares_sum)
+        reduce.last(0, 0, k.shard, k.squares_sum)
+    with jax.named_scope("norm_sums"):
+        norm.own(0)[...] = k.squares_sum[...]
+        norm.start()
+        sums.step(2)
+        norm.step(0)
+        norm.step(1)
+        k.small_out[...] = sums.last()
+        norm.step(2)
+        k.squares[...] = norm.last()
     sums.sent()
     norm.sent()
 
 
-def train_pass(meta, buf, small, head_bias, log_temp, weights, alone):
+def train_pass(inputs, weights, alone):
     whole = pl.BlockSpec(memory_space=pltpu.VMEM)
     scalars = pl.BlockSpec(memory_space=pltpu.SMEM)
     anywhere = pl.BlockSpec(memory_space=pl.ANY)
     dma = pltpu.SemaphoreType.DMA
     count = 2 * LAYERS
-    names = ["meta", "buf", "small", "head_bias", "log_temp"]
+    names = ["states", "actions", "returns", "starts", "repeats", "valid"]
+    names += ["log_temp", "small", "head_bias"]
     out_shape = {"small_out": ((SMALL, D), WIDE)}
     for name in KEEP:
         shape, dtype = WORK_SHAPES[name]
@@ -1032,7 +1086,7 @@
         for name in ("sum", "norm"):
             scratch[name + "_send"] = dma((6,))
             scratch[name + "_recv"] = dma((6,))
-    spaces = dict(head_bias=scalars, log_temp=scalars)
+    spaces = dict.fromkeys(("starts", "repeats", "head_bias", "log_temp"), scalars)
     for name in ("all_a", "all_f", "grad_a", "grad_f", "qkv_w", "out_w", "up_w", "down_w"):
         spaces[name] = anywhere
     for name in KEEP + ("x",):
@@ -1060,18 +1114,8 @@
         cost_estimate=pl.CostEstimate(
             flops=6 * 10**10, bytes_accessed=4 * 10**7, transcendentals=10**7
         ),
-    )(meta, buf, small, head_bias, log_temp, *weights)
+    )(*inputs, *weights)
     return dict(zip(out_shape, results))
-
-
-def small_inputs(buf_states, buf_actions, buf_returns, window_starts, window_repeats, valid_steps):
-    meta = jnp.concatenate(
-        [window_starts[:, None], window_repeats[:, None], valid_steps], 1
-    ).astype(WIDE)
-    meta = jnp.pad(meta, ((0, 128 - meta.shape[0]), (0, 128 - meta.shape[1])))
-    buf = jnp.concatenate([buf_states, buf_actions, buf_returns[:, None]], 1)
-    buf = jnp.pad(buf, ((0, 128 - buf.shape[0]), (0, 128 - buf.shape[1])))
-    return meta, buf
 
 
 def adam_parts(weight, grad, first, second, rate):
@@ -1261,12 +1305,19 @@
     mats = (qkv_weight, out_weight, up_weight, down_weight)
     firsts = (qkv_first, out_first, up_first, down_first)
     seconds = (qkv_second, out_second, up_second, down_second)
-    meta, buf = small_inputs(
-        buf_states, buf_actions, buf_returns, window_starts, window_repeats, valid_steps
+    pass_inputs = (
+        buf_states.T,
+        buf_actions.T,
+        buf_returns[None],
+        window_starts,
+        window_repeats,
+        valid_steps,
+        log_temp,
+        small_rows,
+        head_bias,
     )
-    pass_inputs = (meta, buf, small_rows, head_bias, log_temp)
     if FF // down_weight.shape[1] == BLOCKS and lax.psum(1, "fsdp") == NX * NC:
-        made = train_pass(*pass_inputs, mats, False)
+        made = train_pass(pass_inputs, mats, False)
         return adam_all(
             made["shard"],
             made["small_out"],
@@ -1280,7 +1331,7 @@
             seconds,
         )
     packed = gather_packed(mats, axes, FF // down_weight.shape[1])
-    made = train_pass(*pass_inputs, packed, True)
+    made = train_pass(pass_inputs, packed, True)
     big = scatter_packed((made["grad_a"], made["grad_f"]), mats, axes)
     small = made["small_out"]
     small = lax.psum(small, axes)

time: 339 us -> 308 us (0.909)
  Pallas kernels: 332 us -> 307 us
    pallas_call x1, Pallas kernels: 325 us -> 299 us  [train_pass(): pl.pallas_call(kernel, name='train_pass', out_shape=tuple((jax.ShapeDtype...]
where the time goes in v6:
time: 308 us
  Pallas kernels  307 us (100%)
    pallas_call x1, Pallas kernels, train_pass(): pl.pallas_call(kernel, name='train_pass', out_shape=tuple((jax.ShapeDtype...  299 us
    pallas_call x1, Pallas kernels, adam_all(): pl.pallas_call(adam_kernel, name='adam', grid=(LAYERS,), out_shape=(jax.S...  7.17 us

profile of v6, /device:TPU:0, one launch (start us, length us, event | category | flops | bytes accessed | tf_op | source)
XLA Modules:
  0.0 308.1 jit_solution(3584724157047392519)
XLA Ops:
  1.3 299.5 %train_pass.1 = (f32[88,512]{1,0:T(8,128)}, bf16[2,1024,1536]{2,1,0:T(8,128)(2,1)}, bf16[2,512,1024]{2,1,0:T(8,128)(2,1)}, bf16[2,512,1024]{2,1,0:T(8,128)(2,1)}...) custom-call(f32[11,64]{1,0:T(8,128)} %bitcast.3, ...), custom_call_target="tpu_custom_call" | custom-call | flops 60000002048 | bytes 40000000 | tf_op jit(solution)/shard_map/train_pass/pallas_call | solution.py:1102
  300.8 7.2 %adam.1 = (f32[3]{0:T(128)}, f32[1]{0:T(128)}, f32[1]{0:T(128)}, f32[85,512]{1,0:T(8,128)}, f32[85,512]{1,0:T(8,128)}, /*index=5*/f32[85,512]{1,0:T(8,128)}, f32...) custom-call(f32[3,192,512]{2,1,0:T(8,128)} %get-tuple-element.28.ref, ...), custom_call_target="tpu_custom_call" | custom-call | flops 10000000 | bytes 8000000 | tf_op jit(solution)/shard_map/adam/pallas_call | solution.py:1222

commit v7 on v6

--- a/solution.py
+++ b/solution.py
@@ -1,4 +1,3 @@
-import functools
 import math
 
 import jax
@@ -49,7 +48,7 @@
 BASE = EMB + 2 + 2 * A
 PER = 9 + FF // D
 NROWS = BASE + LAYERS * PER
-SMALL = 88
+SMALL = 96
 HEAD_AT = 64
 EMB_AT = ROWS - 128
 VMEM_BYTES = 64 * 1024 * 1024
@@ -244,7 +243,7 @@
     lax.fori_loop(0, WINS // 2, pair, 0)
 
 
-def forward_qkv(k, l):
+def forward_qkv(k, l, between):
     def chunk(c, rows):
         xhat, _ = norm_parts(k.xs[slot(l), rows, :])
         normed = (xhat * k.row(l, 0) + k.row(l, 1)).astype(LOWER)
@@ -253,10 +252,10 @@
             part = dot(normed, k.w_qkv(l, j)) + k.row(l, 4 + j)
             k.qkv[rows, j * D : (j + 1) * D] = part.astype(LOWER)
 
-    each_chunk(chunk)
-
-
-def forward_windows(k, l):
+    each_chunk(chunk, between)
+
+
+def forward_windows(k, l, between):
     first = iota((SLOT, 128), 1) < HD
 
     def window(w):
@@ -280,17 +279,16 @@
     def turn(rows):
         k.mixed_t[:, rows] = k.left[rows, :].T
 
-    each_window(window, turn)
-
-
-def forward_ffn(k, l, dest, between=None):
+    each_window(window, turn, between)
+
+
+def forward_up(k, l, between):
     def chunk(c, rows):
         mid = k.xs[slot(l), rows, :] + dot(k.left[rows, :], k.w_out(l)) + k.row(l, 7)
         k.mid[rows, :] = mid
         xhat, _ = norm_parts(mid)
         second = (xhat * k.row(l, 2) + k.row(l, 3)).astype(LOWER)
         k.second_t[:, rows] = second.T
-        out = mid + k.row(l, 12)
         for j in range(4):
             cols = slice(j * D, (j + 1) * D)
             h = dot(second, k.w_up(l, j)) + k.row(l, 8 + j)
@@ -299,12 +297,19 @@
             half = 0.5 * h
             acted = (half * over).astype(LOWER)
             slope = over * (0.5 + half * (2.0 - over) * (GELU_C + 3.0 * GELU_A * GELU_C * square))
+            k.work[rows, cols] = acted
             k.slope[rows, cols] = slope.astype(LOWER)
             k.act_t[cols, rows] = acted.T
-            out = out + dot(acted, k.w_down(l, j))
-        k.xs[dest, rows, :] = out
 
     each_chunk(chunk, between)
+
+
+def forward_down(k, l, dest):
+    def chunk(c, rows):
+        w_down = jnp.concatenate([k.w_down(l, j) for j in range(4)], 0)
+        k.xs[dest, rows, :] = k.mid[rows, :] + k.row(l, 12) + dot(k.work[rows, :], w_down)
+
+    each_chunk(chunk)
 
 
 def head_stage(k, at):
@@ -384,14 +389,19 @@
     each_chunk(chunk, between)
 
 
-def backward_ffn_grads(k, l):
+def backward_down_grads(k, l):
     for j in range(4):
-        cols = slice(j * D, (j + 1) * D)
-        store_blocks(k.wf, l, range(BLOCKS), 16 * j, 16, dot(k.second_t[...], k.work[:, cols]))
-        store_blocks(k.wf, l, range(8 * j, 8 * j + 8), 64, 64, dot(k.act_t[cols, :], k.dout[...]))
-
-
-def backward_attn(k, l, grad, between=None):
+        part = dot(k.act_t[j * D : (j + 1) * D, :], k.dout[...])
+        store_blocks(k.wf, l, range(8 * j, 8 * j + 8), 64, 64, part)
+
+
+def backward_up_grads(k, l):
+    for j in range(4):
+        part = dot(k.second_t[...], k.work[:, j * D : (j + 1) * D])
+        store_blocks(k.wf, l, range(BLOCKS), 16 * j, 16, part)
+
+
+def backward_out(k, l, grad):
     def before(c, rows):
         d_branch = k.xs[grad, rows, :].astype(LOWER)
         k.left[rows, :] = d_branch
@@ -400,6 +410,9 @@
 
     each_chunk(before)
     store_blocks(k.wa, l + 1, range(BLOCKS), 48, 16, dot(k.mixed_t[...], k.left[...]))
+
+
+def backward_windows(k, l, between):
     first = iota((SLOT, 128), 1) < HD
     scale = HD**-0.5
 
@@ -492,7 +505,8 @@
 NZ, NY, NX, NC = 4, 2, 2, 2
 NR = NY * NX * NC
 SHARD = PACK
-PART = (ATTN, FFN)
+PARTS, DEEP = 3, 64
+HALF = DEEP // 2
 
 
 class Place:
@@ -501,17 +515,23 @@
         self.z, self.y = dp // NY, dp % NY
         self.x, self.c = fsdp // NC, fsdp % NC
         self.a, self.b = 2 * self.c + self.x, 4 * self.y + self.z
-        self.to_x = (dp, (1 - self.x) * NC + self.c)
-        self.to_y = (self.z * NY + 1 - self.y, fsdp)
-        self.to_c = (dp, self.x * NC + 1 - self.c)
+        self.r = 4 * self.y + fsdp
         self.to_z = [(((self.z + d) % NZ) * NY + self.y, fsdp) for d in range(1, NZ)]
-        self.partners = [self.to_c, self.to_x, self.to_y] + self.to_z
+        self.odd = self.z % 2
+        self.to_pair = ((self.z + 1 - 2 * self.odd) * NY + self.y, fsdp)
+        self.plane = []
+        for d in range(1, 8):
+            y, x, c = [
+                1 - v if d & bit else v for v, bit in ((self.y, 4), (self.x, 2), (self.c, 1))
+            ]
+            self.plane.append((self.z * NY + y, x * NC + c))
+        self.to_c, self.to_x, self.to_y = self.plane[0], self.plane[1], self.plane[3]
 
     def barrier(self):
         sem = pltpu.get_barrier_semaphore()
-        for partner in self.partners:
+        for partner in self.plane + self.to_z:
             pl.semaphore_signal(sem, inc=1, device_id=partner, device_id_type=MESH)
-        pl.semaphore_wait(sem, len(self.partners))
+        pl.semaphore_wait(sem, len(self.plane) + len(self.to_z))
 
 
 def remote(src, dst, send, recv, to):
@@ -520,28 +540,40 @@
     )
 
 
+def part_ref(weights, part):
+    return weights[min(part, 1)], (0, 0, DEEP)[part]
+
+
 class Gather:
-    COPIES = 11
+    COPIES = 13
 
     def __init__(self, place, weights, send, recv):
         self.at, self.weights, self.send, self.recv = place, weights, send, recv
 
     def copy(self, l, part, n):
-        at, count = self.at, PART[part]
-        half = count // 2
-        a, b, rows, to = at.a, pl.ds(4 * at.y, 4), pl.ds(0, count), at.to_c
+        at = self.at
+        array, row = part_ref(self.weights, part)
+        a, b, rows, to = at.a, pl.ds(4 * at.y, 4), pl.ds(row, DEEP), at.to_c
         if n < 3:
             b, to = at.b, at.to_z[n]
         elif n < 5:
             to = (at.to_x, at.to_y)[n - 3]
-        if n in (6, 8, 10):
+        if n in (6, 8, 10, 11, 12):
             a = 2 * at.c + 1 - at.x
-        if n in (7, 9, 10):
+        if n in (7, 9, 10, 11, 12):
             b = pl.ds(4 * (1 - at.y), 4)
         if n in (6, 7):
-            rows, to = pl.ds((n - 6) * half, half), (at.to_y, at.to_x)[n - 6]
-        ref = self.weights[part].at[l, a, b, rows, :]
-        q = 2 * l + part
+            first = row + at.odd * HALF + (n - 6) * (HALF // 2)
+            rows = pl.ds(pl.multiple_of(first, HALF // 2), HALF // 2)
+            to = (at.to_y, at.to_x)[n - 6]
+        if n in (10, 11):
+            rows = pl.ds(pl.multiple_of(row + at.odd * HALF, HALF), HALF)
+        if n == 11:
+            to = at.to_pair
+        if n == 12:
+            rows = pl.ds(pl.multiple_of(row + (1 - at.odd) * HALF, HALF), HALF)
+        ref = array.at[l, a, b, rows, :]
+        q = PARTS * l + part
         return remote(ref, ref, self.send.at[q, n], self.recv.at[q, n], to)
 
     def start(self, l, part, *ns):
@@ -567,10 +599,14 @@
 
     def fourth(self, l, part):
         self.wait(l, part, 6, 7)
-        self.start(l, part, 10)
+        self.start(l, part, 11, 10)
+
+    def fifth(self, l, part):
+        self.wait(l, part, 11)
+        self.start(l, part, 12)
 
     def last(self, l, part):
-        self.wait(l, part, 5, 8, 9, 10)
+        self.wait(l, part, 5, 8, 9, 10, 12)
 
     def sent(self, l, part):
         for n in range(self.COPIES):
@@ -585,12 +621,12 @@
         self.send, self.recv, self.credit = send, recv, credit
 
     def refs(self, l, part):
-        grads = self.grads[part].at[l + 1 - part]
-        r0, r1a, r1b, r2, r3 = self.landing[part]
-        return grads, r0, r1a, r1b, r2, r3
+        array, row = part_ref(self.grads, part)
+        grads = array.at[l + 1 - min(part, 1), :, :, pl.ds(row, DEEP), :]
+        return (grads, *self.landing[part])
 
     def copy(self, l, part, n):
-        at, half = self.at, PART[part] // 2
+        at, half = self.at, HALF
         g, r0, r1a, r1b, r2, r3 = self.refs(l, part)
         top, low, other = pl.ds(0, half), pl.ds(half, half), pl.ds(4 * (1 - at.y), 4)
         if n == 0:
@@ -605,7 +641,7 @@
             src, dst, to = r1b.at[1 - at.x], r2.at[:, low, :], at.to_x
         else:
             src, dst, to = r2.at[(at.z + n - 4) % NZ], r3.at[n - 5], at.to_z[n - 5]
-        q = 2 * l + part
+        q = PARTS * l + part
         return remote(src, dst, self.send.at[q, n], self.recv.at[q, n], to)
 
     def may_send(self, l, part, *partners):
@@ -629,7 +665,7 @@
         self.copy(l, part, 0).start()
 
     def first(self, l, part):
-        at, half = self.at, PART[part] // 2
+        at, half = self.at, HALF
         g, r0, _, _, _, _ = self.refs(l, part)
         top, low = pl.ds(0, half), pl.ds(half, half)
         self.copy(l, part, 0).wait_recv()
@@ -653,7 +689,7 @@
         self.copy(l, part, 2).start()
 
     def second(self, l, part):
-        at, half = self.at, PART[part] // 2
+        at, half = self.at, HALF
         g, r0, r1a, r1b, _, _ = self.refs(l, part)
         top, low = pl.ds(0, half), pl.ds(half, half)
 
@@ -678,7 +714,7 @@
         self.copy(l, part, 4).start()
 
     def chip_sums(self, l, part, z):
-        at, half = self.at, PART[part] // 2
+        at, half = self.at, HALF
         g, r0, r1a, r1b, r2, _ = self.refs(l, part)
         top, low, b = pl.ds(0, half), pl.ds(half, half), 4 * at.y + z
         upper = g[at.a, b, top].astype(WIDE) + r0[at.x, b, top].astype(WIDE)
@@ -689,7 +725,7 @@
         )
 
     def third(self, l, part, out):
-        at, half, row = self.at, PART[part] // 2, (0, ATTN)[part]
+        at, half, row = self.at, HALF, DEEP * part
         r2 = self.landing[part][3]
         for n in (3, 4):
             self.copy(l, part, n).wait_recv()
@@ -708,9 +744,9 @@
         self.allow(l, part, (0, at.to_c), (1, at.to_x), (2, at.to_y))
 
     def last(self, l, part, out, squares):
-        at, row = self.at, (0, ATTN)[part]
+        at, row = self.at, DEEP * part
         r3 = self.landing[part][4]
-        rows = slice(row, row + PART[part])
+        rows = slice(row, row + DEEP)
         total = out[l, rows, :]
         for n in range(3):
             self.copy(l, part, 5 + n).wait_recv()
@@ -724,57 +760,110 @@
 
 
 class Total:
-    COPIES = 6
-
-    def __init__(self, place, ref, first, rows, send, recv):
-        self.at, self.ref, self.first, self.rows = place, ref, first, rows
+    COPIES = 7
+
+    def __init__(self, place, ref, rows, send, recv):
+        self.at, self.ref, self.rows = place, ref, rows // 2
         self.send, self.recv = send, recv
 
-    def own(self, n):
-        return self.ref.at[pl.ds(self.first + n * self.rows, self.rows), :]
-
-    def got(self, n):
-        return self.own(4 + n)
+    def half(self, n):
+        return self.ref.at[pl.ds(pl.multiple_of(n * self.rows, 8), self.rows), :]
+
+    def whole(self):
+        return self.ref.at[pl.ds(0, 2 * self.rows), :]
 
     def copy(self, n):
-        src, dst = self.own(min(n, 3)), self.got(n)
-        return remote(src, dst, self.send.at[n], self.recv.at[n], self.at.partners[n])
+        at = self.at
+        mine, other = self.half(at.c), self.half(1 - at.c)
+        src, dst, to = (
+            (other, self.half(2), at.to_c),
+            (self.half(8), self.half(3), at.to_x),
+            (self.half(9), self.half(4), at.to_y),
+            (self.half(10), self.half(5), at.to_z[0]),
+            (self.half(10), self.half(6), at.to_z[1]),
+            (self.half(10), self.half(7), at.to_z[2]),
+            (mine, self.half(11), at.to_c),
+        )[n]
+        return remote(src, dst, self.send.at[n], self.recv.at[n], to)
 
     def start(self):
         self.copy(0).start()
 
     def step(self, n):
         self.copy(n).wait_recv()
-        self.own(n + 1)[...] = self.own(n)[...] + self.got(n)[...]
+        own = self.half(self.at.c) if n == 0 else self.half(7 + n)
+        self.half(8 + n)[...] = own[...] + self.half(2 + n)[...]
         for m in ((1,), (2,), (3, 4, 5))[n]:
             self.copy(m).start()
 
-    def last(self):
+    def back(self):
         for m in (3, 4, 5):
             self.copy(m).wait_recv()
+        self.copy(0).wait_send()
         total = None
         for z in range(NZ):
-            term = self.own(3)[...]
+            term = self.half(10)[...]
             for n in range(3):
                 from_z = (self.at.z + NZ - 1 - n) % NZ
-                term = jnp.where(from_z == z, self.got(3 + n)[...], term)
+                term = jnp.where(from_z == z, self.half(5 + n)[...], term)
             total = term if total is None else total + term
+        self.half(self.at.c)[...] = total
+        self.copy(6).start()
+
+    def last(self):
+        self.copy(6).wait_recv()
+        self.half(1 - self.at.c)[...] = self.half(11)[...]
+        for n in range(1, self.COPIES):
+            self.copy(n).wait_send()
+
+
+class Norm:
+    COPIES = 10
+
+    def __init__(self, place, plane, column, send, recv):
+        self.at, self.plane, self.column = place, plane, column
+        self.send, self.recv = send, recv
+
+    def copy(self, n):
+        at = self.at
+        if n < 7:
+            ref, to = self.plane.at[at.r], at.plane[n]
+        else:
+            ref, to = self.column.at[at.z], at.to_z[n - 7]
+        return remote(ref, ref, self.send.at[n], self.recv.at[n], to)
+
+    def start(self, tile):
+        self.plane[self.at.r] = tile
+        for n in range(7):
+            self.copy(n).start()
+
+    def total(self, ref, ns):
+        for n in ns:
+            self.copy(n).wait_recv()
+        total = ref[0]
+        for n in range(1, ref.shape[0]):
+            total = total + ref[n]
         return total
 
-    def sent(self):
+    def step(self):
+        self.column[self.at.z] = self.total(self.plane, range(7))
+        for n in range(7, self.COPIES):
+            self.copy(n).start()
+
+    def last(self):
+        total = self.total(self.column, range(7, self.COPIES))
         for n in range(self.COPIES):
             self.copy(n).wait_send()
-
-
-def landing_shapes(count):
-    half = count // 2
-    return [
-        (NX, 8, count, D),
-        (8, half, D),
-        (NX, NZ, half, D),
-        (NZ, count, D),
-        (3, count, D),
-    ]
+        return total
+
+
+LANDING = (
+    (NX, 8, DEEP, D),
+    (8, HALF, D),
+    (NX, NZ, HALF, D),
+    (NZ, DEEP, D),
+    (3, DEEP, D),
+)
 
 
 def stage_rows(qkv, out, up, down, l):
@@ -787,18 +876,28 @@
 
 
 GATHER_PLAN = {
-    (-1, "start"): [("first", 0, 0), ("first", 0, 1), ("first", 1, 0), ("first", 1, 1)],
-    (-1, "setup"): [("second", 0, 0), ("third", 0, 0), ("fourth", 0, 0), ("last", 0, 0)],
-    (0, "qkv"): [("second", 0, 1), ("first", 2, 0), ("second", 1, 0)],
-    (0, "windows"): [("third", 0, 1), ("first", 2, 1), ("fourth", 0, 1), ("last", 0, 1)],
-    (0, "half"): [("third", 1, 0), ("second", 1, 1)],
-    (0, "ffn"): [("fourth", 1, 0), ("second", 2, 0), ("last", 1, 0)],
-    (1, "qkv"): [("third", 1, 1), ("fourth", 1, 1)],
-    (1, "windows"): [("third", 2, 0), ("second", 2, 1), ("last", 1, 1)],
-    (1, "half"): [("fourth", 2, 0)],
-    (1, "ffn"): [("last", 2, 0), ("third", 2, 1)],
-    (2, "qkv"): [("fourth", 2, 1)],
-    (2, "windows"): [("last", 2, 1)],
+    (-1, "begin"): [("first", 0, 0), ("first", 0, 1)],
+    (-1, "setup"): [("first", 0, 2), ("first", 1, 0), ("second", 0, 0)],
+    (0, "start"): [("second", 0, 1), ("first", 1, 1), ("third", 0, 0), ("fourth", 0, 0), ("second", 0, 2), ("first", 1, 2), ("third", 0, 1), ("fifth", 0, 0), ("last", 0, 0), ("second", 1, 0), ("fourth", 0, 1)],
+    (0, "qkv"): [("first", 2, 0), ("third", 0, 2), ("fifth", 0, 1)],
+    (0, "windows_half"): [("second", 1, 1), ("last", 0, 1)],
+    (0, "windows"): [("fourth", 0, 2)],
+    (0, "up_half"): [("first", 2, 1), ("third", 1, 0), ("fifth", 0, 2), ("second", 1, 2)],
+    (0, "up"): [("last", 0, 2), ("fourth", 1, 0), ("second", 2, 0)],
+    (0, "down"): [("first", 2, 2), ("third", 1, 1), ("fifth", 1, 0)],
+    (1, "start"): [("last", 1, 0), ("fourth", 1, 1)],
+    (1, "qkv_half"): [("second", 2, 1)],
+    (1, "qkv"): [("third", 1, 2), ("fifth", 1, 1)],
+    (1, "windows_half"): [("last", 1, 1)],
+    (1, "windows"): [("second", 2, 2), ("fourth", 1, 2)],
+    (1, "up_half"): [("third", 2, 0), ("fifth", 1, 2), ("last", 1, 2)],
+    (1, "up"): [("fourth", 2, 0)],
+    (1, "down"): [("third", 2, 1), ("fifth", 2, 0)],
+    (2, "start"): [("last", 2, 0), ("fourth", 2, 1)],
+    (2, "qkv"): [("third", 2, 2), ("fifth", 2, 1)],
+    (2, "windows_half"): [("last", 2, 1)],
+    (2, "windows"): [("fourth", 2, 2)],
+    (2, "up_half"): [("fifth", 2, 2), ("last", 2, 2)],
 }
 
 
@@ -826,31 +925,29 @@
         src, dst = (there, here) if back else (here, there)
         return [pltpu.make_async_copy(src, dst, k.keep_sem.at[len(KEEP)])]
 
-    parts = [(l, part) for l in range(LAYERS) for part in (0, 1)]
+    arrays = [(l, n) for l in range(LAYERS) for n in (0, 1)]
+    parts = [(l, part) for l in range(LAYERS) for part in range(PARTS)]
     weights = (k.wa, k.wf)
     if alone:
         loads = [
-            pltpu.make_async_copy(ref, weights[part].at[l], k.load_sem.at[2 * l + part])
-            for l, part in parts
-            for ref in [(k.all_a, k.all_f)[part].at[l]]
+            pltpu.make_async_copy((k.all_a, k.all_f)[n].at[l], weights[n].at[l], k.load_sem.at[2 * l + n])
+            for l, n in arrays
         ]
         stores = [
             pltpu.make_async_copy(
-                weights[part].at[l + 1 - part],
-                (k.grad_a, k.grad_f)[part].at[l],
-                k.load_sem.at[2 * l + part],
+                weights[n].at[l + 1 - n], (k.grad_a, k.grad_f)[n].at[l], k.load_sem.at[2 * l + n]
             )
-            for l, part in parts
+            for l, n in arrays
         ]
         start(loads)
     else:
         place = Place()
         gather = Gather(place, weights, k.gather_send, k.gather_recv)
         reduce = Reduce(
-            place, weights, (k.land_a, k.land_f), k.reduce_send, k.reduce_recv, k.credit
+            place, weights, k.landing, k.reduce_send, k.reduce_recv, k.credit
         )
-        sums = Total(place, k.mid, 0, SMALL, k.sum_send, k.sum_recv)
-        norm = Total(place, k.mid, 10 * SMALL, 8, k.norm_send, k.norm_recv)
+        sums = Total(place, k.mid, SMALL, k.sum_send, k.sum_recv)
+        norm = Norm(place, k.norm_plane, k.norm_column, k.norm_send, k.norm_recv)
 
     def run(plan):
         for stage, l, part in plan:
@@ -879,9 +976,11 @@
         for l in range(LAYERS):
             wait(staged[9 * l : 9 * l + 9])
             row = l * PACK
-            for part, (low, high) in enumerate(((0, ATTN), (ATTN, PACK))):
-                weights[part][l, place.a, place.b] = k.xs[2, row + low : row + high, :].astype(LOWER)
-                if ("first", l, part) in GATHER_PLAN[-1, "start"]:
+            for part in range(PARTS):
+                array, first = part_ref(weights, part)
+                mine = k.xs[2, row + DEEP * part : row + DEEP * (part + 1), :].astype(LOWER)
+                array[l, place.a, place.b, first : first + DEEP, :] = mine
+                if ("first", l, part) in GATHER_PLAN[-1, "begin"]:
                     gather.first(l, part)
         k.squares_sum[...] = jnp.zeros_like(k.squares_sum)
 
@@ -900,11 +999,12 @@
         def _():
             wait(kept(KEEP_ATTN, l - 1, False))
 
+        poll(l, "start")
         with jax.named_scope("qkv"):
-            forward_qkv(k, l)
+            forward_qkv(k, l, lambda: poll(l, "qkv_half"))
         poll(l, "qkv")
         with jax.named_scope("attention"):
-            forward_windows(k, l)
+            forward_windows(k, l, lambda: poll(l, "windows_half"))
 
         @pl.when(l < LAYERS - 1)
         def _():
@@ -921,14 +1021,17 @@
         if alone:
             pltpu.make_async_copy(k.all_f.at[l], k.wf.at[l], k.load_sem.at[2 * l + 1]).wait()
         poll(l, "windows")
-        with jax.named_scope("ffn"):
-            forward_ffn(k, l, (l + 1) % 2 + l // 2, lambda: poll(l, "half"))
+        with jax.named_scope("ffn_up"):
+            forward_up(k, l, lambda: poll(l, "up_half"))
+        poll(l, "up")
+        with jax.named_scope("ffn_down"):
+            forward_down(k, l, (l + 1) % 2 + l // 2)
 
         @pl.when(l < LAYERS - 1)
         def _():
             start(kept(KEEP_FFN, l, False))
 
-        poll(l, "ffn")
+        poll(l, "down")
         return carry
 
     lax.fori_loop(0, LAYERS, forward, 0)
@@ -953,40 +1056,54 @@
         def _():
             wait(kept(KEEP_FFN, l, True))
 
-        finish = () if alone else (k.shard, k.squares_sum)
-
-        def ffn_between():
+        def now(name, part):
             if not alone:
-                behind("reduce_third", (reduce.third, 1, k.shard))
-
-        def attn_between():
+                with jax.named_scope("reduce_" + name):
+                    getattr(reduce, name)(l, part, *extra.get(name, ()))
+
+        def then(name, part):
             if not alone:
-                with jax.named_scope("reduce_first"):
-                    reduce.first(l, 1)
-                behind("reduce_last", (reduce.last, 1, *finish))
+
+                @pl.when(n > 0)
+                def _():
+                    with jax.named_scope("reduce_" + name):
+                        getattr(reduce, name)(l + 1, part, *extra.get(name, ()))
+
+        def in_ffn():
+            then("last", 2)
+
+        def in_windows():
+            now("second", 2)
+            then("last", 0)
 
         with jax.named_scope("ffn_back"):
-            backward_ffn(k, l, grad, ffn_between)
-        if not alone:
-            behind("reduce_second", (reduce.second, 0))
-        with jax.named_scope("ffn_grads"):
-            backward_ffn_grads(k, l)
+            backward_ffn(k, l, grad, in_ffn)
+        then("last", 1)
+        then("second", 0)
+        with jax.named_scope("down_grads"):
+            backward_down_grads(k, l)
+        now("start", 2)
+        then("third", 0)
+        with jax.named_scope("up_grads"):
+            backward_up_grads(k, l)
 
         @pl.when(n < LAYERS - 1)
         def _():
             start(kept(KEEP_FFN, l - 1, True))
 
-        if not alone:
-            with jax.named_scope("reduce_start"):
-                reduce.start(l, 1)
-            behind("reduce_third", (reduce.third, 0, k.shard))
+        now("start", 1)
+        now("first", 2)
 
         @pl.when(n > 0)
         def _():
             wait(kept(KEEP_ATTN, l, True))
 
+        with jax.named_scope("out_back"):
+            backward_out(k, l, grad)
+        now("first", 1)
         with jax.named_scope("attention_back"):
-            backward_attn(k, l, grad, attn_between)
+            backward_windows(k, l, in_windows)
+        now("third", 2)
         with jax.named_scope("qkv_grads"):
             backward_attn_grads(k, l)
 
@@ -994,10 +1111,8 @@
         def _():
             start(kept(KEEP_ATTN, l - 1, True))
 
-        if not alone:
-            with jax.named_scope("reduce_start"):
-                reduce.start(l, 0)
-            behind("reduce_last", (reduce.last, 0, *finish))
+        now("start", 0)
+        now("second", 1)
 
         @pl.when(n == LAYERS - 1)
         def _():
@@ -1010,13 +1125,11 @@
         def _():
             start(kept_x(True))
 
-        if not alone:
-            with jax.named_scope("reduce_second"):
-                reduce.second(l, 1)
-            with jax.named_scope("reduce_first"):
-                reduce.first(l, 0)
+        now("first", 0)
+        now("third", 1)
         return carry
 
+    extra = {} if alone else dict(third=(k.shard,), last=(k.shard, k.squares_sum))
     lax.fori_loop(0, LAYERS, backward, 0)
     if alone:
         start(stores)
@@ -1024,30 +1137,25 @@
         wait(stores)
         return
     with jax.named_scope("small_grads"):
-        small_stage(k, sums.own(0), grad)
+        small_stage(k, sums.whole(), grad)
     sums.start()
-    with jax.named_scope("reduce_third"):
-        reduce.third(0, 1, k.shard)
-    with jax.named_scope("reduce_second"):
+    with jax.named_scope("reduce_end"):
+        reduce.last(0, 2, k.shard, k.squares_sum)
         reduce.second(0, 0)
-    sums.step(0)
-    with jax.named_scope("reduce_third"):
+        sums.step(0)
         reduce.third(0, 0, k.shard)
-    sums.step(1)
-    with jax.named_scope("reduce_last"):
+        sums.step(1)
         reduce.last(0, 1, k.shard, k.squares_sum)
+        sums.step(2)
         reduce.last(0, 0, k.shard, k.squares_sum)
-    with jax.named_scope("norm_sums"):
-        norm.own(0)[...] = k.squares_sum[...]
-        norm.start()
-        sums.step(2)
-        norm.step(0)
-        norm.step(1)
-        k.small_out[...] = sums.last()
-        norm.step(2)
+    with jax.named_scope("norm"):
+        squares = k.squares_sum[...]
+        norm.start(sum(squares[:, n * 128 : (n + 1) * 128] for n in range(D // 128)))
+        sums.back()
+        norm.step()
+        sums.last()
+        k.small_out[...] = sums.whole()[...]
         k.squares[...] = norm.last()
-    sums.sent()
-    norm.sent()
 
 
 def train_pass(inputs, weights, alone):
@@ -1055,7 +1163,7 @@
     scalars = pl.BlockSpec(memory_space=pltpu.SMEM)
     anywhere = pl.BlockSpec(memory_space=pl.ANY)
     dma = pltpu.SemaphoreType.DMA
-    count = 2 * LAYERS
+    count = PARTS * LAYERS
     names = ["states", "actions", "returns", "starts", "repeats", "valid"]
     names += ["log_temp", "small", "head_bias"]
     out_shape = {"small_out": ((SMALL, D), WIDE)}
@@ -1073,19 +1181,21 @@
     else:
         names += ["qkv_w", "out_w", "up_w", "down_w"]
         out_shape["shard"] = ((LAYERS, PACK, D), WIDE)
-        out_shape["squares"] = ((8, D), WIDE)
-        for part, name in enumerate("af"):
-            for n, shape in enumerate(landing_shapes(PART[part])):
-                scratch["land_%s%d" % (name, n)] = pltpu.VMEM(shape, LOWER)
+        out_shape["squares"] = ((8, 128), WIDE)
+        for part in range(PARTS):
+            for n, shape in enumerate(LANDING):
+                scratch["land_%d_%d" % (part, n)] = pltpu.VMEM(shape, LOWER)
         scratch["stage_sem"] = dma((LAYERS, 9))
         scratch["squares_sum"] = pltpu.VMEM((8, D), WIDE)
         for name, copies in (("gather", Gather.COPIES), ("reduce", Reduce.COPIES)):
             scratch[name + "_send"] = dma((count, copies))
             scratch[name + "_recv"] = dma((count, copies))
-        scratch["credit"] = pltpu.SemaphoreType.REGULAR((2, 8))
-        for name in ("sum", "norm"):
-            scratch[name + "_send"] = dma((6,))
-            scratch[name + "_recv"] = dma((6,))
+        scratch["credit"] = pltpu.SemaphoreType.REGULAR((PARTS, 8))
+        scratch["norm_plane"] = pltpu.VMEM((8, 8, 128), WIDE)
+        scratch["norm_column"] = pltpu.VMEM((NZ, 8, 128), WIDE)
+        for name, copies in (("sum", Total.COPIES), ("norm", Norm.COPIES)):
+            scratch[name + "_send"] = dma((copies,))
+            scratch[name + "_recv"] = dma((copies,))
     spaces = dict.fromkeys(("starts", "repeats", "head_bias", "log_temp"), scalars)
     for name in ("all_a", "all_f", "grad_a", "grad_f", "qkv_w", "out_w", "up_w", "down_w"):
         spaces[name] = anywhere
@@ -1095,8 +1205,9 @@
 
     def kernel(*given):
         refs = dict(zip(every, given))
-        for name in "af":
-            refs["land_" + name] = [refs.get("land_%s%d" % (name, n)) for n in range(5)]
+        refs["landing"] = [
+            [refs.get("land_%d_%d" % (part, n)) for n in range(len(LANDING))] for part in range(PARTS)
+        ]
         train_kernel(refs, alone)
 
     results = pl.pallas_call(

time: 308 us -> 288 us (0.935)
  Pallas kernels: 307 us -> 286 us
    pallas_call x1, Pallas kernels: 299 us -> 279 us  [train_pass(): pl.pallas_call(kernel, name='train_pass', out_shape=tuple((jax.ShapeDtype...]
where the time goes in v7:
time: 288 us; the launch traced here: 287 us
  Pallas kernels  286 us (99%)
    pallas_call x1, Pallas kernels, train_pass(): pl.pallas_call(kernel, name='train_pass', out_shape=tuple((jax.ShapeDtype...  279 us
    pallas_call x1, Pallas kernels, adam_all(): pl.pallas_call(adam_kernel, name='adam', grid=(LAYERS,), out_shape=(jax.S...  7.18 us

profile of v7, /device:TPU:0, one launch (start us, length us, event | category | flops | bytes accessed | tf_op | source)
XLA Modules:
  0.0 287.3 jit_solution(4033915570645035302)
XLA Ops:
  1.3 278.6 %train_pass.1 = (f32[96,512]{1,0:T(8,128)}, bf16[2,1024,1536]{2,1,0:T(8,128)(2,1)}, bf16[2,512,1024]{2,1,0:T(8,128)(2,1)}, bf16[2,512,1024]{2,1,0:T(8,128)(2,1)}...) custom-call(f32[11,64]{1,0:T(8,128)} %bitcast.3, ...), custom_call_target="tpu_custom_call" | custom-call | flops 60000002048 | bytes 40000000 | tf_op jit(solution)/shard_map/train_pass/pallas_call | solution.py:1213
  280.0 7.2 %adam.1 = (f32[3]{0:T(128)}, f32[1]{0:T(128)}, f32[1]{0:T(128)}, f32[85,512]{1,0:T(8,128)}, f32[85,512]{1,0:T(8,128)}, /*index=5*/f32[85,512]{1,0:T(8,128)}, f32...) custom-call(f32[3,192,512]{2,1,0:T(8,128)} %get-tuple-element.28.ref, ...), custom_call_target="tpu_custom_call" | custom-call | flops 10000000 | bytes 8000000 | tf_op jit(solution)/shard_map/adam/pallas_call | solution.py:1333

commit v8 on v7

--- a/solution.py
+++ b/solution.py
@@ -261,20 +261,21 @@
     def window(w):
         rows = window_rows(w)
         bias = k.bias[rows, :]
-        scores = []
-        for p in range(H // 2):
-            at = p * 128
-            query = stack_pair(k.qkv[rows, at : at + 128] * jnp.asarray(HD**-0.5, LOWER), first)
-            scores.append(dot_nt(k.qkv[rows, D + at : D + at + 128], query) + bias)
-        for p in range(H // 2):
-            at = p * 128
-            peak = jnp.max(scores[p], 0, keepdims=True)
-            expo = jnp.exp(scores[p] - peak)
-            total = jnp.sum(expo, 0, keepdims=True)
-            probs = (expo * (1.0 / total)).astype(LOWER)
-            k.logs[l, w, p : p + 1, :] = peak + jnp.log(total)
-            out = dot_tn(probs, k.qkv[rows, 2 * D + at : 2 * D + at + 128])
-            k.left[rows, at : at + 128] = join_pair(out, first).astype(LOWER)
+        pairs = [slice(p * 128, (p + 1) * 128) for p in range(H // 2)]
+
+        def qkv(n, at):
+            return k.qkv[rows, n * D + at.start : n * D + at.stop]
+
+        scale = jnp.asarray(HD**-0.5, LOWER)
+        scores = [dot_nt(qkv(1, at), stack_pair(qkv(0, at) * scale, first)) + bias for at in pairs]
+        peaks = [jnp.max(s, 0, keepdims=True) for s in scores]
+        expos = [jnp.exp(s - peak) for s, peak in zip(scores, peaks)]
+        totals = [jnp.sum(e, 0, keepdims=True) for e in expos]
+        probs = [(e * (1.0 / total)).astype(LOWER) for e, total in zip(expos, totals)]
+        outs = [dot_tn(p, qkv(2, at)) for p, at in zip(probs, pairs)]
+        for p, at in enumerate(pairs):
+            k.logs[l, w, p : p + 1, :] = peaks[p] + jnp.log(totals[p])
+            k.left[rows, at] = join_pair(outs[p], first).astype(LOWER)
 
     def turn(rows):
         k.mixed_t[:, rows] = k.left[rows, :].T
@@ -419,22 +420,27 @@
     def window(w):
         rows = window_rows(w)
         bias = k.bias[rows, :]
-        for p in range(H // 2):
-            at = p * 128
-            query = stack_pair(k.qkv[rows, at : at + 128] * jnp.asarray(scale, LOWER), first)
-            keyed = k.qkv[rows, D + at : D + at + 128]
-            values = k.qkv[rows, 2 * D + at : 2 * D + at + 128]
-            d_mixed = stack_pair(k.dout[rows, at : at + 128], first)
-            probs = jnp.exp(dot_nt(keyed, query) + bias - k.logs[l, w, p : p + 1, :])
-            d_probs = dot_nt(values, d_mixed)
-            d_values = dot(probs.astype(LOWER), d_mixed)
-            inner = probs * d_probs
-            d_scores = (inner - probs * jnp.sum(inner, 0, keepdims=True)).astype(LOWER)
-            d_keyed = dot(d_scores, query)
-            d_query = join_pair(dot_tn(d_scores, keyed), first) * scale
-            k.work[rows, at : at + 128] = d_query.astype(LOWER)
-            k.work[rows, D + at : D + at + 128] = d_keyed.astype(LOWER)
-            k.work[rows, 2 * D + at : 2 * D + at + 128] = d_values.astype(LOWER)
+        pairs = [slice(p * 128, (p + 1) * 128) for p in range(H // 2)]
+
+        def qkv(n, at):
+            return k.qkv[rows, n * D + at.start : n * D + at.stop]
+
+        low = jnp.asarray(scale, LOWER)
+        query = [stack_pair(qkv(0, at) * low, first) for at in pairs]
+        d_mixed = [stack_pair(k.dout[rows, at], first) for at in pairs]
+        scores = [dot_nt(qkv(1, at), q) + bias for at, q in zip(pairs, query)]
+        d_probs = [dot_nt(qkv(2, at), d) for at, d in zip(pairs, d_mixed)]
+        probs = [jnp.exp(s - k.logs[l, w, p : p + 1, :]) for p, s in enumerate(scores)]
+        d_values = [dot(p.astype(LOWER), d) for p, d in zip(probs, d_mixed)]
+        inner = [p * d for p, d in zip(probs, d_probs)]
+        sums = [jnp.sum(i, 0, keepdims=True) for i in inner]
+        d_scores = [(i - p * t).astype(LOWER) for i, p, t in zip(inner, probs, sums)]
+        d_keyed = [dot(d, q) for d, q in zip(d_scores, query)]
+        d_query = [dot_tn(d, qkv(1, at)) for d, at in zip(d_scores, pairs)]
+        for p, at in enumerate(pairs):
+            values = (join_pair(d_query[p], first) * scale, d_keyed[p], d_values[p])
+            for n, value in enumerate(values):
+                k.work[rows, n * D + at.start : n * D + at.stop] = value.astype(LOWER)
 
     each_window(window, None, between)
 
@@ -875,29 +881,31 @@
     )
 
 
+BEGIN, SETUP, START, QKV_HALF, QKV, WINDOWS_HALF, WINDOWS, UP_HALF, UP, DOWN = range(10)
+FIRST, SECOND, THIRD, FOURTH, FIFTH, LAST, SEND = range(7)
 GATHER_PLAN = {
-    (-1, "begin"): [("first", 0, 0), ("first", 0, 1)],
-    (-1, "setup"): [("first", 0, 2), ("first", 1, 0), ("second", 0, 0)],
-    (0, "start"): [("second", 0, 1), ("first", 1, 1), ("third", 0, 0), ("fourth", 0, 0), ("second", 0, 2), ("first", 1, 2), ("third", 0, 1), ("fifth", 0, 0), ("last", 0, 0), ("second", 1, 0), ("fourth", 0, 1)],
-    (0, "qkv"): [("first", 2, 0), ("third", 0, 2), ("fifth", 0, 1)],
-    (0, "windows_half"): [("second", 1, 1), ("last", 0, 1)],
-    (0, "windows"): [("fourth", 0, 2)],
-    (0, "up_half"): [("first", 2, 1), ("third", 1, 0), ("fifth", 0, 2), ("second", 1, 2)],
-    (0, "up"): [("last", 0, 2), ("fourth", 1, 0), ("second", 2, 0)],
-    (0, "down"): [("first", 2, 2), ("third", 1, 1), ("fifth", 1, 0)],
-    (1, "start"): [("last", 1, 0), ("fourth", 1, 1)],
-    (1, "qkv_half"): [("second", 2, 1)],
-    (1, "qkv"): [("third", 1, 2), ("fifth", 1, 1)],
-    (1, "windows_half"): [("last", 1, 1)],
-    (1, "windows"): [("second", 2, 2), ("fourth", 1, 2)],
-    (1, "up_half"): [("third", 2, 0), ("fifth", 1, 2), ("last", 1, 2)],
-    (1, "up"): [("fourth", 2, 0)],
-    (1, "down"): [("third", 2, 1), ("fifth", 2, 0)],
-    (2, "start"): [("last", 2, 0), ("fourth", 2, 1)],
-    (2, "qkv"): [("third", 2, 2), ("fifth", 2, 1)],
-    (2, "windows_half"): [("last", 2, 1)],
-    (2, "windows"): [("fourth", 2, 2)],
-    (2, "up_half"): [("fifth", 2, 2), ("last", 2, 2)],
+    (-1, BEGIN): [(FIRST, 0, 0), (FIRST, 0, 1), (FIRST, 0, 2)],
+    (-1, SETUP): [(FIRST, 1, 0), (FIRST, 1, 1), (SECOND, 0, 0)],
+    (0, START): [(FIRST, 1, 2), (SECOND, 0, 1), (THIRD, 0, 0), (FOURTH, 0, 0), (SECOND, 0, 2), (THIRD, 0, 1), (FIFTH, 0, 0), (LAST, 0, 0), (SECOND, 1, 0), (FOURTH, 0, 1)],
+    (0, QKV): [(FIRST, 2, 0), (THIRD, 0, 2), (FIFTH, 0, 1)],
+    (0, WINDOWS_HALF): [(SECOND, 1, 1), (LAST, 0, 1)],
+    (0, WINDOWS): [(FIRST, 2, 1), (FOURTH, 0, 2)],
+    (0, UP_HALF): [(THIRD, 1, 0), (FIFTH, 0, 2), (SECOND, 1, 2)],
+    (0, UP): [(FIRST, 2, 2), (LAST, 0, 2), (FOURTH, 1, 0), (SECOND, 2, 0)],
+    (0, DOWN): [(THIRD, 1, 1), (FIFTH, 1, 0)],
+    (1, START): [(LAST, 1, 0), (FOURTH, 1, 1)],
+    (1, QKV_HALF): [(SECOND, 2, 1)],
+    (1, QKV): [(THIRD, 1, 2), (FIFTH, 1, 1)],
+    (1, WINDOWS_HALF): [(LAST, 1, 1)],
+    (1, WINDOWS): [(SECOND, 2, 2), (FOURTH, 1, 2)],
+    (1, UP_HALF): [(THIRD, 2, 0), (FIFTH, 1, 2), (LAST, 1, 2)],
+    (1, UP): [(FOURTH, 2, 0)],
+    (1, DOWN): [(THIRD, 2, 1), (FIFTH, 2, 0)],
+    (2, START): [(LAST, 2, 0), (FOURTH, 2, 1)],
+    (2, QKV): [(THIRD, 2, 2), (FIFTH, 2, 1)],
+    (2, WINDOWS_HALF): [(LAST, 2, 1)],
+    (2, WINDOWS): [(FOURTH, 2, 2)],
+    (2, UP_HALF): [(FIFTH, 2, 2), (LAST, 2, 2)],
 }
 
 
@@ -950,8 +958,16 @@
         norm = Norm(place, k.norm_plane, k.norm_column, k.norm_send, k.norm_recv)
 
     def run(plan):
+        stages = (
+            gather.first,
+            gather.second,
+            gather.third,
+            gather.fourth,
+            gather.fifth,
+            gather.last,
+        )
         for stage, l, part in plan:
-            getattr(gather, stage)(l, part)
+            stages[stage](l, part)
 
     def poll(l, point):
         if alone:
@@ -962,8 +978,7 @@
 
                 @pl.when(l == layer)
                 def _(plan=plan):
-                    with jax.named_scope("gather_" + point):
-                        run(plan)
+                    run(plan)
 
     if not alone:
         staged = []
@@ -980,16 +995,14 @@
                 array, first = part_ref(weights, part)
                 mine = k.xs[2, row + DEEP * part : row + DEEP * (part + 1), :].astype(LOWER)
                 array[l, place.a, place.b, first : first + DEEP, :] = mine
-                if ("first", l, part) in GATHER_PLAN[-1, "begin"]:
+                if (FIRST, l, part) in GATHER_PLAN[-1, BEGIN]:
                     gather.first(l, part)
         k.squares_sum[...] = jnp.zeros_like(k.squares_sum)
 
-    with jax.named_scope("embedding"):
-        setup_stage(k)
+    setup_stage(k)
     start(kept_x(False))
     if not alone:
-        with jax.named_scope("gather_setup"):
-            run(GATHER_PLAN[-1, "setup"])
+        run(GATHER_PLAN[-1, SETUP])
 
     def forward(l, carry):
         if alone:
@@ -999,12 +1012,10 @@
         def _():
             wait(kept(KEEP_ATTN, l - 1, False))
 
-        poll(l, "start")
-        with jax.named_scope("qkv"):
-            forward_qkv(k, l, lambda: poll(l, "qkv_half"))
-        poll(l, "qkv")
-        with jax.named_scope("attention"):
-            forward_windows(k, l, lambda: poll(l, "windows_half"))
+        poll(l, START)
+        forward_qkv(k, l, lambda: poll(l, QKV_HALF))
+        poll(l, QKV)
+        forward_windows(k, l, lambda: poll(l, WINDOWS_HALF))
 
         @pl.when(l < LAYERS - 1)
         def _():
@@ -1020,18 +1031,16 @@
 
         if alone:
             pltpu.make_async_copy(k.all_f.at[l], k.wf.at[l], k.load_sem.at[2 * l + 1]).wait()
-        poll(l, "windows")
-        with jax.named_scope("ffn_up"):
-            forward_up(k, l, lambda: poll(l, "up_half"))
-        poll(l, "up")
-        with jax.named_scope("ffn_down"):
-            forward_down(k, l, (l + 1) % 2 + l // 2)
+        poll(l, WINDOWS)
+        forward_up(k, l, lambda: poll(l, UP_HALF))
+        poll(l, UP)
+        forward_down(k, l, (l + 1) % 2 + l // 2)
 
         @pl.when(l < LAYERS - 1)
         def _():
             start(kept(KEEP_FFN, l, False))
 
-        poll(l, "down")
+        poll(l, DOWN)
         return carry
 
     lax.fori_loop(0, LAYERS, forward, 0)
@@ -1039,8 +1048,15 @@
         for l, part in parts:
             gather.sent(l, part)
     grad = 2
-    with jax.named_scope("head"):
-        head_stage(k, grad)
+    head_stage(k, grad)
+
+    def run_reduce(stage, l, part):
+        if stage == THIRD:
+            reduce.third(l, part, k.shard)
+        elif stage == LAST:
+            reduce.last(l, part, k.shard, k.squares_sum)
+        else:
+            {SEND: reduce.start, FIRST: reduce.first, SECOND: reduce.second}[stage](l, part)
 
     def backward(n, carry):
         l = LAYERS - 1 - n
@@ -1048,114 +1064,100 @@
         def behind(name, *stages):
             @pl.when(n > 0)
             def _():
-                with jax.named_scope(name):
-                    for stage, part, *more in stages:
-                        stage(l + 1, part, *more)
+                for stage, part, *more in stages:
+                    stage(l + 1, part, *more)
 
         @pl.when(n > 0)
         def _():
             wait(kept(KEEP_FFN, l, True))
 
-        def now(name, part):
+        def now(stage, part):
             if not alone:
-                with jax.named_scope("reduce_" + name):
-                    getattr(reduce, name)(l, part, *extra.get(name, ()))
-
-        def then(name, part):
+                run_reduce(stage, l, part)
+
+        def then(stage, part):
             if not alone:
 
                 @pl.when(n > 0)
                 def _():
-                    with jax.named_scope("reduce_" + name):
-                        getattr(reduce, name)(l + 1, part, *extra.get(name, ()))
+                    run_reduce(stage, l + 1, part)
 
         def in_ffn():
-            then("last", 2)
+            then(LAST, 2)
 
         def in_windows():
-            now("second", 2)
-            then("last", 0)
-
-        with jax.named_scope("ffn_back"):
-            backward_ffn(k, l, grad, in_ffn)
-        then("last", 1)
-        then("second", 0)
-        with jax.named_scope("down_grads"):
-            backward_down_grads(k, l)
-        now("start", 2)
-        then("third", 0)
-        with jax.named_scope("up_grads"):
-            backward_up_grads(k, l)
+            now(SECOND, 2)
+            then(LAST, 0)
+
+        backward_ffn(k, l, grad, in_ffn)
+        then(LAST, 1)
+        then(SECOND, 0)
+        backward_down_grads(k, l)
+        now(SEND, 2)
+        then(THIRD, 0)
+        backward_up_grads(k, l)
 
         @pl.when(n < LAYERS - 1)
         def _():
             start(kept(KEEP_FFN, l - 1, True))
 
-        now("start", 1)
-        now("first", 2)
+        now(SEND, 1)
+        now(FIRST, 2)
 
         @pl.when(n > 0)
         def _():
             wait(kept(KEEP_ATTN, l, True))
 
-        with jax.named_scope("out_back"):
-            backward_out(k, l, grad)
-        now("first", 1)
-        with jax.named_scope("attention_back"):
-            backward_windows(k, l, in_windows)
-        now("third", 2)
-        with jax.named_scope("qkv_grads"):
-            backward_attn_grads(k, l)
+        backward_out(k, l, grad)
+        now(FIRST, 1)
+        backward_windows(k, l, in_windows)
+        now(THIRD, 2)
+        backward_attn_grads(k, l)
 
         @pl.when(n < LAYERS - 1)
         def _():
             start(kept(KEEP_ATTN, l - 1, True))
 
-        now("start", 0)
-        now("second", 1)
+        now(SEND, 0)
+        now(SECOND, 1)
 
         @pl.when(n == LAYERS - 1)
         def _():
             wait(kept_x(True))
 
-        with jax.named_scope("qkv_back"):
-            backward_input(k, l, grad)
+        backward_input(k, l, grad)
 
         @pl.when(n == 0)
         def _():
             start(kept_x(True))
 
-        now("first", 0)
-        now("third", 1)
+        now(FIRST, 0)
+        now(THIRD, 1)
         return carry
 
-    extra = {} if alone else dict(third=(k.shard,), last=(k.shard, k.squares_sum))
     lax.fori_loop(0, LAYERS, backward, 0)
     if alone:
         start(stores)
         small_stage(k, k.small_out, grad)
         wait(stores)
         return
-    with jax.named_scope("small_grads"):
-        small_stage(k, sums.whole(), grad)
+    small_stage(k, sums.whole(), grad)
     sums.start()
-    with jax.named_scope("reduce_end"):
-        reduce.last(0, 2, k.shard, k.squares_sum)
-        reduce.second(0, 0)
-        sums.step(0)
-        reduce.third(0, 0, k.shard)
-        sums.step(1)
-        reduce.last(0, 1, k.shard, k.squares_sum)
-        sums.step(2)
-        reduce.last(0, 0, k.shard, k.squares_sum)
-    with jax.named_scope("norm"):
-        squares = k.squares_sum[...]
-        norm.start(sum(squares[:, n * 128 : (n + 1) * 128] for n in range(D // 128)))
-        sums.back()
-        norm.step()
-        sums.last()
-        k.small_out[...] = sums.whole()[...]
-        k.squares[...] = norm.last()
+    reduce.last(0, 2, k.shard, k.squares_sum)
+    reduce.second(0, 0)
+    sums.step(0)
+    reduce.third(0, 0, k.shard)
+    sums.step(1)
+    reduce.last(0, 1, k.shard, k.squares_sum)
+    sums.step(2)
+    reduce.last(0, 0, k.shard, k.squares_sum)
+    squares = k.squares_sum[...]
+    norm.start(sum(squares[:, n * 128 : (n + 1) * 128] for n in range(D // 128)))
+    sums.back()
+    norm.step()
+    sums.last()
+    k.small_out[...] = sums.whole()[...]
+    k.squares[...] = norm.last()
 
 
 def train_pass(inputs, weights, alone):
@@ -1235,7 +1237,7 @@
     fix_one = 1.0 - BETA_ONE**STEP
     fix_two = 1.0 - BETA_TWO**STEP
     fresh = weight - rate * (
-        first / fix_one / (jnp.sqrt(second / fix_two) + ADAM_EPS) + DECAY * weight
+        first * (1.0 / fix_one) / (jnp.sqrt(second * (1.0 / fix_two)) + ADAM_EPS) + DECAY * weight
     )
     return fresh, first, second
 
@@ -1246,7 +1248,6 @@
     mats, firsts, seconds = refs[11:15], refs[15:19], refs[19:23]
     totals, norm, next_temp, s_next, s_first, s_second, b_next, b_first, b_second = refs[23:32]
     m_next, m_copy, m_first, m_second = refs[32:36], refs[36:40], refs[40:44], refs[44:48]
-    l = pl.program_id(0)
     extra = small_grad[NROWS : NROWS + 3, 0:128]
     lane = iota((1, 128), 1)
     bias_mean = jnp.where(lane < A, extra[1:2], 0.0)
@@ -1265,14 +1266,14 @@
     length = jnp.sqrt(square)
     clip = jnp.minimum(1.0, CLIP / (length + 1e-06))
 
-    def rate_of(kind):
+    def rate_of(l, kind):
         group = jnp.full((1, 1), groups[l, kind], jnp.int32).astype(WIDE)
         return LEARN * jnp.exp2(-group)
 
-    def update(kind, rows, cols, grad):
-        at = (0, rows, cols)
+    def update(l, kind, rows, cols, grad):
+        at = (l, rows, cols)
         fresh, first, second = adam_parts(
-            mats[kind][at], clip * grad, firsts[kind][at], seconds[kind][at], rate_of(kind)
+            mats[kind][at], clip * grad, firsts[kind][at], seconds[kind][at], rate_of(l, kind)
         )
         m_next[kind][at] = fresh
         m_copy[kind][at] = fresh.astype(LOWER)
@@ -1280,50 +1281,46 @@
         m_second[kind][at] = second
 
     every = slice(0, 16)
-    for j in range(3):
-        update(0, every, slice(j * D, (j + 1) * D), shard[0, 16 * j : 16 * j + 16, :])
-    update(1, every, slice(0, D), shard[0, 48:64, :])
-    for j in range(4):
-        update(2, every, slice(j * D, (j + 1) * D), shard[0, 64 + 16 * j : 80 + 16 * j, :])
-    update(3, slice(0, 64), slice(0, D), shard[0, 128:192, :])
-
-    @pl.when(l == 0)
-    def _():
-        s_next[...], s_first[...], s_second[...] = adam_parts(
-            small[...], clip * grads, small_first[...], small_second[...], LEARN
-        )
-
-        def scalar(v, n):
-            return jnp.sum(jnp.where(lane == n, v, 0.0))
-
-        def row(ref):
-            v = jnp.zeros((1, 128), WIDE)
-            for n in range(2 * A):
-                v = jnp.where(lane == n, ref[n], v)
-            return v
-
-        grad = bias_mean + pltpu.roll(bias_spread, A, 1)
-        results = adam_parts(row(bias), clip * grad, row(bias_first), row(bias_second), LEARN)
-        for ref, result in zip((b_next, b_first, b_second), results):
-            for n in range(2 * A):
-                ref[n] = scalar(result, n)
-        sums = extra[0:1]
-        for n in range(3):
-            totals[n] = scalar(sums, n)
-        norm[0] = jnp.sum(length)
-        logs = jnp.full((1, 1), log_temp[0], WIDE)
-        ratio = jnp.full((1, 1), scalar(sums, 1), WIDE) / jnp.full((1, 1), scalar(sums, 2), WIDE)
-        next_temp[0] = jnp.sum(logs - TEMP_RATE * jnp.exp(logs) * (ratio + A))
+    for l in range(LAYERS):
+        for j in range(3):
+            update(l, 0, every, slice(j * D, (j + 1) * D), shard[l, 16 * j : 16 * j + 16, :])
+        update(l, 1, every, slice(0, D), shard[l, 48:64, :])
+        for j in range(4):
+            rows = slice(64 + 16 * j, 80 + 16 * j)
+            update(l, 2, every, slice(j * D, (j + 1) * D), shard[l, rows, :])
+        update(l, 3, slice(0, 64), slice(0, D), shard[l, 128:192, :])
+
+    s_next[...], s_first[...], s_second[...] = adam_parts(
+        small[...], clip * grads, small_first[...], small_second[...], LEARN
+    )
+
+    def scalar(v, n):
+        return jnp.sum(jnp.where(lane == n, v, 0.0))
+
+    def row(ref):
+        v = jnp.zeros((1, 128), WIDE)
+        for n in range(2 * A):
+            v = jnp.where(lane == n, ref[n], v)
+        return v
+
+    grad = bias_mean + pltpu.roll(bias_spread, A, 1)
+    results = adam_parts(row(bias), clip * grad, row(bias_first), row(bias_second), LEARN)
+    for ref, result in zip((b_next, b_first, b_second), results):
+        for n in range(2 * A):
+            ref[n] = scalar(result, n)
+    sums = extra[0:1]
+    for n in range(3):
+        totals[n] = scalar(sums, n)
+    norm[0] = jnp.sum(length)
+    logs = jnp.full((1, 1), log_temp[0], WIDE)
+    ratio = jnp.full((1, 1), scalar(sums, 1), WIDE) / jnp.full((1, 1), scalar(sums, 2), WIDE)
+    next_temp[0] = jnp.sum(logs - TEMP_RATE * jnp.exp(logs) * (ratio + A))
 
 
 def adam_all(shard, small_grad, squares, groups, log_temp, smalls, biases, mats, firsts, seconds):
     scalars = pl.BlockSpec(memory_space=pltpu.SMEM)
 
-    def fixed(array):
-        return pl.BlockSpec(array.shape, lambda l: (0,) * array.ndim)
-
-    def layer(array):
-        return pl.BlockSpec((1,) + array.shape[1:], lambda l: (l, 0, 0))
+    whole = pl.BlockSpec(memory_space=pltpu.VMEM)
 
     def like(array, dtype=WIDE):
         return jax.ShapeDtypeStruct(array.shape, dtype)
@@ -1333,7 +1330,6 @@
     return pl.pallas_call(
         adam_kernel,
         name="adam",
-        grid=(LAYERS,),
         out_shape=(
             (jax.ShapeDtypeStruct((3,), WIDE),)
             + (jax.ShapeDtypeStruct((1,), WIDE),) * 2
@@ -1343,14 +1339,8 @@
             + tuple(like(m, LOWER) for m in mats)
             + tuple(like(m) for m in mats) * 2
         ),
-        in_specs=[layer(shard), fixed(small_grad), fixed(squares), scalars, scalars]
-        + [fixed(small)] * 3
-        + [scalars] * 3
-        + [layer(m) for m in stacks],
-        out_specs=(scalars,) * 3
-        + (fixed(small),) * 3
-        + (scalars,) * 3
-        + tuple(layer(m) for m in mats) * 4,
+        in_specs=[whole] * 3 + [scalars] * 2 + [whole] * 3 + [scalars] * 3 + [whole] * 12,
+        out_specs=(scalars,) * 3 + (whole,) * 3 + (scalars,) * 3 + (whole,) * 16,
         compiler_params=pltpu.CompilerParams(vmem_limit_bytes=VMEM_BYTES),
         cost_estimate=pl.CostEstimate(flops=10**7, bytes_accessed=8 * 10**6, transcendentals=10**6),
     )(shard, small_grad, squares, groups, log_temp, *smalls, *biases, *stacks)

time: 288 us -> 272 us (0.944)
  Pallas kernels: 286 us -> 270 us
    pallas_call x1, Pallas kernels: 279 us -> 264 us  [train_pass(): pl.pallas_call(kernel, name='train_pass', out_shape=tuple((jax.ShapeDtype...]
where the time goes in v8:
time: 272 us
  Pallas kernels  270 us (99%)
    pallas_call x1, Pallas kernels, train_pass(): pl.pallas_call(kernel, name='train_pass', out_shape=tuple((jax.ShapeDtype...  264 us
    pallas_call x1, Pallas kernels, adam_all(): pl.pallas_call(adam_kernel, name='adam', out_shape=(jax.ShapeDtypeStruct(...  6.06 us

profile of v8, /device:TPU:0, one launch (start us, length us, event | category | flops | bytes accessed | tf_op | source)
XLA Modules:
  0.0 271.9 jit_solution(14216771614192248466)
XLA Ops:
  1.3 264.4 %train_pass.1 = (f32[96,512]{1,0:T(8,128)}, bf16[2,1024,1536]{2,1,0:T(8,128)(2,1)}, bf16[2,512,1024]{2,1,0:T(8,128)(2,1)}, bf16[2,512,1024]{2,1,0:T(8,128)(2,1)}...) custom-call(f32[11,64]{1,0:T(8,128)} %bitcast.3, ...), custom_call_target="tpu_custom_call" | custom-call | flops 60000002048 | bytes 40000000 | tf_op jit(solution)/shard_map/train_pass/pallas_call | solution.py:1215
  265.7 6.1 %adam.1 = (f32[3]{0:T(128)}, f32[1]{0:T(128)}, f32[1]{0:T(128)}, f32[85,512]{1,0:T(8,128)}, f32[85,512]{1,0:T(8,128)}, /*index=5*/f32[85,512]{1,0:T(8,128)}, f32...) custom-call(f32[3,192,512]{2,1,0:T(8,128)} %get-tuple-element.28.ref, ...), custom_call_target="tpu_custom_call" | custom-call | flops 10000000 | bytes 8000000 | tf_op jit(solution)/shard_map/adam/pallas_call | solution.py:1330

commit v9 on v8

--- a/solution.py
+++ b/solution.py
@@ -226,18 +226,20 @@
     lax.fori_loop(0, CHUNKS, step, 0)
 
 
-def each_window(body, after=None, between=None):
+def each_pair(body, between=None):
     def pair(n, carry):
-        body(2 * n)
-        body(2 * n + 1)
+        chains = [
+            (2 * n + w, window_rows(2 * n + w), slice(p * 128, (p + 1) * 128))
+            for w in range(2)
+            for p in range(H // 2)
+        ]
+        body(pl.ds(pl.multiple_of(n * 128, 128), 128), chains)
         if between is not None:
 
             @pl.when(n == WINS // 4 - 1)
             def _():
                 between()
 
-        if after is not None:
-            after(pl.ds(pl.multiple_of(n * 128, 128), 128))
         return carry
 
     lax.fori_loop(0, WINS // 2, pair, 0)
@@ -255,32 +257,32 @@
     each_chunk(chunk, between)
 
 
+def qkv_part(k, n, rows, at):
+    return k.qkv[rows, n * D + at.start : n * D + at.stop]
+
+
 def forward_windows(k, l, between):
     first = iota((SLOT, 128), 1) < HD
-
-    def window(w):
-        rows = window_rows(w)
-        bias = k.bias[rows, :]
-        pairs = [slice(p * 128, (p + 1) * 128) for p in range(H // 2)]
-
-        def qkv(n, at):
-            return k.qkv[rows, n * D + at.start : n * D + at.stop]
-
-        scale = jnp.asarray(HD**-0.5, LOWER)
-        scores = [dot_nt(qkv(1, at), stack_pair(qkv(0, at) * scale, first)) + bias for at in pairs]
+    scale = jnp.asarray(HD**-0.5, LOWER)
+
+    def pair(both, chains):
+        query = [stack_pair(qkv_part(k, 0, rows, at) * scale, first) for _, rows, at in chains]
+        scores = [
+            dot_nt(qkv_part(k, 1, rows, at), q) + k.bias[rows, :]
+            for q, (_, rows, at) in zip(query, chains)
+        ]
         peaks = [jnp.max(s, 0, keepdims=True) for s in scores]
         expos = [jnp.exp(s - peak) for s, peak in zip(scores, peaks)]
         totals = [jnp.sum(e, 0, keepdims=True) for e in expos]
         probs = [(e * (1.0 / total)).astype(LOWER) for e, total in zip(expos, totals)]
-        outs = [dot_tn(p, qkv(2, at)) for p, at in zip(probs, pairs)]
-        for p, at in enumerate(pairs):
-            k.logs[l, w, p : p + 1, :] = peaks[p] + jnp.log(totals[p])
-            k.left[rows, at] = join_pair(outs[p], first).astype(LOWER)
-
-    def turn(rows):
-        k.mixed_t[:, rows] = k.left[rows, :].T
-
-    each_window(window, turn, between)
+        outs = [dot_tn(p, qkv_part(k, 2, rows, at)) for p, (_, rows, at) in zip(probs, chains)]
+        for peak, total, out, (w, rows, at) in zip(peaks, totals, outs, chains):
+            p = at.start // 128
+            k.logs[l, w, p : p + 1, :] = peak + jnp.log(total)
+            k.left[rows, at] = join_pair(out, first).astype(LOWER)
+        k.mixed_t[:, both] = k.left[both, :].T
+
+    each_pair(pair, between)
 
 
 def forward_up(k, l, between):
@@ -290,9 +292,12 @@
         xhat, _ = norm_parts(mid)
         second = (xhat * k.row(l, 2) + k.row(l, 3)).astype(LOWER)
         k.second_t[:, rows] = second.T
+        ahead = dot(second, k.w_up(l, 0))
         for j in range(4):
             cols = slice(j * D, (j + 1) * D)
-            h = dot(second, k.w_up(l, j)) + k.row(l, 8 + j)
+            h = ahead + k.row(l, 8 + j)
+            if j < 3:
+                ahead = dot(second, k.w_up(l, j + 1))
             square = h * h
             over = 1.0 + jnp.tanh(h * (GELU_C + GELU_C * GELU_A * square))
             half = 0.5 * h
@@ -375,9 +380,12 @@
         k.dout[rows, :] = d_down
         k.sgl[l, 12:13, :] += col_sum(d_down.astype(WIDE))
         d_second = jnp.zeros((CHUNK, D), WIDE)
+        ahead = dot_nt(d_down, k.w_down(l, 0))
         for j in range(4):
             cols = slice(j * D, (j + 1) * D)
-            d_acted = dot_nt(d_down, k.w_down(l, j))
+            d_acted = ahead
+            if j < 3:
+                ahead = dot_nt(d_down, k.w_down(l, j + 1))
             d_hidden = (d_acted * k.slope[rows, cols].astype(WIDE)).astype(LOWER)
             k.work[rows, cols] = d_hidden
             k.sgl[l, 8 + j : 9 + j, :] += col_sum(d_hidden.astype(WIDE))
@@ -416,33 +424,30 @@
 def backward_windows(k, l, between):
     first = iota((SLOT, 128), 1) < HD
     scale = HD**-0.5
-
-    def window(w):
-        rows = window_rows(w)
-        bias = k.bias[rows, :]
-        pairs = [slice(p * 128, (p + 1) * 128) for p in range(H // 2)]
-
-        def qkv(n, at):
-            return k.qkv[rows, n * D + at.start : n * D + at.stop]
-
-        low = jnp.asarray(scale, LOWER)
-        query = [stack_pair(qkv(0, at) * low, first) for at in pairs]
-        d_mixed = [stack_pair(k.dout[rows, at], first) for at in pairs]
-        scores = [dot_nt(qkv(1, at), q) + bias for at, q in zip(pairs, query)]
-        d_probs = [dot_nt(qkv(2, at), d) for at, d in zip(pairs, d_mixed)]
-        probs = [jnp.exp(s - k.logs[l, w, p : p + 1, :]) for p, s in enumerate(scores)]
+    low = jnp.asarray(scale, LOWER)
+
+    def pair(both, chains):
+        query = [stack_pair(qkv_part(k, 0, rows, at) * low, first) for _, rows, at in chains]
+        d_mixed = [stack_pair(k.dout[rows, at], first) for _, rows, at in chains]
+        shift = [
+            k.bias[rows, :] - k.logs[l, w, at.start // 128 : at.start // 128 + 1, :]
+            for w, rows, at in chains
+        ]
+        scores = [dot_nt(qkv_part(k, 1, rows, at), q) for q, (_, rows, at) in zip(query, chains)]
+        d_probs = [dot_nt(qkv_part(k, 2, rows, at), d) for d, (_, rows, at) in zip(d_mixed, chains)]
+        probs = [jnp.exp(s + more) for s, more in zip(scores, shift)]
         d_values = [dot(p.astype(LOWER), d) for p, d in zip(probs, d_mixed)]
         inner = [p * d for p, d in zip(probs, d_probs)]
         sums = [jnp.sum(i, 0, keepdims=True) for i in inner]
         d_scores = [(i - p * t).astype(LOWER) for i, p, t in zip(inner, probs, sums)]
         d_keyed = [dot(d, q) for d, q in zip(d_scores, query)]
-        d_query = [dot_tn(d, qkv(1, at)) for d, at in zip(d_scores, pairs)]
-        for p, at in enumerate(pairs):
-            values = (join_pair(d_query[p], first) * scale, d_keyed[p], d_values[p])
-            for n, value in enumerate(values):
-                k.work[rows, n * D + at.start : n * D + at.stop] = value.astype(LOWER)
-
-    each_window(window, None, between)
+        d_query = [dot_tn(d, qkv_part(k, 1, rows, at)) for d, (_, rows, at) in zip(d_scores, chains)]
+        for n, (_, rows, at) in enumerate(chains):
+            values = (join_pair(d_query[n], first) * scale, d_keyed[n], d_values[n])
+            for m, value in enumerate(values):
+                k.work[rows, m * D + at.start : m * D + at.stop] = value.astype(LOWER)
+
+    each_pair(pair, between)
 
 
 def backward_attn_grads(k, l):

time: 272 us -> 269 us (0.989)
  Pallas kernels: 270 us -> 267 us
    pallas_call x1, Pallas kernels: 264 us -> 261 us  [train_pass(): pl.pallas_call(kernel, name='train_pass', out_shape=tuple((jax.ShapeDtype...]
where the time goes in v9:
time: 269 us; the launch traced here: 268 us
  Pallas kernels  267 us (99%)
    pallas_call x1, Pallas kernels, train_pass(): pl.pallas_call(kernel, name='train_pass', out_shape=tuple((jax.ShapeDtype...  261 us
    pallas_call x1, Pallas kernels, adam_all(): pl.pallas_call(adam_kernel, name='adam', out_shape=(jax.ShapeDtypeStruct(...  6.06 us

profile of v9, /device:TPU:0, one launch (start us, length us, event | category | flops | bytes accessed | tf_op | source)
XLA Modules:
  0.0 268.5 jit_solution(15048907312053333778)
XLA Ops:
  1.3 260.9 %train_pass.1 = (f32[96,512]{1,0:T(8,128)}, bf16[2,1024,1536]{2,1,0:T(8,128)(2,1)}, bf16[2,512,1024]{2,1,0:T(8,128)(2,1)}, bf16[2,512,1024]{2,1,0:T(8,128)(2,1)}...) custom-call(f32[11,64]{1,0:T(8,128)} %bitcast.3, ...), custom_call_target="tpu_custom_call" | custom-call | flops 60000002048 | bytes 40000000 | tf_op jit(solution)/shard_map/train_pass/pallas_call | solution.py:1220
  262.2 6.1 %adam.1 = (f32[3]{0:T(128)}, f32[1]{0:T(128)}, f32[1]{0:T(128)}, f32[85,512]{1,0:T(8,128)}, f32[85,512]{1,0:T(8,128)}, /*index=5*/f32[85,512]{1,0:T(8,128)}, f32...) custom-call(f32[3,192,512]{2,1,0:T(8,128)} %get-tuple-element.28.ref, ...), custom_call_target="tpu_custom_call" | custom-call | flops 10000000 | bytes 8000000 | tf_op jit(solution)/shard_map/adam/pallas_call | solution.py:1335

commit v10 on v9

--- a/solution.py
+++ b/solution.py
@@ -681,22 +681,15 @@
         top, low = pl.ds(0, half), pl.ds(half, half)
         self.copy(l, part, 0).wait_recv()
 
-        def along_x(n, carry):
-            x = 1 - at.x
-            total = g[2 * at.c + x, n, top].astype(WIDE) + r0[x, n, top].astype(WIDE)
-            r0[x, n, top] = total.astype(LOWER)
-            return carry
-
-        def along_y(n, carry):
-            x, b = n // 4, 4 * (1 - at.y) + n % 4
-            total = g[2 * at.c + x, b, low].astype(WIDE) + r0[x, b, low].astype(WIDE)
-            r0[x, b, low] = total.astype(LOWER)
-            return carry
-
-        lax.fori_loop(0, 8, along_x, 0)
+        x = 1 - at.x
+        total = g[2 * at.c + x, :, top].astype(WIDE) + r0[x, :, top].astype(WIDE)
+        r0[x, :, top] = total.astype(LOWER)
         self.may_send(l, part, 1, 2)
         self.copy(l, part, 1).start()
-        lax.fori_loop(0, 8, along_y, 0)
+        other = pl.ds(4 * (1 - at.y), 4)
+        for x in range(NX):
+            total = g[2 * at.c + x, other, low].astype(WIDE) + r0[x, other, low].astype(WIDE)
+            r0[x, other, low] = total.astype(LOWER)
         self.copy(l, part, 2).start()
 
     def second(self, l, part):
@@ -704,24 +697,15 @@
         g, r0, r1a, r1b, _, _ = self.refs(l, part)
         top, low = pl.ds(0, half), pl.ds(half, half)
 
-        def along_y(n, carry):
-            b = 4 * (1 - at.y) + n
-            total = g[at.a, b, top].astype(WIDE) + r0[at.x, b, top].astype(WIDE)
-            r1a[b] = (total + r1a[b].astype(WIDE)).astype(LOWER)
-            return carry
-
-        def along_x(n, carry):
-            x, b = 1 - at.x, 4 * at.y + n
-            total = g[2 * at.c + x, b, low].astype(WIDE) + r0[x, b, low].astype(WIDE)
-            r1b[x, n] = (total + r1b[x, n].astype(WIDE)).astype(LOWER)
-            return carry
-
+        x, other, column = 1 - at.x, pl.ds(4 * (1 - at.y), 4), pl.ds(4 * at.y, 4)
         self.copy(l, part, 1).wait_recv()
-        lax.fori_loop(0, NZ, along_y, 0)
+        total = g[at.a, other, top].astype(WIDE) + r0[at.x, other, top].astype(WIDE)
+        r1a[other] = (total + r1a[other].astype(WIDE)).astype(LOWER)
         self.may_send(l, part, 6, 7)
         self.copy(l, part, 3).start()
         self.copy(l, part, 2).wait_recv()
-        lax.fori_loop(0, NZ, along_x, 0)
+        total = g[2 * at.c + x, column, low].astype(WIDE) + r0[x, column, low].astype(WIDE)
+        r1b[x] = (total + r1b[x].astype(WIDE)).astype(LOWER)
         self.copy(l, part, 4).start()
 
     def chip_sums(self, l, part, z):
@@ -891,7 +875,8 @@
 GATHER_PLAN = {
     (-1, BEGIN): [(FIRST, 0, 0), (FIRST, 0, 1), (FIRST, 0, 2)],
     (-1, SETUP): [(FIRST, 1, 0), (FIRST, 1, 1), (SECOND, 0, 0)],
-    (0, START): [(FIRST, 1, 2), (SECOND, 0, 1), (THIRD, 0, 0), (FOURTH, 0, 0), (SECOND, 0, 2), (THIRD, 0, 1), (FIFTH, 0, 0), (LAST, 0, 0), (SECOND, 1, 0), (FOURTH, 0, 1)],
+    (0, START): [(FIRST, 1, 2), (SECOND, 0, 1), (THIRD, 0, 0), (FOURTH, 0, 0), (SECOND, 0, 2), (THIRD, 0, 1), (FIFTH, 0, 0), (LAST, 0, 0)],
+    (0, QKV_HALF): [(SECOND, 1, 0), (FOURTH, 0, 1)],
     (0, QKV): [(FIRST, 2, 0), (THIRD, 0, 2), (FIFTH, 0, 1)],
     (0, WINDOWS_HALF): [(SECOND, 1, 1), (LAST, 0, 1)],
     (0, WINDOWS): [(FIRST, 2, 1), (FOURTH, 0, 2)],
@@ -1076,8 +1061,15 @@
         def _():
             wait(kept(KEEP_FFN, l, True))
 
-        def now(stage, part):
-            if not alone:
+        def now(stage, part, early=None):
+            if alone:
+                return
+            if early is None:
+                run_reduce(stage, l, part)
+                return
+
+            @pl.when((n == LAYERS - 1) if early else (n < LAYERS - 1))
+            def _():
                 run_reduce(stage, l, part)
 
         def then(stage, part):
@@ -1089,17 +1081,18 @@
 
         def in_ffn():
             then(LAST, 2)
+            then(THIRD, 1)
+            then(FIRST, 0)
 
         def in_windows():
-            now(SECOND, 2)
-            then(LAST, 0)
+            now(FIRST, 1, False)
+            now(SECOND, 2, True)
 
         backward_ffn(k, l, grad, in_ffn)
+        backward_down_grads(k, l)
+        now(SEND, 2)
         then(LAST, 1)
         then(SECOND, 0)
-        backward_down_grads(k, l)
-        now(SEND, 2)
-        then(THIRD, 0)
         backward_up_grads(k, l)
 
         @pl.when(n < LAYERS - 1)
@@ -1107,16 +1100,20 @@
             start(kept(KEEP_FFN, l - 1, True))
 
         now(SEND, 1)
-        now(FIRST, 2)
+        now(FIRST, 2, True)
 
         @pl.when(n > 0)
         def _():
             wait(kept(KEEP_ATTN, l, True))
 
         backward_out(k, l, grad)
-        now(FIRST, 1)
+        now(FIRST, 2, False)
+        now(FIRST, 1, True)
+        then(THIRD, 0)
         backward_windows(k, l, in_windows)
-        now(THIRD, 2)
+        now(SECOND, 2, False)
+        now(THIRD, 2, True)
+        then(LAST, 0)
         backward_attn_grads(k, l)
 
         @pl.when(n < LAYERS - 1)
@@ -1124,7 +1121,8 @@
             start(kept(KEEP_ATTN, l - 1, True))
 
         now(SEND, 0)
-        now(SECOND, 1)
+        now(THIRD, 2, False)
+        now(SECOND, 1, True)
 
         @pl.when(n == LAYERS - 1)
         def _():
@@ -1136,8 +1134,9 @@
         def _():
             start(kept_x(True))
 
-        now(FIRST, 0)
-        now(THIRD, 1)
+        now(SECOND, 1, False)
+        now(FIRST, 0, True)
+        now(THIRD, 1, True)
         return carry
 
     lax.fori_loop(0, LAYERS, backward, 0)

time: 269 us -> 267 us (level)
  no operation moved by 1% of the time
where the time goes in v10:
time: 267 us
  Pallas kernels  266 us (100%)
    pallas_call x1, Pallas kernels, train_pass(): pl.pallas_call(kernel, name='train_pass', out_shape=tuple((jax.ShapeDtype...  260 us
    pallas_call x1, Pallas kernels, adam_all(): pl.pallas_call(adam_kernel, name='adam', out_shape=(jax.ShapeDtypeStruct(...  6.06 us

profile of v10, /device:TPU:0, one launch (start us, length us, event | category | flops | bytes accessed | tf_op | source)
XLA Modules:
  0.0 267.1 jit_solution(5693225516752618857)
XLA Ops:
  1.3 259.5 %train_pass.1 = (f32[96,512]{1,0:T(8,128)}, bf16[2,1024,1536]{2,1,0:T(8,128)(2,1)}, bf16[2,512,1024]{2,1,0:T(8,128)(2,1)}, bf16[2,512,1024]{2,1,0:T(8,128)(2,1)}...) custom-call(f32[11,64]{1,0:T(8,128)} %bitcast.3, ...), custom_call_target="tpu_custom_call" | custom-call | flops 60000002048 | bytes 40000000 | tf_op jit(solution)/shard_map/train_pass/pallas_call | solution.py:1219
  260.9 6.1 %adam.1 = (f32[3]{0:T(128)}, f32[1]{0:T(128)}, f32[1]{0:T(128)}, f32[85,512]{1,0:T(8,128)}, f32[85,512]{1,0:T(8,128)}, /*index=5*/f32[85,512]{1,0:T(8,128)}, f32...) custom-call(f32[3,192,512]{2,1,0:T(8,128)} %get-tuple-element.28.ref, ...), custom_call_target="tpu_custom_call" | custom-call | flops 10000000 | bytes 8000000 | tf_op jit(solution)/shard_map/adam/pallas_call | solution.py:1334
